TPU v7x, 32 devices: a whole 2x2x4 slice. The times are simulated.
32 devices in a mesh: dp: 8 (over z, x), mp: 4 (over y, core).
Axes of the slice: x: 2, y: 2, z: 4, core: 2. Of those that a mesh axis runs over, the one named last changes fastest.
Arguments:
- inputs: bfloat16 [8192, 768], P('dp'), may hold values from -16 to 16
- segments: int32 [8192], P('dp'), may hold values from -1 to 3, as said below
- norm1_gain: bfloat16 [768], P('dp'), may hold values from 0.099609375 to 1.8984375
- norm1_shift: bfloat16 [768], P('dp'), may hold values from -4 to 4
- qkv_weight: bfloat16 [3, 768, 768], P(None, 'dp', 'mp'), may hold values from -0.21875 to 0.21875
- qv_bias: bfloat16 [12, 128], P('mp', 'dp'), may hold values from -3 to 3
- attn_weight: bfloat16 [768, 768], P('mp', 'dp'), may hold values from -1.75 to 1.75
- attn_bias: bfloat16 [768], P('dp'), may hold values from -4 to 4
- norm2_gain: bfloat16 [768], P('dp'), may hold values from 0.099609375 to 1.8984375
- norm2_shift: bfloat16 [768], P('dp'), may hold values from -4 to 4
- fc_weight: bfloat16 [768, 3072], P('dp', 'mp'), may hold values from -0.21875 to 0.21875
- fc_bias: bfloat16 [4, 768], P('mp', 'dp'), may hold values from -6 to 6
- proj_weight: bfloat16 [3072, 768], P('mp', 'dp'), may hold values from -0.109375 to 0.109375
- proj_bias: bfloat16 [768], P('dp'), may hold values from -4 to 4
- cotangent: bfloat16 [8192, 768], P('dp'), may hold values from -16 to 16
Outputs:
- outputs: bfloat16 [8192, 768], P('dp')
- inputs_grad: bfloat16 [8192, 768], P('dp')
- norm1_gain_grad: float32 [768], P('dp')
- norm1_shift_grad: float32 [768], P('dp')
- qkv_weight_grad: float32 [3, 768, 768], P(None, 'dp', 'mp')
- qv_bias_grad: float32 [12, 128], P('mp', 'dp')
- attn_weight_grad: float32 [768, 768], P('mp', 'dp')
- attn_bias_grad: float32 [768], P('dp')
- norm2_gain_grad: float32 [768], P('dp')
- norm2_shift_grad: float32 [768], P('dp')
- fc_weight_grad: float32 [768, 3072], P('dp', 'mp')
- fc_bias_grad: float32 [4, 768], P('mp', 'dp')
- proj_weight_grad: float32 [3072, 768], P('mp', 'dp')
- proj_bias_grad: float32 [768], P('dp')
Inputs may be any that keep to these rules, and one draw needn't show every extreme that they name: `segments`: in each block of 1024 slots the used slots come first and their ids never fall, starting at 0; unused slots after them hold -1. Every block uses 1024 // 2 slots or more and holds at most four sequences; in every draw one block holds a single sequence of all 1024 slots.
All inputs are finite; a program needn't handle non-finite values.
Results may differ from a plain program's by a relative error of at most 0.015.
Values may be sent and summed in bfloat16 or wider, within the bound.
No kernel may reach another device: no remote copies, remote signals or barrier semaphores. Data moves between devices by JAX's collectives and lax.ppermute only.
A program may use at most 128 MiB of HBM per device.

v0:
```python
import functools

import jax
import jax.numpy as jnp
from jax import lax
from jax.experimental import pallas as pl
from jax.experimental.pallas import tpu as pltpu
from jax.sharding import PartitionSpec as P

HD = 64
TILE = 128
EXTRA = 16
CHUNKS = 8
EPSILON = 1e-05
NEGATIVE = -1e30
BF = jnp.bfloat16
F32 = jnp.float32
CORE_PAIRS = ((0, 1), (1, 0), (2, 3), (3, 2))
CHIP_PAIRS = ((0, 2), (2, 0), (1, 3), (3, 1))
CURVE = 0.7978845608028654


def dot(left, right, left_dim, right_dim):
    return lax.dot_general(
        left, right, (((left_dim,), (right_dim,)), ((), ())), preferred_element_type=F32
    )


def swap_core(value):
    return lax.ppermute(value, "mp", CORE_PAIRS)


def swap_chip(value):
    return lax.ppermute(value, "mp", CHIP_PAIRS)


def swap_bit(value, bit):
    return lax.ppermute(value, "dp", [(i, i ^ (1 << bit)) for i in range(CHUNKS)])


def call(kernel, outs, *args, scratch=(), smem=1, flops=0, name=None):
    specs = [pl.BlockSpec(memory_space=pltpu.SMEM)] * smem
    specs += [pl.BlockSpec(memory_space=pltpu.VMEM)] * (len(args) - smem)
    size = sum(a.size * a.dtype.itemsize for a in args)
    size += sum(o.size * jnp.dtype(o.dtype).itemsize for o in outs)
    return pl.pallas_call(
        kernel,
        out_shape=outs,
        in_specs=specs,
        out_specs=[pl.BlockSpec(memory_space=pltpu.VMEM)] * len(outs),
        scratch_shapes=list(scratch),
        compiler_params=pltpu.CompilerParams(vmem_limit_bytes=56 * 1024 * 1024),
        cost_estimate=pl.CostEstimate(flops=flops, bytes_accessed=size, transcendentals=0),
        name=name,
    )(*args)


def shape(dims, dtype=BF):
    return jax.ShapeDtypeStruct(tuple(dims), dtype)


def gather_blocks(message):
    got = {0: message}
    got[4] = swap_bit(message, 2)
    got[1] = swap_bit(message, 0)
    got[2] = swap_bit(message, 1)
    got[5] = swap_bit(got[4], 0)
    got[6] = swap_bit(got[4], 1)
    got[3] = swap_bit(got[2], 0)
    got[7] = swap_bit(got[5], 1)
    return jnp.stack([got[r] for r in range(CHUNKS)])


def loop(count, step, fn):
    def run(i, carry):
        fn(pl.multiple_of(i * step, step))
        return carry

    lax.fori_loop(0, count // step, run, 0)


def norm_stats(value):
    average = jnp.mean(value, -1, keepdims=True)
    centred = value - average
    spread = jnp.mean(centred * centred, -1, keepdims=True)
    factor = lax.rsqrt(spread + EPSILON)
    return centred * factor, factor


def norm_backward(incoming, scaled, factor, gain):
    weighted = incoming * gain
    first_mean = jnp.mean(weighted, -1, keepdims=True)
    second_mean = jnp.mean(weighted * scaled, -1, keepdims=True)
    return factor * (weighted - first_mean - scaled * second_mean)


def tile_sum(ref, base):
    total = ref[0, base : base + EXTRA, :].astype(F32)
    for r in range(1, CHUNKS):
        total = total + ref[r, base : base + EXTRA, :].astype(F32)
    return total


def own_start(start, core):
    tile = start // TILE
    return pl.multiple_of((2 * tile + core) * TILE + start % TILE, 32)


def colsum(value):
    return jnp.sum(value, 0, keepdims=True)


def norm_kernel(info, x_ref, w_ref, low_ref, vec_ref):
    base = w_ref.shape[1] - EXTRA
    vec_ref[...] = tile_sum(w_ref, base)
    gain, shift = vec_ref[0:1, :], vec_ref[1:2, :]

    def run(at):
        scaled, _ = norm_stats(x_ref[pl.ds(at, 32), :].astype(F32))
        low_ref[pl.ds(at, 32), :] = (scaled * gain + shift).astype(BF)

    loop(x_ref.shape[0], 32, run)


def attend_kernel(
    info,
    low_ref,
    own_ref,
    sib_ref,
    seg_ref,
    part_ref,
    mixed_ref,
    q_ref,
    k_ref,
    v_ref,
    probs_ref,
    wq_ref,
    wk_ref,
    wv_ref,
    wo_ref,
    firstown_ref,
    proj_ref,
    s_ref,
    o_ref,
):
    flip, core = info[0], info[1]
    width = own_ref.shape[2] // 4
    base = own_ref.shape[1] - EXTRA
    rows = low_ref.shape[0]
    heads = 2 * width // HD
    own_count = rows // 2
    for r in range(CHUNKS):
        at = pl.multiple_of((r ^ flip) * base, 32)
        for side, ref in ((0, own_ref), (1, sib_ref)):
            for part, out in enumerate((wq_ref, wk_ref, wv_ref, wo_ref)):
                out[pl.ds(at, base), side * width : (side + 1) * width] = ref[
                    r, 0:base, part * width : (part + 1) * width
                ]
    vec_own = tile_sum(own_ref, base)
    vec_sib = tile_sum(sib_ref, base)
    bias_q = jnp.concatenate([vec_own[7:8, :width], vec_sib[7:8, :width]], 1)
    bias_v = jnp.concatenate(
        [vec_own[7:8, width : 2 * width], vec_sib[7:8, width : 2 * width]], 1
    )
    for j in range(own_count // TILE):
        at = own_start(j * TILE, core)
        firstown_ref[j * TILE : (j + 1) * TILE, :] = low_ref[pl.ds(at, TILE), :]
    scale = float(HD) ** -0.5
    proj_ref[0:own_count, :] = dot(firstown_ref[...], wq_ref[...], 1, 0) + bias_q
    for h in range(heads):
        q_ref[h] = (
            proj_ref[0:own_count, h * HD : (h + 1) * HD].astype(BF).astype(F32) * scale
        ).astype(BF)
    proj_ref[...] = dot(low_ref[...], wk_ref[...], 1, 0)
    for h in range(heads):
        k_ref[h] = proj_ref[:, h * HD : (h + 1) * HD].astype(BF)
    proj_ref[...] = dot(low_ref[...], wv_ref[...], 1, 0) + bias_v
    for h in range(heads):
        v_ref[h] = proj_ref[:, h * HD : (h + 1) * HD].astype(BF)
    lane = lax.broadcasted_iota(jnp.int32, (TILE, TILE), 1)
    line = lax.broadcasted_iota(jnp.int32, (TILE, TILE), 0)
    for j in range(own_count // TILE):
        end = (j + 1) * 2 * TILE
        off = TILE * j * (j + 1)
        at = own_start(j * TILE, core)
        seg_tile = jnp.broadcast_to(seg_ref[0:1, pl.ds(at, TILE)], (TILE, TILE))
        seg_col = jnp.max(jnp.where(lane == line, seg_tile, -2), -1, keepdims=True)
        place = lax.broadcasted_iota(jnp.int32, (TILE, end), 1)
        own_place = at + lax.broadcasted_iota(jnp.int32, (TILE, end), 0)
        allowed = (seg_col == seg_ref[0:1, 0:end]) & (place <= own_place)
        bias = jnp.where(allowed, 0.0, NEGATIVE)
        s_ref[heads, :, 0:end] = bias

        def run(h, carry, j=j, end=end, off=off):
            scores = dot(q_ref[h, j * TILE : (j + 1) * TILE, :], k_ref[h, 0:end, :], 1, 1)
            s_ref[0, :, 0:end] = scores
            for sub in range(4):
                sl = slice(sub * 32, sub * 32 + 32)
                sc = s_ref[0, sl, 0:end] + s_ref[heads, sl, 0:end]
                weights = jnp.exp(sc - jnp.max(sc, -1, keepdims=True))
                inverse = 1.0 / jnp.sum(weights, -1, keepdims=True)
                probs_ref[h, sl, off : off + end] = (weights * inverse).astype(BF)
            o_ref[h, j * TILE : (j + 1) * TILE, :] = dot(
                probs_ref[h, :, off : off + end], v_ref[h, 0:end, :], 1, 0
            )
            return carry

        lax.fori_loop(0, heads, run, 0)
    for h in range(heads):
        mixed_ref[:, h * HD : (h + 1) * HD] = o_ref[h].astype(BF)
    part_ref[...] = dot(mixed_ref[...], wo_ref[...], 1, 1).astype(BF)


def mlp_kernel(
    info,
    x_ref,
    seg_ref,
    cot_ref,
    part_ref,
    recv_ref,
    vec_ref,
    vecsib_ref,
    own_ref,
    sib_ref,
    da_ref,
    act_ref,
    dhid_ref,
    second_ref,
    dy_ref,
    mid_ref,
    fc_ref,
    proj_ref,
    hid_ref,
    dact_ref,
):
    flip, core = info[0], info[1]
    own_count = part_ref.shape[0]
    base = own_ref.shape[1]
    units = own_ref.shape[2] // 2
    for r in range(CHUNKS):
        at = pl.multiple_of((r ^ flip) * base, 32)
        for side, ref in ((0, own_ref), (1, sib_ref)):
            cols = slice(side * units, (side + 1) * units)
            fc_ref[pl.ds(at, base), cols] = ref[r, :, 0:units]
            proj_ref[pl.ds(at, base), cols] = ref[r, :, units : 2 * units]
    gain, shift, bias = vec_ref[3:4, :], vec_ref[4:5, :], vec_ref[2:3, :]
    sub = 32
    lane = lax.broadcasted_iota(jnp.int32, (sub, TILE), 1)
    line = lax.broadcasted_iota(jnp.int32, (sub, TILE), 0)

    def first(at):
        src = own_start(at, core)
        tile_at = pl.multiple_of((2 * (at // TILE) + core) * TILE, TILE)
        seg_tile = jnp.broadcast_to(seg_ref[0:1, pl.ds(tile_at, TILE)], (sub, TILE))
        seg_col = jnp.max(
            jnp.where(lane == line + at % TILE, seg_tile, -2), -1, keepdims=True
        )
        rows = pl.ds(at, sub)
        cot = cot_ref[pl.ds(src, sub), :].astype(F32)
        dy_ref[rows, :] = jnp.where(seg_col >= 0, cot, 0.0).astype(BF)
        middle = (
            x_ref[pl.ds(src, sub), :].astype(F32)
            + (part_ref[rows, :].astype(F32) + recv_ref[rows, :].astype(F32))
            + bias
        )
        mid_ref[rows, :] = middle
        scaled, _ = norm_stats(middle)
        second_ref[rows, :] = (scaled * gain + shift).astype(BF)

    loop(own_count, sub, first)
    step = 512
    for c in range(2 * units // step):
        cols = slice(c * step, (c + 1) * step)
        hid_ref[...] = dot(second_ref[...], fc_ref[:, cols], 1, 0)
        dact_ref[...] = dot(dy_ref[...], proj_ref[:, cols], 1, 0)
        left, right = c * step, (c + 1) * step
        pieces = []
        if left < units:
            pieces.append(vec_ref[5:6, left : min(right, units)])
        if right > units:
            pieces.append(vecsib_ref[5:6, max(left, units) - units : right - units])
        bias_fc = jnp.concatenate(pieces, 1) if len(pieces) > 1 else pieces[0]

        def gelu(at, cols=cols, bias_fc=bias_fc):
            rows = pl.ds(at, 16)
            u = hid_ref[rows, :] + bias_fc
            u2 = u * u
            bend = jnp.tanh(CURVE * u * (1.0 + 0.044715 * u2))
            half = 0.5 * (1.0 + bend)
            act_ref[rows, cols] = (u * half).astype(BF)
            slope = half + (0.5 * CURVE) * u * (1.0 - bend * bend) * (1.0 + 0.134145 * u2)
            dhid_ref[rows, cols] = (dact_ref[rows, :] * slope).astype(BF)

        loop(own_count, 16, gelu)
    da_ref[...] = dot(dhid_ref[...], fc_ref[...], 1, 1).astype(BF)


def mlp_out_kernel(info, act_ref, own_ref, sib_ref, part_ref, proj_ref):
    flip = info[0]
    base = own_ref.shape[1]
    units = own_ref.shape[2] // 2
    for r in range(CHUNKS):
        at = pl.multiple_of((r ^ flip) * base, 32)
        proj_ref[pl.ds(at, base), 0:units] = own_ref[r, :, units : 2 * units]
        proj_ref[pl.ds(at, base), units : 2 * units] = sib_ref[r, :, units : 2 * units]
    part_ref[...] = dot(act_ref[...], proj_ref[...], 1, 1).astype(BF)


def mlp_grad_kernel(
    info, act_ref, dhid_ref, second_ref, dy_ref, own_ref, sib_ref, sums_ref, acc_ref
):
    flip = info[0]
    base = own_ref.shape[1]
    units = own_ref.shape[2] // 2
    for kind, left, right in ((0, second_ref, dhid_ref), (1, dy_ref, act_ref)):
        for side, out in ((0, own_ref), (1, sib_ref)):
            acc_ref[...] = dot(left[...], right[:, side * units : (side + 1) * units], 0, 0)
            for b in range(CHUNKS):
                out[b ^ flip, :, kind * units : (kind + 1) * units] = acc_ref[
                    b * base : (b + 1) * base, :
                ].astype(BF)
    one = jnp.ones((8, act_ref.shape[0]), BF)
    fc_sums = dot(one, dhid_ref[...], 1, 0)
    sums_ref[0:8, :] = fc_sums[:, 0:units]
    sums_ref[8:16, :] = fc_sums[:, units : 2 * units]
    sums_ref[16:24, :] = dot(one, dy_ref[...], 1, 0)


def attend_back_kernel(
    info,
    mid_ref,
    dy_ref,
    da_ref,
    recv_ref,
    vec_ref,
    wo_ref,
    mixed_ref,
    q_ref,
    k_ref,
    v_ref,
    probs_ref,
    dmid_ref,
    branch_ref,
    sums_ref,
    dq_ref,
    keep_ref,
    send_ref,
    dm_ref,
    do_ref,
    dkt_ref,
    dvt_ref,
    dqh_ref,
    dp_ref,
    ds_ref,
    delta_ref,
):
    core = info[1]
    own_count = mid_ref.shape[0]
    heads = q_ref.shape[0]
    rows = k_ref.shape[1]
    gain = vec_ref[3:4, :]
    sums_ref[...] = jnp.zeros_like(sums_ref)
    sub = 32

    def first(at):
        rs = pl.ds(at, sub)
        scaled, factor = norm_stats(mid_ref[rs, :])
        incoming = da_ref[rs, :].astype(F32) + recv_ref[rs, :].astype(F32)
        dmid = dy_ref[rs, :].astype(F32) + norm_backward(incoming, scaled, factor, gain)
        dmid_ref[rs, :] = dmid
        low = dmid.astype(BF)
        branch_ref[rs, :] = low
        sums_ref[2:3, :] += colsum(low.astype(F32))
        sums_ref[3:4, :] += colsum(incoming * scaled)
        sums_ref[4:5, :] += colsum(incoming)

    loop(own_count, sub, first)
    dm_ref[...] = dot(branch_ref[...], wo_ref[...], 1, 0).astype(BF)
    for h in range(heads):
        cols = slice(h * HD, (h + 1) * HD)
        do_ref[h] = dm_ref[:, cols]
        delta_ref[h] = jnp.broadcast_to(
            jnp.sum(
                dm_ref[:, cols].astype(F32) * mixed_ref[:, cols].astype(F32), -1, keepdims=True
            ),
            (own_count, TILE),
        )
    scale = float(HD) ** -0.5

    def head(h, carry):
        for j in reversed(range(own_count // TILE)):
            end = (j + 1) * 2 * TILE
            off = TILE * j * (j + 1)
            rs = slice(j * TILE, (j + 1) * TILE)
            dp_ref[:, 0:end] = dot(do_ref[h, rs, :], v_ref[h, 0:end, :], 1, 1)
            for s in range(4):
                sl = slice(s * 32, s * 32 + 32)
                delta = delta_ref[h, j * TILE + s * 32 : j * TILE + s * 32 + 32, 0:1]
                p = probs_ref[h, sl, off : off + end].astype(F32)
                ds_ref[sl, 0:end] = (p * (dp_ref[sl, 0:end] - delta)).astype(BF)
            ds = ds_ref[:, 0:end]
            dqh_ref[h, rs, :] = dot(ds, k_ref[h, 0:end, :], 1, 0) * scale
            dk = dot(q_ref[h, rs, :], ds, 0, 0)
            dv = dot(do_ref[h, rs, :], probs_ref[h, :, off : off + end], 0, 0)
            if j == own_count // TILE - 1:
                dkt_ref[h] = dk
                dvt_ref[h] = dv
            else:
                dkt_ref[h, :, 0:end] += dk
                dvt_ref[h, :, 0:end] += dv
        return carry

    lax.fori_loop(0, heads, head, 0)
    width2 = heads * HD
    for h in range(heads):
        dq_ref[:, h * HD : (h + 1) * HD] = dqh_ref[h].astype(BF)
        twin = (h + heads // 2) % heads
        for j in range(own_count // TILE):
            mine = pl.multiple_of((2 * j + core) * TILE, TILE)
            yours = pl.multiple_of((2 * j + 1 - core) * TILE, TILE)
            cols = slice(j * TILE, (j + 1) * TILE)
            for part, ref in ((0, dkt_ref), (1, dvt_ref)):
                at = part * width2
                keep_ref[at + h * HD : at + (h + 1) * HD, cols] = ref[h, :, pl.ds(mine, TILE)]
                send_ref[at + twin * HD : at + (twin + 1) * HD, cols] = ref[
                    h, :, pl.ds(yours, TILE)
                ].astype(BF)


def attn_grad_kernel(info, branch_ref, mixed_ref, out_ref):
    out_ref[...] = dot(branch_ref[...], mixed_ref[...], 0, 0)


def first_grad_kernel(
    info, dq_ref, keep_ref, got_ref, wq_ref, wk_ref, wv_ref, part_ref, dkv_ref
):
    width2 = dq_ref.shape[1]
    dkv_ref[...] = (keep_ref[...] + got_ref[...].astype(F32)).astype(BF)
    part_ref[...] = (
        dot(dq_ref[...], wq_ref[...], 1, 1)
        + dot(dkv_ref[0:width2, :], wk_ref[...], 0, 1)
        + dot(dkv_ref[width2 : 2 * width2, :], wv_ref[...], 0, 1)
    ).astype(BF)


def qkv_grad_kernel(
    info,
    first_ref,
    dq_ref,
    dkv_ref,
    attn_ref,
    part_ref,
    x_ref,
    mlp_sums_ref,
    att_sums_ref,
    own_ref,
    sib_ref,
    tile_own_ref,
    tile_sib_ref,
    sum_ref,
):
    flip, core = info[0], info[1]
    width2 = dq_ref.shape[1]
    width = width2 // 2
    base = own_ref.shape[1]
    for part in range(4):
        if part == 0:
            whole = dot(first_ref[...], dq_ref[...], 0, 0)
        elif part == 3:
            whole = attn_ref[...]
        else:
            whole = dot(
                first_ref[...], dkv_ref[(part - 1) * width2 : part * width2, :], 0, 1
            )
        for b in range(CHUNKS):
            rows = slice(b * base, (b + 1) * base)
            cols = slice(part * width, (part + 1) * width)
            own_ref[b ^ flip, :, cols] = whole[rows, 0:width].astype(BF)
            sib_ref[b ^ flip, :, cols] = whole[rows, width:width2].astype(BF)
    sum_ref[...] = jnp.zeros_like(sum_ref)

    def run(at):
        src = own_start(at, core)
        scaled, _ = norm_stats(x_ref[pl.ds(src, 32), :].astype(F32))
        incoming = part_ref[pl.ds(at, 32), :].astype(F32)
        sum_ref[0:1, :] += colsum(incoming * scaled)
        sum_ref[1:2, :] += colsum(incoming)

    loop(part_ref.shape[0], 32, run)
    ones = jnp.ones((8, dq_ref.shape[0]), BF)
    qs = dot(ones, dq_ref[...], 1, 0)[0:1, :]
    vs = dot(ones, dkv_ref[width2 : 2 * width2, :], 1, 1)[0:1, :]
    sum_ref[2:5, :] = att_sums_ref[2:5, :]
    sum_ref[6:7, :] = mlp_sums_ref[16:17, :]
    for side, out in ((0, tile_own_ref), (1, tile_sib_ref)):
        sl = slice(side * width, (side + 1) * width)
        sum_ref[5:6, :] = mlp_sums_ref[8 * side : 8 * side + 1, :]
        sum_ref[7:8, 0:width] = qs[:, sl]
        sum_ref[7:8, width : 2 * width] = vs[:, sl]
        out[...] = sum_ref[...].astype(BF)


def final_kernel(info, x_ref, part_ref, recv_ref, dmid_ref, vec_ref, out_ref):
    core = info[1]
    gain = vec_ref[0:1, :]

    def run(at):
        src = own_start(at, core)
        rs = pl.ds(at, 32)
        scaled, factor = norm_stats(x_ref[pl.ds(src, 32), :].astype(F32))
        incoming = part_ref[rs, :].astype(F32) + recv_ref[rs, :].astype(F32)
        out_ref[rs, :] = (
            dmid_ref[rs, :] + norm_backward(incoming, scaled, factor, gain)
        ).astype(BF)

    loop(part_ref.shape[0], 32, run)


def output_kernel(info, seg_ref, mid_ref, part_ref, recv_ref, vec_ref, out_ref):
    core = info[1]
    bias = vec_ref[6:7, :]
    sub = 32
    lane = lax.broadcasted_iota(jnp.int32, (sub, TILE), 1)
    line = lax.broadcasted_iota(jnp.int32, (sub, TILE), 0)

    def run(at):
        tile_at = pl.multiple_of((2 * (at // TILE) + core) * TILE, TILE)
        seg_tile = jnp.broadcast_to(seg_ref[0:1, pl.ds(tile_at, TILE)], (sub, TILE))
        seg_col = jnp.max(
            jnp.where(lane == line + at % TILE, seg_tile, -2), -1, keepdims=True
        )
        rs = pl.ds(at, sub)
        final = (
            mid_ref[rs, :]
            + (part_ref[rs, :].astype(F32) + recv_ref[rs, :].astype(F32))
            + bias
        )
        out_ref[rs, :] = jnp.where(seg_col >= 0, final, 0.0).astype(BF)

    loop(part_ref.shape[0], sub, run)


def merge_kernel(info, own_ref, got_ref, out_ref):
    core = info[1]
    for j in range(own_ref.shape[0] // TILE):
        sl = slice(j * TILE, (j + 1) * TILE)
        mine = pl.multiple_of((2 * j + core) * TILE, TILE)
        yours = pl.multiple_of((2 * j + 1 - core) * TILE, TILE)
        out_ref[pl.ds(mine, TILE), :] = own_ref[sl, :]
        out_ref[pl.ds(yours, TILE), :] = got_ref[sl, :]


def all_rows(info, own):
    return call(
        merge_kernel,
        [shape((2 * own.shape[0], own.shape[1]))],
        info,
        own,
        swap_core(own),
        name="merge",
    )[0]


def scatter_first_kernel(info, own_ref, got_ref, *refs):
    tiles, (keep_a, send_a, keep_b, send_b) = refs[:-4], refs[-4:]
    base = own_ref.shape[1]
    half = own_ref.shape[2] // 2
    for keep, send, bit, at in ((keep_a, send_a, 0, 0), (keep_b, send_b, 1, half)):
        cols = slice(at, at + half)
        kept, sent = 0, 0
        for r in range(CHUNKS):
            value = own_ref[r, :, cols].astype(F32) + got_ref[r, :, cols].astype(F32)
            if (r >> bit) & 1:
                send[sent * base : (sent + 1) * base, :] = value.astype(BF)
                sent += 1
            else:
                keep[kept * base : (kept + 1) * base, :] = value
                kept += 1
        if tiles:
            value = tiles[0][:, cols].astype(F32) + tiles[1][:, cols].astype(F32)
            value = value + tiles[2][:, cols].astype(F32)
            send[4 * base : 4 * base + EXTRA, :] = value.astype(BF)
            keep[4 * base : 4 * base + EXTRA, :] = value


def scatter_second_kernel(
    tiled, info, keep_a, got_a, keep_b, got_b, next_a, send_a, next_b, send_b
):
    extra = EXTRA if tiled else 0
    base = (keep_a.shape[0] - extra) // 4
    for keep, got, left, send, order in (
        (keep_a, got_a, next_a, send_a, (0, 1, 0, 1)),
        (keep_b, got_b, next_b, send_b, (0, 1, 0, 1)),
    ):
        kept, sent = 0, 0
        for r in range(4):
            rows = slice(r * base, (r + 1) * base)
            value = keep[rows, :] + got[rows, :].astype(F32)
            if order[r]:
                send[sent * base : (sent + 1) * base, :] = value.astype(BF)
                sent += 1
            else:
                left[kept * base : (kept + 1) * base, :] = value
                kept += 1
        if tiled:
            low = keep[4 * base : 4 * base + extra, :].astype(BF).astype(F32)
            value = low + got[4 * base : 4 * base + extra, :].astype(F32)
            send[2 * base : 2 * base + extra, :] = value.astype(BF)
            left[2 * base : 2 * base + extra, :] = value


def scatter_third_kernel(tiled, info, keep_a, got_a, keep_b, got_b, left, send):
    extra = EXTRA if tiled else 0
    base = (keep_a.shape[0] - extra) // 2
    half = keep_a.shape[1]
    for keep, got, at in ((keep_a, got_a, 0), (keep_b, got_b, half)):
        cols = slice(at, at + half)
        left[0:base, cols] = keep[0:base, :] + got[0:base, :].astype(F32)
        send[0:base, cols] = (
            keep[base : 2 * base, :] + got[base : 2 * base, :].astype(F32)
        ).astype(BF)
        if tiled:
            rows = slice(2 * base, 2 * base + extra)
            value = keep[rows, :].astype(BF).astype(F32) + got[rows, :].astype(F32)
            left[base : base + extra, cols] = value
            send[base : base + extra, cols] = value.astype(BF)


def scatter_last_kernel(tiled, info, left, got, out):
    extra = EXTRA if tiled else 0
    base = left.shape[0] - extra
    out[0:base, :] = left[0:base, :] + got[0:base, :].astype(F32)
    if tiled:
        rows = slice(base, base + extra)
        out[rows, :] = left[rows, :].astype(BF).astype(F32) + got[rows, :].astype(F32)


def scatter_blocks(info, own, sib, count, tiles=None):
    got = swap_core(sib)
    base, columns = own.shape[1:]
    tiled = tiles is not None
    extra = EXTRA if tiled else 0
    if count != CHUNKS:
        total = own.astype(F32) + got.astype(F32)
        total = lax.psum_scatter(
            total.reshape(CHUNKS * base, columns), "dp", scatter_dimension=0, tiled=True
        )
        if not tiled:
            return total, None
        return total, lax.psum(sum(t.astype(F32) for t in tiles), "dp")
    half = columns // 2
    rows = 4 * base + extra
    keep_a, send_a, keep_b, send_b = call(
        scatter_first_kernel,
        [shape((rows, half), F32), shape((rows, half))] * 2,
        info,
        own,
        got,
        *(tiles or ()),
        name="scatter_first",
    )
    rows = 2 * base + extra
    keep_a, send_a, keep_b, send_b = call(
        functools.partial(scatter_second_kernel, tiled),
        [shape((rows, half), F32), shape((rows, half))] * 2,
        info,
        keep_a,
        swap_bit(send_a, 0),
        keep_b,
        swap_bit(send_b, 1),
        name="scatter_second",
    )
    rows = base + extra
    left, send = call(
        functools.partial(scatter_third_kernel, tiled),
        [shape((rows, columns), F32), shape((rows, columns))],
        info,
        keep_a,
        swap_bit(send_a, 1),
        keep_b,
        swap_bit(send_b, 0),
        name="scatter_third",
    )
    out = call(
        functools.partial(scatter_last_kernel, tiled),
        [shape((rows, columns), F32)],
        info,
        left,
        swap_bit(send, 2),
        name="scatter_last",
    )[0]
    return out[:base], (out[base:] if tiled else None)


def body(
    inputs,
    segments,
    norm1_gain,
    norm1_shift,
    qkv_weight,
    qv_bias,
    attn_weight,
    attn_bias,
    norm2_gain,
    norm2_shift,
    fc_weight,
    fc_bias,
    proj_weight,
    proj_bias,
    cotangent,
):
    count = lax.axis_size("dp")
    index = lax.axis_index("dp")
    core = lax.axis_index("mp") % 2
    rows, depth = inputs.shape
    local = depth // count
    width = qkv_weight.shape[2]
    heads = width // HD
    units = fc_weight.shape[1]
    width2 = 2 * width
    heads2 = 2 * heads
    own_count = rows // 2
    base = depth // CHUNKS
    flip = index if count == CHUNKS else jnp.zeros_like(index)
    info = jnp.stack([flip, core]).astype(jnp.int32)
    seg_row = segments.reshape(1, rows)

    bias_width = qv_bias.shape[1]
    bias_rows = lax.dynamic_update_slice(
        jnp.zeros((heads, 2 * HD), BF), qv_bias, (0, index * bias_width)
    )
    bias_row = bias_rows.reshape(heads, 2, HD).transpose(1, 0, 2).reshape(1, width2)
    vectors = jnp.stack(
        [norm1_gain, norm1_shift, attn_bias, norm2_gain, norm2_shift, fc_bias[0], proj_bias]
    )
    placed = lax.dynamic_update_slice(
        jnp.zeros((vectors.shape[0], depth), BF), vectors, (0, index * local)
    )
    tile = jnp.concatenate(
        [
            placed,
            jnp.pad(bias_row, ((0, EXTRA - vectors.shape[0] - 1), (0, depth - width2))),
        ],
        0,
    )
    mats = jnp.concatenate(
        [qkv_weight.transpose(1, 0, 2).reshape(local, 3 * width), attn_weight.T], 1
    )
    wide = jnp.concatenate([fc_weight, proj_weight.T], 1)
    if count == CHUNKS:
        own_a = gather_blocks(jnp.concatenate([mats, tile], 0))
        wide = lax.optimization_barrier((wide, own_a))[0]
        own_b = gather_blocks(wide)
    else:
        full = lax.all_gather(mats, "dp", axis=0, tiled=True).reshape(CHUNKS, base, depth)
        total = jnp.sum(lax.all_gather(tile, "dp", axis=0).astype(F32), 0).astype(BF)
        total = jnp.pad(total[None], ((0, CHUNKS - 1), (0, 0), (0, 0)))
        own_a = jnp.concatenate([full, total], 1)
        own_b = lax.all_gather(wide, "dp", axis=0, tiled=True).reshape(CHUNKS, base, 2 * units)
    sib_a = swap_core(own_a)
    first_low, vec = call(
        norm_kernel,
        [shape((rows, depth)), shape((EXTRA, depth), F32)],
        info,
        inputs,
        own_a,
        name="norm_first",
    )
    pairs = heads2 * TILE * (own_count // TILE) * (own_count // TILE + 1) * TILE
    weight = shape((depth, width2))
    part, mixed, q, k, v, probs, wq, wk, wv, wo, first_own = call(
        attend_kernel,
        [
            shape((own_count, depth)),
            shape((own_count, width2)),
            shape((heads2, own_count, HD)),
            shape((heads2, rows, HD)),
            shape((heads2, rows, HD)),
            shape((heads2, TILE, TILE * (own_count // TILE) * (own_count // TILE + 1))),
            weight,
            weight,
            weight,
            weight,
            shape((own_count, depth)),
        ],
        info,
        first_low,
        own_a,
        sib_a,
        seg_row,
        scratch=[
            pltpu.VMEM((rows, width2), F32),
            pltpu.VMEM((heads2 + 1, TILE, rows), F32),
            pltpu.VMEM((heads2, own_count, HD), F32),
        ],
        flops=4 * pairs * HD + 5 * rows * depth * width2,
        name="attend",
    )
    got = swap_chip(part)
    sib_b = swap_core(own_b)
    vec_sib = jnp.sum(sib_a[:, base:].astype(F32), 0)
    hid = shape((own_count, 2 * units))
    da, act, dhid, second, dy, middle = call(
        mlp_kernel,
        [
            shape((own_count, depth)),
            hid,
            hid,
            shape((own_count, depth)),
            shape((own_count, depth)),
            shape((own_count, depth), F32),
        ],
        info,
        inputs,
        seg_row,
        cotangent,
        part,
        got,
        vec,
        vec_sib,
        own_b,
        sib_b,
        scratch=[
            pltpu.VMEM((depth, 2 * units), BF),
            pltpu.VMEM((depth, 2 * units), BF),
            pltpu.VMEM((own_count, 512), F32),
            pltpu.VMEM((own_count, 512), F32),
        ],
        flops=12 * own_count * depth * units,
        name="mlp",
    )
    da_got = swap_chip(da)
    mlp_part = call(
        mlp_out_kernel,
        [shape((own_count, depth))],
        info,
        act,
        own_b,
        sib_b,
        scratch=[pltpu.VMEM((depth, 2 * units), BF)],
        flops=4 * own_count * depth * units,
        name="mlp_out",
    )[0]
    grad_own, grad_sib, mlp_sums = call(
        mlp_grad_kernel,
        [
            shape((CHUNKS, base, 2 * units)),
            shape((CHUNKS, base, 2 * units)),
            shape((24, depth), F32),
        ],
        info,
        act,
        dhid,
        second,
        dy,
        scratch=[pltpu.VMEM((depth, units), F32)],
        flops=8 * own_count * depth * units,
        name="mlp_grad",
    )
    big, _ = scatter_blocks(info, grad_own, grad_sib, count)
    fc_weight_grad = big[:, :units]
    proj_weight_grad = big[:, units:].T

    dmid, branch, att_sums, dq, keep, send = call(
        attend_back_kernel,
        [
            shape((own_count, depth), F32),
            shape((own_count, depth)),
            shape((8, depth), F32),
            shape((own_count, width2)),
            shape((2 * width2, own_count), F32),
            shape((2 * width2, own_count)),
        ],
        info,
        middle,
        dy,
        da,
        da_got,
        vec,
        wo,
        mixed,
        q,
        k,
        v,
        probs,
        scratch=[
            pltpu.VMEM((own_count, width2), BF),
            pltpu.VMEM((heads2, own_count, HD), BF),
            pltpu.VMEM((heads2, HD, rows), F32),
            pltpu.VMEM((heads2, HD, rows), F32),
            pltpu.VMEM((heads2, own_count, HD), F32),
            pltpu.VMEM((TILE, rows), F32),
            pltpu.VMEM((TILE, rows), BF),
            pltpu.VMEM((heads2, own_count, TILE), F32),
        ],
        flops=8 * pairs * HD,
        name="attend_back",
    )
    keep_got = swap_core(send)
    attn_full = call(
        attn_grad_kernel,
        [shape((depth, width2), F32)],
        info,
        branch,
        mixed,
        flops=2 * own_count * depth * width2,
        name="attn_grad",
    )[0]
    first_part, dkv = call(
        first_grad_kernel,
        [shape((own_count, depth)), shape((2 * width2, own_count))],
        info,
        dq,
        keep,
        keep_got,
        wq,
        wk,
        wv,
        flops=6 * own_count * depth * width2,
        name="first_grad",
    )
    first_got = swap_chip(first_part)
    qkv_own, qkv_sib, tile_own, tile_sib = call(
        qkv_grad_kernel,
        [shape((CHUNKS, base, 4 * width))] * 2 + [shape((EXTRA, depth))] * 2,
        info,
        first_own,
        dq,
        dkv,
        attn_full,
        first_part,
        inputs,
        mlp_sums,
        att_sums,
        scratch=[pltpu.VMEM((EXTRA, depth), F32)],
        flops=6 * own_count * depth * width2,
        name="qkv_grad",
    )
    mask = (jnp.arange(EXTRA) < 2)[:, None]
    tile_got = swap_core(tile_sib)
    part_sum = jnp.where(mask, tile_own.astype(F32) + tile_got.astype(F32), 0.0).astype(BF)
    other = swap_chip(part_sum)
    mine, tile = scatter_blocks(info, qkv_own, qkv_sib, count, (tile_own, tile_got, other))
    inputs_low = call(
        final_kernel,
        [shape((own_count, depth))],
        info,
        inputs,
        first_part,
        first_got,
        dmid,
        vec,
        name="final",
    )[0]
    inputs_grad = all_rows(info, inputs_low)
    out_low = call(
        output_kernel,
        [shape((own_count, depth))],
        info,
        seg_row,
        middle,
        mlp_part,
        swap_chip(mlp_part),
        vec,
        name="output",
    )[0]
    outputs = all_rows(info, out_low)

    qkv_weight_grad = mine[:, : 3 * width].reshape(local, 3, width).transpose(1, 0, 2)
    attn_weight_grad = mine[:, 3 * width :].T
    parts = lax.dynamic_slice(tile, (0, index * local), (7, local))
    bias_sum = tile[7, :width2].reshape(2, heads, HD).transpose(1, 0, 2).reshape(heads, 2 * HD)
    qv_bias_grad = lax.dynamic_slice(bias_sum, (0, index * bias_width), (heads, bias_width))
    return (
        outputs,
        inputs_grad,
        parts[0],
        parts[1],
        qkv_weight_grad,
        qv_bias_grad,
        attn_weight_grad,
        parts[2],
        parts[3],
        parts[4],
        fc_weight_grad,
        parts[5][None],
        proj_weight_grad,
        parts[6],
    )


def solution(mesh):
    return jax.shard_map(
        body,
        mesh=mesh,
        in_specs=(
            P("dp", None),
            P("dp"),
            P("dp"),
            P("dp"),
            P(None, "dp", "mp"),
            P("mp", "dp"),
            P("mp", "dp"),
            P("dp"),
            P("dp"),
            P("dp"),
            P("dp", "mp"),
            P("mp", "dp"),
            P("mp", "dp"),
            P("dp"),
            P("dp", None),
        ),
        out_specs=(
            P("dp", None),
            P("dp", None),
            P("dp"),
            P("dp"),
            P(None, "dp", "mp"),
            P("mp", "dp"),
            P("mp", "dp"),
            P("dp"),
            P("dp"),
            P("dp"),
            P("dp", "mp"),
            P("mp", "dp"),
            P("mp", "dp"),
            P("dp"),
        ),
        check_vma=False,
    )
```

profile of v0, /device:TPU:0, one launch (start us, length us, event | category | flops | bytes accessed | tf_op | source)
XLA Modules:
  0.0 319.1 jit_solution(13324211995907987535)
XLA Ops:
  5.5 3.1 collective-permute-start
  10.2 2.6 collective-permute-start.3
  13.8 6.6 %collective-permute-done.3 = bf16[112,768]{1,0:T(8,128)(2,1)S(1)} collective-permute-done((bf16[112,768]{1,0:T(8,128)(2,1)S(1)}, bf16[112,768]{1,0:T(8,128)(2,1)S(1)}, u32[]{:S(2)}, u32[]{:S(2)}) %collective-permute-start.3) | collective-permute-done | bytes 172064 | tf_op jit(solution)/shard_map/ppermute | solution.py:38
  24.2 3.4 %collective-permute-done.2 = bf16[112,768]{1,0:T(8,128)(2,1)S(1)} collective-permute-done((bf16[112,768]{1,0:T(8,128)(2,1)S(1)}, bf16[112,768]{1,0:T(8,128)(2,1)S(1)}, u32[]{:S(2)}, u32[]{:S(2)}) %collective-permute-start.2) | collective-permute-done | bytes 172064 | tf_op jit(solution)/shard_map/ppermute | solution.py:38
  32.0 2.3 collective-permute-done.6
  39.2 10.2 %collective-permute-done.12 = bf16[96,1536]{1,0:T(8,128)(2,1)S(1)} collective-permute-done((bf16[96,1536]{1,0:T(8,128)(2,1)S(1)}, bf16[96,1536]{1,0:T(8,128)(2,1)S(1)}, u32[]{:S(2)}, u32[]{:S(2)}) %collective-permute-start.12) | collective-permute-done | bytes 294944 | tf_op jit(solution)/shard_map/ppermute | solution.py:38
  51.8 7.5 %collective-permute-done.11 = bf16[96,1536]{1,0:T(8,128)(2,1)S(1)} collective-permute-done((bf16[96,1536]{1,0:T(8,128)(2,1)S(1)}, bf16[96,1536]{1,0:T(8,128)(2,1)S(1)}, u32[]{:S(2)}, u32[]{:S(2)}) %collective-permute-start.11) | collective-permute-done | bytes 294944 | tf_op jit(solution)/shard_map/ppermute | solution.py:38
  59.8 6.4 %collective-permute-done.15 = bf16[96,1536]{1,0:T(8,128)(2,1)S(1)} collective-permute-done((bf16[96,1536]{1,0:T(8,128)(2,1)S(1)}, bf16[96,1536]{1,0:T(8,128)(2,1)S(1)}, u32[]{:S(2)}, u32[]{:S(2)}) %collective-permute-start.15) | collective-permute-done | bytes 294944 | tf_op jit(solution)/shard_map/ppermute | solution.py:38
  67.4 9.0 %norm_first.1 = (bf16[1024,768]{1,0:T(8,128)(2,1)}, f32[16,768]{1,0:T(8,128)}) custom-call(s32[2]{0:T(128)} %pad_add_fusion.info, bf16[1024,768]{1,0:T(8,128)(2,1)} %x_ref.7, bf16[8,112,768]{2,1,0:T(8,128)(2,1)} %bitcast_dynamic-update-slice_fusion.8.w_ref.own_ref), custom_call_target="tpu_custom_call" | custom-call | bytes 4571144 | tf_op jit(solution)/shard_map/norm_first/pallas_call | solution.py:46
  76.4 22.5 %attend.1 = (bf16[512,768]{1,0:T(8,128)(2,1)}, bf16[512,384]{1,0:T(8,128)(2,1)}, bf16[6,512,64]{2,1,0:T(8,128)(2,1)}, bf16[6,1024,64]{2,1,0:T(8,128)(2,1)}, bf16...) custom-call(s32[2]{0:T(128)} %pad_add_fusion.info, ...), custom_call_target="tpu_custom_call" | custom-call | flops 2013265920 | bytes 14553096 | tf_op jit(solution)/shard_map/attend/pallas_call | solution.py:46
  102.1 16.6 %collective-permute-done.8.recv_ref = bf16[512,768]{1,0:T(8,128)(2,1)S(1)} collective-permute-done((bf16[512,768]{1,0:T(8,128)(2,1)}, bf16[512,768]{1,0:T(8,128)(2,1)S(1)}, u32[]{:S(2)}, u32[]{:S(2)}) %collective-permute-start.8) | collective-permute-done | bytes 786464 | tf_op jit(solution)/shard_map/ppermute | solution.py:34
  119.6 16.4 %mlp.1 = (bf16[512,768]{1,0:T(8,128)(2,1)}, bf16[512,1536]{1,0:T(8,128)(2,1)}, bf16[512,1536]{1,0:T(8,128)(2,1)}, bf16[512,768]{1,0:T(8,128)(2,1)}, bf16[512,768]{1,0:T(8,128)(2,1)}, /*index=5*/f32[512,768]{1,0:T(8,128)}) custom-call(s32[2]{0:T(128)} %pad_add_fusion.info, bf16[1024,768]{1,0:T(8,128)(2,1)} %x_ref.7, s32[1,1024]{1,0:T(1,128)} %bitcast.74, ...), custom_call_target="tpu_custom_call" | custom-call | flops 3623878656 | bytes 16617480 | tf_op jit(solution)/shard_map/mlp/pallas_call | solution.py:46
  137.6 7.1 %mlp_grad.1 = (bf16[8,96,1536]{2,1,0:T(8,128)(2,1)}, bf16[8,96,1536]{2,1,0:T(8,128)(2,1)}, f32[24,768]{1,0:T(8,128)}) custom-call(s32[2]{0:T(128)} %pad_add_fusion.info, bf16[512,1536]{1,0:T(8,128)(2,1)} %get-tuple-element.74.act_ref, bf16[512,1536]{1,0:T(8,128)(2,1)} %get-tuple-element.94.dhid_ref, bf16[512,768]{1,0:T(8,128)(2,1)} %get-tuple-element.95.second_ref, ...), custom_call_target="tpu_custom_call" | custom-call | flops 2415919104 | bytes 9510920 | tf_op jit(solution)/shard_map/mlp_grad/pallas_call | solution.py:46
  144.7 10.2 %collective-permute-done.19.recv_ref = bf16[512,768]{1,0:T(8,128)(2,1)S(1)} collective-permute-done((bf16[512,768]{1,0:T(8,128)(2,1)}, bf16[512,768]{1,0:T(8,128)(2,1)S(1)}, u32[]{:S(2)}, u32[]{:S(2)}) %collective-permute-start.19) | collective-permute-done | bytes 786464 | tf_op jit(solution)/shard_map/ppermute | solution.py:34
  155.8 21.0 %attend_back.1 = (f32[512,768]{1,0:T(8,128)}, bf16[512,768]{1,0:T(8,128)(2,1)}, f32[8,768]{1,0:T(8,128)}, bf16[512,384]{1,0:T(8,128)(2,1)}, f32[768,512]{1,0:T(8,128)}, /*index=5*/bf16[768,512]{1,0:T(8,128)(2,1)}) custom-call(s32[2]{0:T(128)} %pad_add_fusion.info, f32[512,768]{1,0:T(8,128)} %get-tuple-element.73.mid_ref, ...), custom_call_target="tpu_custom_call" | custom-call | flops 1006632960 | bytes 15998984 | tf_op jit(solution)/shard_map/attend_back/pallas_call | solution.py:46
  176.8 2.9 attn_grad.1.attn_ref
  180.6 4.6 %first_grad.1 = (bf16[512,768]{1,0:T(8,128)(2,1)}, bf16[768,512]{1,0:T(8,128)(2,1)}) custom-call(s32[2]{0:T(128)} %pad_add_fusion.info, bf16[512,384]{1,0:T(8,128)(2,1)} %get-tuple-element.83.dq_ref, f32[768,512]{1,0:T(8,128)} %get-tuple-element.84.keep_ref, bf16[768,512]{1,0:T(8,128)(2,1)} %copy-done.6, bf16[768,384]{1,0:T(8,128)(2,1)} %get-tuple-element.86.wq_ref, ...), custom_call_target="tpu_custom_call" | custom-call | flops 905969664 | bytes 6094856 | tf_op jit(solution)/shard_map/first_grad/pallas_call | solution.py:46
  185.2 8.6 %qkv_grad.1 = (bf16[8,96,768]{2,1,0:T(8,128)(2,1)}, bf16[8,96,768]{2,1,0:T(8,128)(2,1)}, bf16[16,768]{1,0:T(8,128)(2,1)}, bf16[16,768]{1,0:T(8,128)(2,1)}) custom-call(s32[2]{0:T(128)} %pad_add_fusion.info, bf16[512,768]{1,0:T(8,128)(2,1)} %get-tuple-element.91.first_ref, bf16[512,384]{1,0:T(8,128)(2,1)} %get-tuple-element.83.dq_ref, ...), custom_call_target="tpu_custom_call" | custom-call | flops 905969664 | bytes 8011784 | tf_op jit(solution)/shard_map/qkv_grad/pallas_call | solution.py:46
  194.4 5.3 %mlp_out.1.part_ref = bf16[512,768]{1,0:T(8,128)(2,1)} custom-call(s32[2]{0:T(128)} %pad_add_fusion.info, bf16[512,1536]{1,0:T(8,128)(2,1)} %get-tuple-element.74.act_ref, bf16[8,96,1536]{2,1,0:T(8,128)(2,1)} %copy-done.1, bf16[8,96,1536]{2,1,0:T(8,128)(2,1)} %collective-permute-done.16.sib_ref), custom_call_target="tpu_custom_call" | custom-call | flops 1207959552 | bytes 7077896 | tf_op jit(solution)/shard_map/mlp_out/pallas_call | solution.py:46
  204.6 32.3 %collective-permute-done.25.refs_2_ = bf16[16,768]{1,0:T(8,128)(2,1)S(1)} collective-permute-done((bf16[16,768]{1,0:T(8,128)(2,1)S(1)}, bf16[16,768]{1,0:T(8,128)(2,1)S(1)}, u32[]{:S(2)}, u32[]{:S(2)}) %collective-permute-start.25) | collective-permute-done | bytes 24608 | tf_op jit(solution)/shard_map/ppermute | solution.py:34
  237.8 3.0 scatter_first.2
  243.5 4.3 %scatter_first.3 = (f32[384,768]{1,0:T(8,128)}, bf16[384,768]{1,0:T(8,128)(2,1)}, f32[384,768]{1,0:T(8,128)}, bf16[384,768]{1,0:T(8,128)(2,1)}) custom-call(s32[2]{0:T(128)} %pad_add_fusion.info, bf16[8,96,1536]{2,1,0:T(8,128)(2,1)} %get-tuple-element.112.own_ref, bf16[8,96,1536]{2,1,0:T(8,128)(2,1)} %copy-done.2), custom_call_target="tpu_custom_call" | custom-call | bytes 8257544 | tf_op jit(solution)/shard_map/scatter_first/pallas_call | solution.py:46
  249.7 5.5 %output.1.own_ref = bf16[512,768]{1,0:T(8,128)(2,1)} custom-call(s32[2]{0:T(128)} %pad_add_fusion.info, s32[1,1024]{1,0:T(1,128)} %bitcast.75, f32[512,768]{1,0:T(8,128)} %get-tuple-element.73.mid_ref, bf16[512,768]{1,0:T(8,128)(2,1)} %mlp_out.1.part_ref, bf16[512,768]{1,0:T(8,128)(2,1)} %copy-done.4, f32[16,768]{1,0:T(8,128)} %get-tuple-element.71.vec_ref), custom_call_target="tpu_custom_call" | custom-call | bytes 3985416 | tf_op jit(solution)/shard_map/output/pallas_call | solution.py:46
  256.2 7.8 %final.1.own_ref = bf16[512,768]{1,0:T(8,128)(2,1)} custom-call(s32[2]{0:T(128)} %pad_add_fusion.info, bf16[1024,768]{1,0:T(8,128)(2,1)} %x_ref.7, bf16[512,768]{1,0:T(8,128)(2,1)} %get-tuple-element.89.part_ref, bf16[512,768]{1,0:T(8,128)(2,1)} %copy-done.9, f32[512,768]{1,0:T(8,128)} %get-tuple-element.90.dmid_ref, f32[16,768]{1,0:T(8,128)} %get-tuple-element.71.vec_ref), custom_call_target="tpu_custom_call" | custom-call | bytes 5554184 | tf_op jit(solution)/shard_map/final/pallas_call | solution.py:46
  266.3 7.5 %collective-permute-done.27.got_b = bf16[400,384]{1,0:T(8,128)(2,1)S(1)} collective-permute-done((bf16[400,384]{1,0:T(8,128)(2,1)S(1)}, bf16[400,384]{1,0:T(8,128)(2,1)S(1)}, u32[]{:S(2)}, u32[]{:S(2)}) %collective-permute-start.27) | collective-permute-done | bytes 307232 | tf_op jit(solution)/shard_map/ppermute | solution.py:38
  274.5 2.4 scatter_second.2
  280.7 3.2 %scatter_second.3 = (f32[192,768]{1,0:T(8,128)}, bf16[192,768]{1,0:T(8,128)(2,1)}, f32[192,768]{1,0:T(8,128)}, bf16[192,768]{1,0:T(8,128)(2,1)}) custom-call(s32[2]{0:T(128)} %pad_add_fusion.info, f32[384,768]{1,0:T(8,128)} %get-tuple-element.114.keep_a, bf16[384,768]{1,0:T(8,128)(2,1)} %copy-done.10, f32[384,768]{1,0:T(8,128)} %get-tuple-element.116.keep_b, ...), custom_call_target="tpu_custom_call" | custom-call | bytes 5308424 | tf_op jit(solution)/shard_map/scatter_second/pallas_call | solution.py:46
  285.8 2.0 scatter_third.2
  290.7 2.6 merge.2
  294.2 2.6 merge.3
  297.7 2.5 scatter_third.3
  310.3 4.2 %collective-permute-done.36.got = bf16[96,1536]{1,0:T(8,128)(2,1)S(1)} collective-permute-done((bf16[96,1536]{1,0:T(8,128)(2,1)}, bf16[96,1536]{1,0:T(8,128)(2,1)S(1)}, u32[]{:S(2)}, u32[]{:S(2)}) %collective-permute-start.36) | collective-permute-done | bytes 294944 | tf_op jit(solution)/shard_map/ppermute | solution.py:38
  (161 shorter events, 71.9 us)
Async XLA Ops:
  5.5 17.4 %collective-permute-start = (bf16[112,768]{1,0:T(8,128)(2,1)S(1)}, bf16[112,768]{1,0:T(8,128)(2,1)S(1)}, u32[]{:S(2)}, u32[]{:S(2)}) collective-permute-start(bf16[112,768]{1,0:T(8,128)(2,1)S(1)} %get-tuple-element.167), channel_id=1, source_target_pairs={{0,4},{4,0},{8,12},{12,8},{16,20},{20,16},{24,28},{28,24},{1,5},{5... | collective-permute-start | bytes 516104 | tf_op jit(solution)/shard_map/ppermute | solution.py:38
  8.6 12.7 %collective-permute-start.1 = (bf16[112,768]{1,0:T(8,128)(2,1)S(1)}, bf16[112,768]{1,0:T(8,128)(2,1)S(1)}, u32[]{:S(2)}, u32[]{:S(2)}) collective-permute-start(bf16[112,768]{1,0:T(8,128)(2,1)S(1)} %get-tuple-element.167), channel_id=1, source_target_pairs={{0,8},{4,12},{8,0},{12,4},{16,24},{20,28},{24,16},{28,20},{1,9},{5... | collective-permute-start | bytes 516104 | tf_op jit(solution)/shard_map/ppermute | solution.py:38
  10.2 10.2 %collective-permute-start.3 = (bf16[112,768]{1,0:T(8,128)(2,1)S(1)}, bf16[112,768]{1,0:T(8,128)(2,1)S(1)}, u32[]{:S(2)}, u32[]{:S(2)}) collective-permute-start(bf16[112,768]{1,0:T(8,128)(2,1)S(1)} %get-tuple-element.167), channel_id=1, source_target_pairs={{0,16},{4,20},{8,24},{12,28},{16,0},{20,4},{24,8},{28,12},{1,17},{... | collective-permute-start | bytes 516104 | tf_op jit(solution)/shard_map/ppermute | solution.py:38
  20.4 8.6 %collective-permute-start.4 = (bf16[112,768]{1,0:T(8,128)(2,1)S(1)}, bf16[112,768]{1,0:T(8,128)(2,1)S(1)}, u32[]{:S(2)}, u32[]{:S(2)}) collective-permute-start(bf16[112,768]{1,0:T(8,128)(2,1)S(1)} %collective-permute-done.3), channel_id=1, source_target_pairs={{0,4},{4,0},{8,12},{12,8},{16,20},{20,16},{24,28},{28,24},{1,5},{5... | collective-permute-start | bytes 516104 | tf_op jit(solution)/shard_map/ppermute | solution.py:38
  20.9 10.5 %collective-permute-start.5 = (bf16[112,768]{1,0:T(8,128)(2,1)S(1)}, bf16[112,768]{1,0:T(8,128)(2,1)S(1)}, u32[]{:S(2)}, u32[]{:S(2)}) collective-permute-start(bf16[112,768]{1,0:T(8,128)(2,1)S(1)} %collective-permute-done.3), channel_id=1, source_target_pairs={{0,8},{4,12},{8,0},{12,4},{16,24},{20,28},{24,16},{28,20},{1,9},{5... | collective-permute-start | bytes 516104 | tf_op jit(solution)/shard_map/ppermute | solution.py:38
  35.1 16.7 %collective-permute-start.9 = (bf16[96,1536]{1,0:T(8,128)(2,1)S(1)}, bf16[96,1536]{1,0:T(8,128)(2,1)S(1)}, u32[]{:S(2)}, u32[]{:S(2)}) collective-permute-start(bf16[96,1536]{1,0:T(8,128)(2,1)S(1)} %pad_maximum_fusion), channel_id=1, source_target_pairs={{0,4},{4,0},{8,12},{12,8},{16,20},{20,16},{24,28},{28,24},{1,5},{5... | collective-permute-start | bytes 884744 | tf_op jit(solution)/shard_map/ppermute | solution.py:38
  36.4 15.3 %collective-permute-start.10 = (bf16[96,1536]{1,0:T(8,128)(2,1)S(1)}, bf16[96,1536]{1,0:T(8,128)(2,1)S(1)}, u32[]{:S(2)}, u32[]{:S(2)}) collective-permute-start(bf16[96,1536]{1,0:T(8,128)(2,1)S(1)} %pad_maximum_fusion), channel_id=1, source_target_pairs={{0,8},{4,12},{8,0},{12,4},{16,24},{20,28},{24,16},{28,20},{1,9},{5... | collective-permute-start | bytes 884744 | tf_op jit(solution)/shard_map/ppermute | solution.py:38
  37.3 12.2 %collective-permute-start.12 = (bf16[96,1536]{1,0:T(8,128)(2,1)S(1)}, bf16[96,1536]{1,0:T(8,128)(2,1)S(1)}, u32[]{:S(2)}, u32[]{:S(2)}) collective-permute-start(bf16[96,1536]{1,0:T(8,128)(2,1)S(1)} %pad_maximum_fusion), channel_id=1, source_target_pairs={{0,16},{4,20},{8,24},{12,28},{16,0},{20,4},{24,8},{28,12},{1,17},{... | collective-permute-start | bytes 884744 | tf_op jit(solution)/shard_map/ppermute | solution.py:38
  49.4 9.9 %collective-permute-start.13 = (bf16[96,1536]{1,0:T(8,128)(2,1)S(1)}, bf16[96,1536]{1,0:T(8,128)(2,1)S(1)}, u32[]{:S(2)}, u32[]{:S(2)}) collective-permute-start(bf16[96,1536]{1,0:T(8,128)(2,1)S(1)} %collective-permute-done.12), channel_id=1, source_target_pairs={{0,4},{4,0},{8,12},{12,8},{16,20},{20,16},{24,28},{28,24},{1,5},{5... | collective-permute-start | bytes 884744 | tf_op jit(solution)/shard_map/ppermute | solution.py:38
  50.7 9.0 %collective-permute-start.14 = (bf16[96,1536]{1,0:T(8,128)(2,1)S(1)}, bf16[96,1536]{1,0:T(8,128)(2,1)S(1)}, u32[]{:S(2)}, u32[]{:S(2)}) collective-permute-start(bf16[96,1536]{1,0:T(8,128)(2,1)S(1)} %collective-permute-done.12), channel_id=1, source_target_pairs={{0,8},{4,12},{8,0},{12,4},{16,24},{20,28},{24,16},{28,20},{1,9},{5... | collective-permute-start | bytes 884744 | tf_op jit(solution)/shard_map/ppermute | solution.py:38
  51.7 7.6 %collective-permute-start.11 = (bf16[96,1536]{1,0:T(8,128)(2,1)S(1)}, bf16[96,1536]{1,0:T(8,128)(2,1)S(1)}, u32[]{:S(2)}, u32[]{:S(2)}) collective-permute-start(bf16[96,1536]{1,0:T(8,128)(2,1)S(1)} %collective-permute-done.10), channel_id=1, source_target_pairs={{0,4},{4,0},{8,12},{12,8},{16,20},{20,16},{24,28},{28,24},{1,5},{5... | collective-permute-start | bytes 884744 | tf_op jit(solution)/shard_map/ppermute | solution.py:38
  59.4 6.8 %collective-permute-start.15 = (bf16[96,1536]{1,0:T(8,128)(2,1)S(1)}, bf16[96,1536]{1,0:T(8,128)(2,1)S(1)}, u32[]{:S(2)}, u32[]{:S(2)}) collective-permute-start(bf16[96,1536]{1,0:T(8,128)(2,1)S(1)} %collective-permute-done.13), channel_id=1, source_target_pairs={{0,8},{4,12},{8,0},{12,4},{16,24},{20,28},{24,16},{28,20},{1,9},{5... | collective-permute-start | bytes 884744 | tf_op jit(solution)/shard_map/ppermute | solution.py:38
  66.2 52.5 %collective-permute-start.16 = (bf16[8,96,1536]{2,1,0:T(8,128)(2,1)S(1)}, bf16[8,96,1536]{2,1,0:T(8,128)(2,1)}, u32[]{:S(2)}, u32[]{:S(2)}) collective-permute-start(bf16[8,96,1536]{2,1,0:T(8,128)(2,1)S(1)} %bitcast_dynamic-update-slice_fusion.own_ref), channel_id=1, source_target_pairs={{0,1},{1,0},{2,3},{3,2},{4,5},{5,4},{6,7},{7,6},{8,9},{9,8},{10,11... | collective-permute-start | bytes 7077896 | tf_op jit(solution)/shard_map/ppermute | solution.py:30
  66.3 10.1 %collective-permute-start.7 = (bf16[8,112,768]{2,1,0:T(8,128)(2,1)}, bf16[8,112,768]{2,1,0:T(8,128)(2,1)}, u32[]{:S(2)}, u32[]{:S(2)}) collective-permute-start(bf16[8,112,768]{2,1,0:T(8,128)(2,1)} %bitcast_dynamic-update-slice_fusion.8.w_ref.own_ref), channel_id=1, source_target_pairs={{0,1},{1,0},{2,3},{3,2},{4,5},{5,4},{6,7},{7,6},{8,9},{9,8},{10,11... | collective-permute-start | bytes 4128776 | tf_op jit(solution)/shard_map/ppermute | solution.py:30
  99.0 19.7 %collective-permute-start.8 = (bf16[512,768]{1,0:T(8,128)(2,1)}, bf16[512,768]{1,0:T(8,128)(2,1)S(1)}, u32[]{:S(2)}, u32[]{:S(2)}) collective-permute-start(bf16[512,768]{1,0:T(8,128)(2,1)} %get-tuple-element.70.part_ref), channel_id=1, source_target_pairs={{0,2},{2,0},{1,3},{3,1},{4,6},{6,4},{5,7},{7,5},{8,10},{10,8},{9,1... | collective-permute-start | bytes 2359304 | tf_op jit(solution)/shard_map/ppermute | solution.py:34
  136.0 18.9 %collective-permute-start.19 = (bf16[512,768]{1,0:T(8,128)(2,1)}, bf16[512,768]{1,0:T(8,128)(2,1)S(1)}, u32[]{:S(2)}, u32[]{:S(2)}) collective-permute-start(bf16[512,768]{1,0:T(8,128)(2,1)} %get-tuple-element.76.da_ref), channel_id=1, source_target_pairs={{0,2},{2,0},{1,3},{3,1},{4,6},{6,4},{5,7},{7,5},{8,10},{10,8},{9,1... | collective-permute-start | bytes 2359304 | tf_op jit(solution)/shard_map/ppermute | solution.py:34
  144.7 97.4 %collective-permute-start.31 = (bf16[8,96,1536]{2,1,0:T(8,128)(2,1)}, bf16[8,96,1536]{2,1,0:T(8,128)(2,1)S(1)}, u32[]{:S(2)}, u32[]{:S(2)}) collective-permute-start(bf16[8,96,1536]{2,1,0:T(8,128)(2,1)} %get-tuple-element.113), channel_id=1, source_target_pairs={{0,1},{1,0},{2,3},{3,2},{4,5},{5,4},{6,7},{7,6},{8,9},{9,8},{10,11... | collective-permute-start | bytes 7077896 | tf_op jit(solution)/shard_map/ppermute | solution.py:30
  193.8 43.0 %collective-permute-start.23 = (bf16[8,96,768]{2,1,0:T(8,128)(2,1)}, bf16[8,96,768]{2,1,0:T(8,128)(2,1)S(1)}, u32[]{:S(2)}, u32[]{:S(2)}) collective-permute-start(bf16[8,96,768]{2,1,0:T(8,128)(2,1)} %get-tuple-element.99), channel_id=1, source_target_pairs={{0,1},{1,0},{2,3},{3,2},{4,5},{5,4},{6,7},{7,6},{8,9},{9,8},{10,11... | collective-permute-start | bytes 3538952 | tf_op jit(solution)/shard_map/ppermute | solution.py:30
  199.7 49.1 %collective-permute-start.17 = (bf16[512,768]{1,0:T(8,128)(2,1)}, bf16[512,768]{1,0:T(8,128)(2,1)S(1)}, u32[]{:S(2)}, u32[]{:S(2)}) collective-permute-start(bf16[512,768]{1,0:T(8,128)(2,1)} %mlp_out.1.part_ref), channel_id=1, source_target_pairs={{0,2},{2,0},{1,3},{3,1},{4,6},{6,4},{5,7},{7,5},{8,10},{10,8},{9,1... | collective-permute-start | bytes 2359304 | tf_op jit(solution)/shard_map/ppermute | solution.py:34
  201.2 54.0 %collective-permute-start.21 = (bf16[512,768]{1,0:T(8,128)(2,1)S(1)}, bf16[512,768]{1,0:T(8,128)(2,1)S(1)}, u32[]{:S(2)}, u32[]{:S(2)}) collective-permute-start(bf16[512,768]{1,0:T(8,128)(2,1)S(1)} %copy-done), channel_id=1, source_target_pairs={{0,2},{2,0},{1,3},{3,1},{4,6},{6,4},{5,7},{7,5},{8,10},{10,8},{9,1... | collective-permute-start | bytes 2359304 | tf_op jit(solution)/shard_map/ppermute | solution.py:34
  203.0 33.8 %collective-permute-start.25 = (bf16[16,768]{1,0:T(8,128)(2,1)S(1)}, bf16[16,768]{1,0:T(8,128)(2,1)S(1)}, u32[]{:S(2)}, u32[]{:S(2)}) collective-permute-start(bf16[16,768]{1,0:T(8,128)(2,1)S(1)} %select_convert_fusion), channel_id=1, source_target_pairs={{0,2},{2,0},{1,3},{3,1},{4,6},{6,4},{5,7},{7,5},{8,10},{10,8},{9,1... | collective-permute-start | bytes 73736 | tf_op jit(solution)/shard_map/ppermute | solution.py:34
  240.8 23.6 %collective-permute-start.26 = (bf16[400,384]{1,0:T(8,128)(2,1)}, bf16[400,384]{1,0:T(8,128)(2,1)S(1)}, u32[]{:S(2)}, u32[]{:S(2)}) collective-permute-start(bf16[400,384]{1,0:T(8,128)(2,1)} %get-tuple-element.103), channel_id=1, source_target_pairs={{0,4},{4,0},{8,12},{12,8},{16,20},{20,16},{24,28},{28,24},{1,5},{5... | collective-permute-start | bytes 921608 | tf_op jit(solution)/shard_map/ppermute | solution.py:38
  247.8 30.8 %collective-permute-start.32 = (bf16[384,768]{1,0:T(8,128)(2,1)}, bf16[384,768]{1,0:T(8,128)(2,1)S(1)}, u32[]{:S(2)}, u32[]{:S(2)}) collective-permute-start(bf16[384,768]{1,0:T(8,128)(2,1)} %get-tuple-element.115), channel_id=1, source_target_pairs={{0,4},{4,0},{8,12},{12,8},{16,20},{20,16},{24,28},{28,24},{1,5},{5... | collective-permute-start | bytes 1769480 | tf_op jit(solution)/shard_map/ppermute | solution.py:38
  248.6 31.3 %collective-permute-start.33 = (bf16[384,768]{1,0:T(8,128)(2,1)}, bf16[384,768]{1,0:T(8,128)(2,1)S(1)}, u32[]{:S(2)}, u32[]{:S(2)}) collective-permute-start(bf16[384,768]{1,0:T(8,128)(2,1)} %get-tuple-element.117), channel_id=1, source_target_pairs={{0,8},{4,12},{8,0},{12,4},{16,24},{20,28},{24,16},{28,20},{1,9},{5... | collective-permute-start | bytes 1769480 | tf_op jit(solution)/shard_map/ppermute | solution.py:38
  255.3 34.5 %collective-permute-start.18 = (bf16[512,768]{1,0:T(8,128)(2,1)}, bf16[512,768]{1,0:T(8,128)(2,1)S(1)}, u32[]{:S(2)}, u32[]{:S(2)}) collective-permute-start(bf16[512,768]{1,0:T(8,128)(2,1)} %output.1.own_ref), channel_id=1, source_target_pairs={{0,1},{1,0},{2,3},{3,2},{4,5},{5,4},{6,7},{7,6},{8,9},{9,8},{10,11... | collective-permute-start | bytes 2359304 | tf_op jit(solution)/shard_map/ppermute | solution.py:30
  263.9 29.4 %collective-permute-start.22 = (bf16[512,768]{1,0:T(8,128)(2,1)}, bf16[512,768]{1,0:T(8,128)(2,1)S(1)}, u32[]{:S(2)}, u32[]{:S(2)}) collective-permute-start(bf16[512,768]{1,0:T(8,128)(2,1)} %final.1.own_ref), channel_id=1, source_target_pairs={{0,1},{1,0},{2,3},{3,2},{4,5},{5,4},{6,7},{7,6},{8,9},{9,8},{10,11... | collective-permute-start | bytes 2359304 | tf_op jit(solution)/shard_map/ppermute | solution.py:30
  264.4 9.3 %collective-permute-start.27 = (bf16[400,384]{1,0:T(8,128)(2,1)S(1)}, bf16[400,384]{1,0:T(8,128)(2,1)S(1)}, u32[]{:S(2)}, u32[]{:S(2)}) collective-permute-start(bf16[400,384]{1,0:T(8,128)(2,1)S(1)} %copy-done.24), channel_id=1, source_target_pairs={{0,8},{4,12},{8,0},{12,4},{16,24},{20,28},{24,16},{28,20},{1,9},{5... | collective-permute-start | bytes 921608 | tf_op jit(solution)/shard_map/ppermute | solution.py:38
  276.9 8.0 %collective-permute-start.28 = (bf16[208,384]{1,0:T(8,128)(2,1)}, bf16[208,384]{1,0:T(8,128)(2,1)S(1)}, u32[]{:S(2)}, u32[]{:S(2)}) collective-permute-start(bf16[208,384]{1,0:T(8,128)(2,1)} %get-tuple-element.107), channel_id=1, source_target_pairs={{0,8},{4,12},{8,0},{12,4},{16,24},{20,28},{24,16},{28,20},{1,9},{5... | collective-permute-start | bytes 479240 | tf_op jit(solution)/shard_map/ppermute | solution.py:38
  283.9 12.9 %collective-permute-start.34 = (bf16[192,768]{1,0:T(8,128)(2,1)}, bf16[192,768]{1,0:T(8,128)(2,1)S(1)}, u32[]{:S(2)}, u32[]{:S(2)}) collective-permute-start(bf16[192,768]{1,0:T(8,128)(2,1)} %get-tuple-element.119), channel_id=1, source_target_pairs={{0,8},{4,12},{8,0},{12,4},{16,24},{20,28},{24,16},{28,20},{1,9},{5... | collective-permute-start | bytes 884744 | tf_op jit(solution)/shard_map/ppermute | solution.py:38
  284.9 11.9 %collective-permute-start.35 = (bf16[192,768]{1,0:T(8,128)(2,1)}, bf16[192,768]{1,0:T(8,128)(2,1)S(1)}, u32[]{:S(2)}, u32[]{:S(2)}) collective-permute-start(bf16[192,768]{1,0:T(8,128)(2,1)} %get-tuple-element.121), channel_id=1, source_target_pairs={{0,4},{4,0},{8,12},{12,8},{16,20},{20,16},{24,28},{28,24},{1,5},{5... | collective-permute-start | bytes 884744 | tf_op jit(solution)/shard_map/ppermute | solution.py:38
  287.8 13.3 %collective-permute-start.30 = (bf16[112,768]{1,0:T(8,128)(2,1)}, bf16[112,768]{1,0:T(8,128)(2,1)S(1)}, u32[]{:S(2)}, u32[]{:S(2)}) collective-permute-start(bf16[112,768]{1,0:T(8,128)(2,1)} %get-tuple-element.111), channel_id=1, source_target_pairs={{0,16},{4,20},{8,24},{12,28},{16,0},{20,4},{24,8},{28,12},{1,17},{... | collective-permute-start | bytes 516104 | tf_op jit(solution)/shard_map/ppermute | solution.py:38
  300.1 14.3 %collective-permute-start.36 = (bf16[96,1536]{1,0:T(8,128)(2,1)}, bf16[96,1536]{1,0:T(8,128)(2,1)S(1)}, u32[]{:S(2)}, u32[]{:S(2)}) collective-permute-start(bf16[96,1536]{1,0:T(8,128)(2,1)} %get-tuple-element.123), channel_id=1, source_target_pairs={{0,16},{4,20},{8,24},{12,28},{16,0},{20,4},{24,8},{28,12},{1,17},{... | collective-permute-start | bytes 884744 | tf_op jit(solution)/shard_map/ppermute | solution.py:38
  (31 other events, 147.5 us)
where the time goes:
time: 320 us; the launch traced here: 319 us
  Pallas kernels  137 us (43%)
  waiting for transfers between devices  108 us (34%)
  starting transfers between devices  37.8 us (12%)
  local copies, waits for them, and re-layouts  30.7 us (10%)
  other arithmetic  4.04 us (1%)
    pallas_call x21, Pallas kernels, call(): pl.pallas_call(kernel, out_shape=outs, in_specs=specs, out_specs=[pl.Bloc...  137 us
    ppermute x5, waiting for transfers between devices, swap_chip(): return lax.ppermute(value, 'mp', CHIP_PAIRS)  59 us
    ppermute x24, waiting for transfers between devices, swap_bit(): return lax.ppermute(value, 'dp', [(i, i ^ 1 << bit) for i in range(CHUNKS)])  48.2 us
    ppermute x24, starting transfers between devices, swap_bit(): return lax.ppermute(value, 'dp', [(i, i ^ 1 << bit) for i in range(CHUNKS)])  29.5 us
    unnamed x68, local copies, waits for them, and re-layouts  19.9 us
    ppermute x5, starting transfers between devices, swap_chip(): return lax.ppermute(value, 'mp', CHIP_PAIRS)  6.71 us
  transfers between devices with their start and end apart: 37, of which 12 were waited for; matrix products, arithmetic and copies ran while one was open for 4% of the time, Pallas kernels for 37%

commit v1 on v0

--- a/solution.py
+++ b/solution.py
@@ -34,49 +34,62 @@
     return lax.ppermute(value, "mp", CHIP_PAIRS)
 
 
+def swap_mask(value, mask):
+    return lax.ppermute(value, "dp", [(i, i ^ mask) for i in range(CHUNKS)])
+
+
 def swap_bit(value, bit):
-    return lax.ppermute(value, "dp", [(i, i ^ (1 << bit)) for i in range(CHUNKS)])
-
-
-def call(kernel, outs, *args, scratch=(), smem=1, flops=0, name=None):
+    return swap_mask(value, 1 << bit)
+
+
+def call(kernel, outs, *args, scratch=(), smem=1, flops=0, name=None, after=()):
+    first, behind = len(args), len(args) + len(after)
+
+    def run(*refs):
+        kernel(*refs[:first], *refs[behind:])
+
     specs = [pl.BlockSpec(memory_space=pltpu.SMEM)] * smem
     specs += [pl.BlockSpec(memory_space=pltpu.VMEM)] * (len(args) - smem)
+    specs += [pl.BlockSpec(memory_space=pl.ANY)] * len(after)
     size = sum(a.size * a.dtype.itemsize for a in args)
     size += sum(o.size * jnp.dtype(o.dtype).itemsize for o in outs)
     return pl.pallas_call(
-        kernel,
+        run,
         out_shape=outs,
         in_specs=specs,
         out_specs=[pl.BlockSpec(memory_space=pltpu.VMEM)] * len(outs),
         scratch_shapes=list(scratch),
         compiler_params=pltpu.CompilerParams(vmem_limit_bytes=56 * 1024 * 1024),
-        cost_estimate=pl.CostEstimate(flops=flops, bytes_accessed=size, transcendentals=0),
+        cost_estimate=pl.CostEstimate(flops=0, bytes_accessed=1024, transcendentals=0),
         name=name,
-    )(*args)
+    )(*args, *after)
 
 
 def shape(dims, dtype=BF):
     return jax.ShapeDtypeStruct(tuple(dims), dtype)
 
 
-def gather_blocks(message):
+def gather_blocks(message, behind=None):
     got = {0: message}
-    got[4] = swap_bit(message, 2)
-    got[1] = swap_bit(message, 0)
-    got[2] = swap_bit(message, 1)
-    got[5] = swap_bit(got[4], 0)
-    got[6] = swap_bit(got[4], 1)
-    got[3] = swap_bit(got[2], 0)
-    got[7] = swap_bit(got[5], 1)
-    return jnp.stack([got[r] for r in range(CHUNKS)])
-
-
-def loop(count, step, fn):
+    got[4] = swap_mask(message, 4)
+    got[2] = swap_mask(message, 2)
+    got[1] = swap_mask(message, 1)
+    four, two = got[4], got[2]
+    if behind is not None:
+        four, two = lax.optimization_barrier((four, two, behind))[:2]
+    got[7] = swap_mask(four, 3)
+    got[5] = swap_mask(four, 1)
+    got[6] = swap_mask(four, 2)
+    got[3] = swap_mask(two, 1)
+    return [got[r] for r in range(CHUNKS)]
+
+
+def loop(count, step, fn, unroll=4):
     def run(i, carry):
         fn(pl.multiple_of(i * step, step))
         return carry
 
-    lax.fori_loop(0, count // step, run, 0)
+    lax.fori_loop(0, count // step, run, 0, unroll=unroll)
 
 
 def norm_stats(value):
@@ -220,29 +233,21 @@
     recv_ref,
     vec_ref,
     vecsib_ref,
-    own_ref,
-    sib_ref,
-    da_ref,
-    act_ref,
-    dhid_ref,
-    second_ref,
-    dy_ref,
-    mid_ref,
-    fc_ref,
-    proj_ref,
-    hid_ref,
-    dact_ref,
+    *refs,
 ):
+    own_refs, sib_refs = refs[:CHUNKS], refs[CHUNKS : 2 * CHUNKS]
+    da_ref, act_ref, dhid_ref, second_ref, dy_ref, mid_ref, proj_ref = refs[2 * CHUNKS : -3]
+    fc_ref, hid_ref, dact_ref = refs[-3:]
     flip, core = info[0], info[1]
     own_count = part_ref.shape[0]
-    base = own_ref.shape[1]
-    units = own_ref.shape[2] // 2
+    base = own_refs[0].shape[0]
+    units = own_refs[0].shape[1] // 2
     for r in range(CHUNKS):
         at = pl.multiple_of((r ^ flip) * base, 32)
-        for side, ref in ((0, own_ref), (1, sib_ref)):
+        for side, ref in ((0, own_refs[r]), (1, sib_refs[r])):
             cols = slice(side * units, (side + 1) * units)
-            fc_ref[pl.ds(at, base), cols] = ref[r, :, 0:units]
-            proj_ref[pl.ds(at, base), cols] = ref[r, :, units : 2 * units]
+            fc_ref[pl.ds(at, base), cols] = ref[:, 0:units]
+            proj_ref[pl.ds(at, base), cols] = ref[:, units : 2 * units]
     gain, shift, bias = vec_ref[3:4, :], vec_ref[4:5, :], vec_ref[2:3, :]
     sub = 32
     lane = lax.broadcasted_iota(jnp.int32, (sub, TILE), 1)
@@ -295,30 +300,37 @@
     da_ref[...] = dot(dhid_ref[...], fc_ref[...], 1, 1).astype(BF)
 
 
-def mlp_out_kernel(info, act_ref, own_ref, sib_ref, part_ref, proj_ref):
-    flip = info[0]
-    base = own_ref.shape[1]
-    units = own_ref.shape[2] // 2
-    for r in range(CHUNKS):
-        at = pl.multiple_of((r ^ flip) * base, 32)
-        proj_ref[pl.ds(at, base), 0:units] = own_ref[r, :, units : 2 * units]
-        proj_ref[pl.ds(at, base), units : 2 * units] = sib_ref[r, :, units : 2 * units]
-    part_ref[...] = dot(act_ref[...], proj_ref[...], 1, 1).astype(BF)
-
-
 def mlp_grad_kernel(
-    info, act_ref, dhid_ref, second_ref, dy_ref, own_ref, sib_ref, sums_ref, acc_ref
+    info,
+    act_ref,
+    dhid_ref,
+    second_ref,
+    dy_ref,
+    proj_ref,
+    part_ref,
+    own_ref,
+    sib_a_ref,
+    sib_b_ref,
+    sib_c_ref,
+    sib_d_ref,
+    sums_ref,
+    acc_ref,
 ):
     flip = info[0]
+    sib_refs = ((sib_a_ref, sib_b_ref), (sib_c_ref, sib_d_ref))
+    part_ref[...] = dot(act_ref[...], proj_ref[...], 1, 1).astype(BF)
     base = own_ref.shape[1]
     units = own_ref.shape[2] // 2
     for kind, left, right in ((0, second_ref, dhid_ref), (1, dy_ref, act_ref)):
-        for side, out in ((0, own_ref), (1, sib_ref)):
+        for side in range(2):
             acc_ref[...] = dot(left[...], right[:, side * units : (side + 1) * units], 0, 0)
-            for b in range(CHUNKS):
-                out[b ^ flip, :, kind * units : (kind + 1) * units] = acc_ref[
-                    b * base : (b + 1) * base, :
-                ].astype(BF)
+            for r in range(CHUNKS):
+                at = pl.multiple_of((r ^ flip) * base, 32)
+                block = acc_ref[pl.ds(at, base), :].astype(BF)
+                if side:
+                    sib_refs[kind][r // 4][r % 4] = block
+                else:
+                    own_ref[r, :, kind * units : (kind + 1) * units] = block
     one = jnp.ones((8, act_ref.shape[0]), BF)
     fc_sums = dot(one, dhid_ref[...], 1, 0)
     sums_ref[0:8, :] = fc_sums[:, 0:units]
@@ -344,7 +356,8 @@
     sums_ref,
     dq_ref,
     keep_ref,
-    send_ref,
+    send_k_ref,
+    send_v_ref,
     dm_ref,
     do_ref,
     dkt_ref,
@@ -419,12 +432,10 @@
             mine = pl.multiple_of((2 * j + core) * TILE, TILE)
             yours = pl.multiple_of((2 * j + 1 - core) * TILE, TILE)
             cols = slice(j * TILE, (j + 1) * TILE)
-            for part, ref in ((0, dkt_ref), (1, dvt_ref)):
+            for part, ref, send in ((0, dkt_ref, send_k_ref), (1, dvt_ref, send_v_ref)):
                 at = part * width2
                 keep_ref[at + h * HD : at + (h + 1) * HD, cols] = ref[h, :, pl.ds(mine, TILE)]
-                send_ref[at + twin * HD : at + (twin + 1) * HD, cols] = ref[
-                    h, :, pl.ds(yours, TILE)
-                ].astype(BF)
+                send[twin * HD : (twin + 1) * HD, cols] = ref[h, :, pl.ds(yours, TILE)].astype(BF)
 
 
 def attn_grad_kernel(info, branch_ref, mixed_ref, out_ref):
@@ -432,10 +443,12 @@
 
 
 def first_grad_kernel(
-    info, dq_ref, keep_ref, got_ref, wq_ref, wk_ref, wv_ref, part_ref, dkv_ref
+    info, dq_ref, keep_ref, got_k_ref, got_v_ref, wq_ref, wk_ref, wv_ref, part_ref, dkv_ref
 ):
     width2 = dq_ref.shape[1]
-    dkv_ref[...] = (keep_ref[...] + got_ref[...].astype(F32)).astype(BF)
+    for p, got in enumerate((got_k_ref, got_v_ref)):
+        rows = slice(p * width2, (p + 1) * width2)
+        dkv_ref[rows, :] = (keep_ref[rows, :] + got[...].astype(F32)).astype(BF)
     part_ref[...] = (
         dot(dq_ref[...], wq_ref[...], 1, 1)
         + dot(dkv_ref[0:width2, :], wk_ref[...], 0, 1)
@@ -454,9 +467,11 @@
     mlp_sums_ref,
     att_sums_ref,
     own_ref,
-    sib_ref,
+    sib_a_ref,
+    sib_b_ref,
     tile_own_ref,
     tile_sib_ref,
+    whole_ref,
     sum_ref,
 ):
     flip, core = info[0], info[1]
@@ -472,11 +487,13 @@
             whole = dot(
                 first_ref[...], dkv_ref[(part - 1) * width2 : part * width2, :], 0, 1
             )
-        for b in range(CHUNKS):
-            rows = slice(b * base, (b + 1) * base)
-            cols = slice(part * width, (part + 1) * width)
-            own_ref[b ^ flip, :, cols] = whole[rows, 0:width].astype(BF)
-            sib_ref[b ^ flip, :, cols] = whole[rows, width:width2].astype(BF)
+        whole_ref[...] = whole
+        cols = slice(part * width, (part + 1) * width)
+        for r in range(CHUNKS):
+            at = pl.multiple_of((r ^ flip) * base, 32)
+            block = whole_ref[pl.ds(at, base), :].astype(BF)
+            own_ref[r, :, cols] = block[:, 0:width]
+            (sib_a_ref, sib_b_ref)[r // 4][r % 4, :, cols] = block[:, width:width2]
     sum_ref[...] = jnp.zeros_like(sum_ref)
 
     def run(at):
@@ -561,16 +578,19 @@
     )[0]
 
 
-def scatter_first_kernel(info, own_ref, got_ref, *refs):
+def scatter_first_kernel(pieces, info, own_ref, *refs):
+    got_refs, refs = refs[:pieces], refs[pieces:]
     tiles, (keep_a, send_a, keep_b, send_b) = refs[:-4], refs[-4:]
     base = own_ref.shape[1]
     half = own_ref.shape[2] // 2
-    for keep, send, bit, at in ((keep_a, send_a, 0, 0), (keep_b, send_b, 1, half)):
-        cols = slice(at, at + half)
+    for side, keep, send in ((0, keep_a, send_a), (1, keep_b, send_b)):
+        cols = slice(side * half, (side + 1) * half)
+        got_cols = cols if pieces == 2 else slice(0, half)
         kept, sent = 0, 0
         for r in range(CHUNKS):
-            value = own_ref[r, :, cols].astype(F32) + got_ref[r, :, cols].astype(F32)
-            if (r >> bit) & 1:
+            got = got_refs[r // 4 if pieces == 2 else 2 * side + r // 4]
+            value = own_ref[r, :, cols].astype(F32) + got[r % 4, :, got_cols].astype(F32)
+            if (r >> side) & 1:
                 send[sent * base : (sent + 1) * base, :] = value.astype(BF)
                 sent += 1
             else:
@@ -578,7 +598,6 @@
                 kept += 1
         if tiles:
             value = tiles[0][:, cols].astype(F32) + tiles[1][:, cols].astype(F32)
-            value = value + tiles[2][:, cols].astype(F32)
             send[4 * base : 4 * base + EXTRA, :] = value.astype(BF)
             keep[4 * base : 4 * base + EXTRA, :] = value
 
@@ -626,70 +645,81 @@
             send[base : base + extra, cols] = value.astype(BF)
 
 
-def scatter_last_kernel(tiled, info, left, got, out):
+def scatter_big_kernel(info, left, got, fc_ref, proj_ref):
+    units = fc_ref.shape[1]
+    total = left[...] + got[...].astype(F32)
+    fc_ref[...] = total[:, :units]
+    proj_ref[...] = jnp.transpose(total[:, units:])
+
+
+def scatter_small_kernel(info, left, got, qkv_ref, attn_ref, tile_ref):
+    base = left.shape[0] - EXTRA
+    width = qkv_ref.shape[2]
+    total = left[0:base, :] + got[0:base, :].astype(F32)
+    for p in range(3):
+        qkv_ref[p] = total[:, p * width : (p + 1) * width]
+    attn_ref[...] = jnp.transpose(total[:, 3 * width :])
+    rows = slice(base, base + EXTRA)
+    tile_ref[...] = left[rows, :].astype(BF).astype(F32) + got[rows, :].astype(F32)
+
+
+def scatter_start(info, own, sib, tiles=(), after=()):
+    base, columns = own.shape[1:]
+    half = columns // 2
+    rows = 4 * base + (EXTRA if tiles else 0)
+    return call(
+        functools.partial(scatter_first_kernel, len(sib)),
+        [shape((rows, half), F32), shape((rows, half))] * 2,
+        info,
+        own,
+        *[swap_core(piece) for piece in sib],
+        *tiles,
+        name="scatter_first",
+        after=after,
+    )
+
+
+def scatter_send(state, bits):
+    keep_a, send_a, keep_b, send_b = state
+    return keep_a, swap_bit(send_a, bits[0]), keep_b, swap_bit(send_b, bits[1])
+
+
+def scatter_middle(info, state, tiled, after=()):
+    half = state[0].shape[1]
     extra = EXTRA if tiled else 0
-    base = left.shape[0] - extra
-    out[0:base, :] = left[0:base, :] + got[0:base, :].astype(F32)
-    if tiled:
-        rows = slice(base, base + extra)
-        out[rows, :] = left[rows, :].astype(BF).astype(F32) + got[rows, :].astype(F32)
-
-
-def scatter_blocks(info, own, sib, count, tiles=None):
-    got = swap_core(sib)
-    base, columns = own.shape[1:]
-    tiled = tiles is not None
-    extra = EXTRA if tiled else 0
-    if count != CHUNKS:
-        total = own.astype(F32) + got.astype(F32)
-        total = lax.psum_scatter(
-            total.reshape(CHUNKS * base, columns), "dp", scatter_dimension=0, tiled=True
-        )
-        if not tiled:
-            return total, None
-        return total, lax.psum(sum(t.astype(F32) for t in tiles), "dp")
-    half = columns // 2
-    rows = 4 * base + extra
-    keep_a, send_a, keep_b, send_b = call(
-        scatter_first_kernel,
-        [shape((rows, half), F32), shape((rows, half))] * 2,
-        info,
-        own,
-        got,
-        *(tiles or ()),
-        name="scatter_first",
-    )
-    rows = 2 * base + extra
-    keep_a, send_a, keep_b, send_b = call(
+    rows = (state[0].shape[0] - extra) // 2 + extra
+    return call(
         functools.partial(scatter_second_kernel, tiled),
         [shape((rows, half), F32), shape((rows, half))] * 2,
         info,
-        keep_a,
-        swap_bit(send_a, 0),
-        keep_b,
-        swap_bit(send_b, 1),
+        *state,
         name="scatter_second",
-    )
-    rows = base + extra
+        after=after,
+    )
+
+
+def scatter_late(info, state, tiled, after=()):
+    half = state[0].shape[1]
+    extra = EXTRA if tiled else 0
+    rows = (state[0].shape[0] - extra) // 2 + extra
     left, send = call(
         functools.partial(scatter_third_kernel, tiled),
-        [shape((rows, columns), F32), shape((rows, columns))],
-        info,
-        keep_a,
-        swap_bit(send_a, 1),
-        keep_b,
-        swap_bit(send_b, 0),
+        [shape((rows, 2 * half), F32), shape((rows, 2 * half))],
+        info,
+        *state,
         name="scatter_third",
-    )
-    out = call(
-        functools.partial(scatter_last_kernel, tiled),
-        [shape((rows, columns), F32)],
-        info,
-        left,
-        swap_bit(send, 2),
-        name="scatter_last",
-    )[0]
-    return out[:base], (out[base:] if tiled else None)
+        after=after,
+    )
+    return left, swap_bit(send, 2)
+
+
+def scatter_plain(own, sib):
+    if len(sib) == 4:
+        sib = [jnp.concatenate([sib[i], sib[i + 2]], 2) for i in range(2)]
+    sib = jnp.concatenate(sib, 0)
+    total = own.astype(F32) + swap_core(sib).astype(F32)
+    total = total.reshape(total.shape[0] * total.shape[1], total.shape[2])
+    return lax.psum_scatter(total, "dp", scatter_dimension=0, tiled=True)
 
 
 def body(
@@ -748,15 +778,15 @@
     )
     wide = jnp.concatenate([fc_weight, proj_weight.T], 1)
     if count == CHUNKS:
-        own_a = gather_blocks(jnp.concatenate([mats, tile], 0))
+        own_a = jnp.stack(gather_blocks(jnp.concatenate([mats, tile], 0)))
         wide = lax.optimization_barrier((wide, own_a))[0]
-        own_b = gather_blocks(wide)
     else:
         full = lax.all_gather(mats, "dp", axis=0, tiled=True).reshape(CHUNKS, base, depth)
         total = jnp.sum(lax.all_gather(tile, "dp", axis=0).astype(F32), 0).astype(BF)
         total = jnp.pad(total[None], ((0, CHUNKS - 1), (0, 0), (0, 0)))
         own_a = jnp.concatenate([full, total], 1)
         own_b = lax.all_gather(wide, "dp", axis=0, tiled=True).reshape(CHUNKS, base, 2 * units)
+        own_b = [own_b[r] for r in range(CHUNKS)]
     sib_a = swap_core(own_a)
     first_low, vec = call(
         norm_kernel,
@@ -766,6 +796,8 @@
         own_a,
         name="norm_first",
     )
+    if count == CHUNKS:
+        blocks = gather_blocks(wide, first_low)
     pairs = heads2 * TILE * (own_count // TILE) * (own_count // TILE + 1) * TILE
     weight = shape((depth, width2))
     part, mixed, q, k, v, probs, wq, wk, wv, wo, first_own = call(
@@ -797,10 +829,12 @@
         name="attend",
     )
     got = swap_chip(part)
-    sib_b = swap_core(own_b)
+    if count == CHUNKS:
+        own_b = lax.optimization_barrier((blocks, part))[0]
+    sib_b = [swap_core(block) for block in own_b]
     vec_sib = jnp.sum(sib_a[:, base:].astype(F32), 0)
     hid = shape((own_count, 2 * units))
-    da, act, dhid, second, dy, middle = call(
+    da, act, dhid, second, dy, middle, proj_full = call(
         mlp_kernel,
         [
             shape((own_count, depth)),
@@ -809,6 +843,7 @@
             shape((own_count, depth)),
             shape((own_count, depth)),
             shape((own_count, depth), F32),
+            shape((depth, 2 * units)),
         ],
         info,
         inputs,
@@ -818,10 +853,9 @@
         got,
         vec,
         vec_sib,
-        own_b,
-        sib_b,
+        *own_b,
+        *sib_b,
         scratch=[
-            pltpu.VMEM((depth, 2 * units), BF),
             pltpu.VMEM((depth, 2 * units), BF),
             pltpu.VMEM((own_count, 512), F32),
             pltpu.VMEM((own_count, 512), F32),
@@ -830,22 +864,12 @@
         name="mlp",
     )
     da_got = swap_chip(da)
-    mlp_part = call(
-        mlp_out_kernel,
-        [shape((own_count, depth))],
-        info,
-        act,
-        own_b,
-        sib_b,
-        scratch=[pltpu.VMEM((depth, 2 * units), BF)],
-        flops=4 * own_count * depth * units,
-        name="mlp_out",
-    )[0]
-    grad_own, grad_sib, mlp_sums = call(
+    mlp_part, grad_own, *grad_sib, mlp_sums = call(
         mlp_grad_kernel,
         [
+            shape((own_count, depth)),
             shape((CHUNKS, base, 2 * units)),
-            shape((CHUNKS, base, 2 * units)),
+            *[shape((CHUNKS // 2, base, units))] * 4,
             shape((24, depth), F32),
         ],
         info,
@@ -853,15 +877,22 @@
         dhid,
         second,
         dy,
+        proj_full,
         scratch=[pltpu.VMEM((depth, units), F32)],
-        flops=8 * own_count * depth * units,
+        flops=12 * own_count * depth * units,
         name="mlp_grad",
     )
-    big, _ = scatter_blocks(info, grad_own, grad_sib, count)
-    fc_weight_grad = big[:, :units]
-    proj_weight_grad = big[:, units:].T
-
-    dmid, branch, att_sums, dq, keep, send = call(
+    mlp_got = swap_chip(mlp_part)
+    exact = count == CHUNKS
+    if exact:
+        big_state = scatter_start(info, grad_own, grad_sib)
+        big_sent = big_state[1]
+        big_state = scatter_send(big_state, (0, 1))
+    else:
+        big = scatter_plain(grad_own, grad_sib)
+        fc_weight_grad, proj_weight_grad = big[:, :units], big[:, units:].T
+
+    dmid, branch, att_sums, dq, keep, *send = call(
         attend_back_kernel,
         [
             shape((own_count, depth), F32),
@@ -869,7 +900,7 @@
             shape((8, depth), F32),
             shape((own_count, width2)),
             shape((2 * width2, own_count), F32),
-            shape((2 * width2, own_count)),
+            *[shape((width2, own_count))] * 2,
         ],
         info,
         middle,
@@ -895,8 +926,9 @@
         ],
         flops=8 * pairs * HD,
         name="attend_back",
-    )
-    keep_got = swap_core(send)
+        after=(big_sent,) if exact else (),
+    )
+    keep_got = [swap_core(piece) for piece in send]
     attn_full = call(
         attn_grad_kernel,
         [shape((depth, width2), F32)],
@@ -905,6 +937,7 @@
         mixed,
         flops=2 * own_count * depth * width2,
         name="attn_grad",
+        after=(mlp_got, big_state[1], big_state[3]) if exact else (),
     )[0]
     first_part, dkv = call(
         first_grad_kernel,
@@ -912,17 +945,22 @@
         info,
         dq,
         keep,
-        keep_got,
+        *keep_got,
         wq,
         wk,
         wv,
         flops=6 * own_count * depth * width2,
         name="first_grad",
+        after=(attn_full,),
     )
     first_got = swap_chip(first_part)
-    qkv_own, qkv_sib, tile_own, tile_sib = call(
+    qkv_own, *qkv_sib, tile_own, tile_sib = call(
         qkv_grad_kernel,
-        [shape((CHUNKS, base, 4 * width))] * 2 + [shape((EXTRA, depth))] * 2,
+        [
+            shape((CHUNKS, base, 4 * width)),
+            *[shape((CHUNKS // 2, base, 4 * width))] * 2,
+            *[shape((EXTRA, depth))] * 2,
+        ],
         info,
         first_own,
         dq,
@@ -932,15 +970,48 @@
         inputs,
         mlp_sums,
         att_sums,
-        scratch=[pltpu.VMEM((EXTRA, depth), F32)],
+        scratch=[pltpu.VMEM((depth, width2), F32), pltpu.VMEM((EXTRA, depth), F32)],
         flops=6 * own_count * depth * width2,
         name="qkv_grad",
     )
+    tiles = (tile_own, swap_core(tile_sib))
+    if exact:
+        big_state = scatter_middle(info, big_state, False, after=(qkv_own,))
+        small_state = scatter_start(info, qkv_own, qkv_sib, tiles, after=(big_state[0],))
+        small_sent = small_state[1]
+        big_state = scatter_send(big_state, (1, 0))
+        small_state = scatter_send(small_state, (0, 1))
+        big_last = scatter_late(info, big_state, False)
+        small_state = scatter_middle(info, small_state, True, after=(big_last[0],))
+        small_state = scatter_send(small_state, (1, 0))
+        fc_weight_grad, proj_weight_grad = call(
+            scatter_big_kernel,
+            [shape((local, units), F32), shape((units, local), F32)],
+            info,
+            *big_last,
+            name="scatter_big",
+        )
+        small_last = scatter_late(info, small_state, True)
+        qkv_weight_grad, attn_weight_grad, tile = call(
+            scatter_small_kernel,
+            [
+                shape((3, local, width), F32),
+                shape((width, local), F32),
+                shape((EXTRA, depth), F32),
+            ],
+            info,
+            *small_last,
+            name="scatter_small",
+            after=(fc_weight_grad,),
+        )
+    else:
+        mine = scatter_plain(qkv_own, qkv_sib)
+        qkv_weight_grad = mine[:, : 3 * width].reshape(local, 3, width).transpose(1, 0, 2)
+        attn_weight_grad = mine[:, 3 * width :].T
+        tile = lax.psum(tiles[0].astype(F32) + tiles[1].astype(F32), "dp")
+    tile_got = swap_chip(tile.astype(BF)).astype(F32)
     mask = (jnp.arange(EXTRA) < 2)[:, None]
-    tile_got = swap_core(tile_sib)
-    part_sum = jnp.where(mask, tile_own.astype(F32) + tile_got.astype(F32), 0.0).astype(BF)
-    other = swap_chip(part_sum)
-    mine, tile = scatter_blocks(info, qkv_own, qkv_sib, count, (tile_own, tile_got, other))
+    tile = jnp.where(mask, tile.astype(BF).astype(F32) + tile_got, tile)
     inputs_low = call(
         final_kernel,
         [shape((own_count, depth))],
@@ -951,6 +1022,7 @@
         dmid,
         vec,
         name="final",
+        after=(small_sent,) if exact else (),
     )[0]
     inputs_grad = all_rows(info, inputs_low)
     out_low = call(
@@ -960,14 +1032,12 @@
         seg_row,
         middle,
         mlp_part,
-        swap_chip(mlp_part),
+        mlp_got,
         vec,
         name="output",
     )[0]
     outputs = all_rows(info, out_low)
 
-    qkv_weight_grad = mine[:, : 3 * width].reshape(local, 3, width).transpose(1, 0, 2)
-    attn_weight_grad = mine[:, 3 * width :].T
     parts = lax.dynamic_slice(tile, (0, index * local), (7, local))
     bias_sum = tile[7, :width2].reshape(2, heads, HD).transpose(1, 0, 2).reshape(heads, 2 * HD)
     qv_bias_grad = lax.dynamic_slice(bias_sum, (0, index * bias_width), (heads, bias_width))

time: 320 us -> 259 us (0.81)
  waiting for transfers between devices: 108 us -> 68.8 us
  Pallas kernels: 137 us -> 119 us
  local copies, waits for them, and re-layouts: 30.7 us -> 18.5 us
  starting transfers between devices: 37.8 us -> 46.9 us
    ppermute x5, waiting for transfers between devices: 59 us -> 19.7 us  [swap_chip(): return lax.ppermute(value, 'mp', CHIP_PAIRS)]
    pallas_call x21 -> x20, Pallas kernels: 137 us -> 119 us  [call(): pl.pallas_call(run, out_shape=outs, in_specs=specs, out_specs=[pl.BlockSp...]
    ppermute x24, starting transfers between devices: 29.5 us -> 36.1 us  [swap_mask(): return lax.ppermute(value, 'dp', [(i, i ^ mask) for i in range(CHUNKS)])]
    unnamed x68 -> x108, local copies, waits for them, and re-layouts: 19.9 us -> 13.8 us
  transfers between devices with their start and end apart: 37 -> 49, of which waited for: 12 -> 16; matrix products, arithmetic and copies ran while one was open for 4% -> 2% of each run, Pallas kernels for 37% -> 31%
where the time goes in v1:
time: 259 us; the launch traced here: 258 us
  Pallas kernels  119 us (46%)
  waiting for transfers between devices  68.8 us (27%)
  starting transfers between devices  46.9 us (18%)
  local copies, waits for them, and re-layouts  18.5 us (7%)
  other arithmetic  3.19 us (1%)
    pallas_call x20, Pallas kernels, call(): pl.pallas_call(run, out_shape=outs, in_specs=specs, out_specs=[pl.BlockSp...  119 us
    ppermute x24, waiting for transfers between devices, swap_mask(): return lax.ppermute(value, 'dp', [(i, i ^ mask) for i in range(CHUNKS)])  45.9 us
    ppermute x24, starting transfers between devices, swap_mask(): return lax.ppermute(value, 'dp', [(i, i ^ mask) for i in range(CHUNKS)])  36.1 us
    ppermute x5, waiting for transfers between devices, swap_chip(): return lax.ppermute(value, 'mp', CHIP_PAIRS)  19.7 us
    unnamed x108, local copies, waits for them, and re-layouts  13.8 us
    ppermute x5, starting transfers between devices, swap_chip(): return lax.ppermute(value, 'mp', CHIP_PAIRS)  6.66 us
  transfers between devices with their start and end apart: 49, of which 16 were waited for; matrix products, arithmetic and copies ran while one was open for 2% of the time, Pallas kernels for 31%

profile of v1, /device:TPU:0, one launch (start us, length us, event | category | flops | bytes accessed | tf_op | source)
XLA Modules:
  0.0 257.9 jit_solution(4815806853902774152)
XLA Ops:
  4.8 4.2 %collective-permute-start.3 = (bf16[112,768]{1,0:T(8,128)(2,1)S(1)}, bf16[112,768]{1,0:T(8,128)(2,1)S(1)}, u32[]{:S(2)}, u32[]{:S(2)}) collective-permute-start(bf16[112,768]{1,0:T(8,128)(2,1)S(1)} %get-tuple-element.211), channel_id=1, source_target_pairs={{0,16},{4,20},{8,24},{12,28},{16,0},{20,4},{24,8},{28,12},{1,17},{... | collective-permute-start | bytes 516104 | tf_op jit(solution)/shard_map/ppermute | solution.py:38
  12.2 5.0 %collective-permute-done.3 = bf16[112,768]{1,0:T(8,128)(2,1)S(1)} collective-permute-done((bf16[112,768]{1,0:T(8,128)(2,1)S(1)}, bf16[112,768]{1,0:T(8,128)(2,1)S(1)}, u32[]{:S(2)}, u32[]{:S(2)}) %collective-permute-start.3) | collective-permute-done | bytes 172064 | tf_op jit(solution)/shard_map/ppermute | solution.py:38
  22.4 7.7 %collective-permute-done.2 = bf16[112,768]{1,0:T(8,128)(2,1)S(1)} collective-permute-done((bf16[112,768]{1,0:T(8,128)(2,1)S(1)}, bf16[112,768]{1,0:T(8,128)(2,1)S(1)}, u32[]{:S(2)}, u32[]{:S(2)}) %collective-permute-start.2) | collective-permute-done | bytes 172064 | tf_op jit(solution)/shard_map/ppermute | solution.py:38
  31.9 3.4 %collective-permute-start.11 = (bf16[96,1536]{1,0:T(8,128)(2,1)S(1)}, bf16[96,1536]{1,0:T(8,128)(2,1)}, u32[]{:S(2)}, u32[]{:S(2)}) collective-permute-start(bf16[96,1536]{1,0:T(8,128)(2,1)S(1)} %pad_maximum_fusion.refs_8_), channel_id=1, source_target_pairs={{0,16},{4,20},{8,24},{12,28},{16,0},{20,4},{24,8},{28,12},{1,17},{... | collective-permute-start | bytes 884744 | tf_op jit(solution)/shard_map/ppermute | solution.py:38
  37.4 4.9 %norm_first.1 = (bf16[1024,768]{1,0:T(8,128)(2,1)}, f32[16,768]{1,0:T(8,128)}) custom-call(s32[2]{0:T(128)} %pad_add_fusion.refs_0_, bf16[1024,768]{1,0:T(8,128)(2,1)} %refs_1_.5, bf16[8,112,768]{2,1,0:T(8,128)(2,1)} %copy-done), custom_call_target="tpu_custom_call" | custom-call | bytes 1024 | tf_op jit(solution)/shard_map/norm_first/pallas_call | solution.py:56
  42.3 3.6 %collective-permute-done.10.refs_10_ = bf16[96,1536]{1,0:T(8,128)(2,1)S(1)} collective-permute-done((bf16[96,1536]{1,0:T(8,128)(2,1)S(1)}, bf16[96,1536]{1,0:T(8,128)(2,1)S(1)}, u32[]{:S(2)}, u32[]{:S(2)}) %collective-permute-start.10) | collective-permute-done | bytes 294944 | tf_op jit(solution)/shard_map/ppermute | solution.py:38
  45.9 3.2 %collective-permute-done.11.refs_12_ = bf16[96,1536]{1,0:T(8,128)(2,1)} collective-permute-done((bf16[96,1536]{1,0:T(8,128)(2,1)S(1)}, bf16[96,1536]{1,0:T(8,128)(2,1)}, u32[]{:S(2)}, u32[]{:S(2)}) %collective-permute-start.11) | collective-permute-done | bytes 294944 | tf_op jit(solution)/shard_map/ppermute | solution.py:38
  51.4 2.7 %collective-permute-start.15 = (bf16[96,1536]{1,0:T(8,128)(2,1)}, bf16[96,1536]{1,0:T(8,128)(2,1)S(1)}, u32[]{:S(2)}, u32[]{:S(2)}) collective-permute-start(bf16[96,1536]{1,0:T(8,128)(2,1)} %collective-permute-done.11.refs_12_), channel_id=1, source_target_pairs={{0,12},{4,8},{8,4},{12,0},{16,28},{20,24},{24,20},{28,16},{1,13},{... | collective-permute-start | bytes 884744 | tf_op jit(solution)/shard_map/ppermute | solution.py:38
  54.1 22.5 %attend.1 = (bf16[512,768]{1,0:T(8,128)(2,1)}, bf16[512,384]{1,0:T(8,128)(2,1)}, bf16[6,512,64]{2,1,0:T(8,128)(2,1)}, bf16[6,1024,64]{2,1,0:T(8,128)(2,1)}, bf16...) custom-call(s32[2]{0:T(128)} %pad_add_fusion.refs_0_, ...), custom_call_target="tpu_custom_call" | custom-call | bytes 1024 | tf_op jit(solution)/shard_map/attend/pallas_call | solution.py:56
  83.0 10.7 %collective-permute-done.8.refs_5_ = bf16[512,768]{1,0:T(8,128)(2,1)S(1)} collective-permute-done((bf16[512,768]{1,0:T(8,128)(2,1)}, bf16[512,768]{1,0:T(8,128)(2,1)S(1)}, u32[]{:S(2)}, u32[]{:S(2)}) %collective-permute-start.8) | collective-permute-done | bytes 786464 | tf_op jit(solution)/shard_map/ppermute | solution.py:34
  94.7 14.5 %mlp.1 = (bf16[512,768]{1,0:T(8,128)(2,1)}, bf16[512,1536]{1,0:T(8,128)(2,1)}, bf16[512,1536]{1,0:T(8,128)(2,1)}, bf16[512,768]{1,0:T(8,128)(2,1)}, bf16[512,768...) custom-call(s32[2]{0:T(128)} %pad_add_fusion.refs_0_, bf16[1024,768]{1,0:T(8,128)(2,1)} %refs_1_.5, ...), custom_call_target="tpu_custom_call" | custom-call | bytes 1024 | tf_op jit(solution)/shard_map/mlp/pallas_call | solution.py:56
  109.2 9.7 %mlp_grad.1 = (bf16[512,768]{1,0:T(8,128)(2,1)}, bf16[8,96,1536]{2,1,0:T(8,128)(2,1)}, bf16[4,96,768]{2,1,0:T(8,128)(2,1)}, bf16[4,96,768]{2,1,0:T(8,128)(2,1)},...) custom-call(s32[2]{0:T(128)} %pad_add_fusion.refs_0_, ...), custom_call_target="tpu_custom_call" | custom-call | bytes 1024 | tf_op jit(solution)/shard_map/mlp_grad/pallas_call | solution.py:56
  124.5 4.2 %scatter_first.2 = (f32[384,768]{1,0:T(8,128)}, bf16[384,768]{1,0:T(8,128)(2,1)}, f32[384,768]{1,0:T(8,128)}, bf16[384,768]{1,0:T(8,128)(2,1)}) custom-call(s32[2]{0:T(128)} %pad_add_fusion.refs_0_, bf16[8,96,1536]{2,1,0:T(8,128)(2,1)} %get-tuple-element.119.refs_1_, bf16[4,96,768]{2,1,0:T(8,128)(2,1)} %copy-done.13, bf16[4,96,768]{2,1,0:T(8,128)(2,1)} %copy-done.14, ...), custom_call_target="tpu_custom_call" | custom-call | bytes 1024 | tf_op jit(solution)/shard_map/scatter_first/pallas_call | solution.py:56
  130.8 9.0 %collective-permute-done.26.refs_4_ = bf16[512,768]{1,0:T(8,128)(2,1)S(1)} collective-permute-done((bf16[512,768]{1,0:T(8,128)(2,1)S(1)}, bf16[512,768]{1,0:T(8,128)(2,1)S(1)}, u32[]{:S(2)}, u32[]{:S(2)}) %collective-permute-start.26) | collective-permute-done | bytes 786464 | tf_op jit(solution)/shard_map/ppermute | solution.py:34
  140.6 18.7 %attend_back.1 = (f32[512,768]{1,0:T(8,128)}, bf16[512,768]{1,0:T(8,128)(2,1)}, f32[8,768]{1,0:T(8,128)}, bf16[512,384]{1,0:T(8,128)(2,1)}, f32[768,512]{1,0:T(8...) custom-call(s32[2]{0:T(128)} %pad_add_fusion.refs_0_, f32[512,768]{1,0:T(8,128)} %get-tuple-element.105.refs_2_.refs_1_, ...), custom_call_target="tpu_custom_call" | custom-call | bytes 1024 | tf_op jit(solution)/shard_map/attend_back/pallas_call | solution.py:56
  161.2 2.9 %attn_grad.1.refs_8_.refs_4_ = f32[768,384]{1,0:T(8,128)} custom-call(s32[2]{0:T(128)} %pad_add_fusion.refs_0_, bf16[512,768]{1,0:T(8,128)(2,1)} %get-tuple-element.132.refs_1_, bf16[512,384]{1,0:T(8,128)(2,1)} %get-tuple-element.114.refs_7_.refs_2_, bf16[512,768]{1,0:T(8,128)(2,1)} %copy-done.1, bf16[384,768]{1,0:T(8,128)(2,1)} %copy-done.3, ...), custom_call_target="tpu_custom_call" | custom-call | bytes 1024 | tf_op jit(solution)/shard_map/attn_grad/pallas_call | solution.py:56
  164.9 4.6 %first_grad.1 = (bf16[512,768]{1,0:T(8,128)(2,1)}, bf16[768,512]{1,0:T(8,128)(2,1)}) custom-call(s32[2]{0:T(128)} %pad_add_fusion.refs_0_, bf16[512,384]{1,0:T(8,128)(2,1)} %get-tuple-element.125.refs_1_.refs_2_, f32[768,512]{1,0:T(8,128)} %get-tuple-element.126.refs_2_, bf16[384,512]{1,0:T(8,128)(2,1)} %copy-done.19, bf16[384,512]{1,0:T(8,128)(2,1)} %copy-done.20, ...), custom_call_target="tpu_custom_call" | custom-call | bytes 1024 | tf_op jit(solution)/shard_map/first_grad/pallas_call | solution.py:56
  169.5 6.8 %qkv_grad.1 = (bf16[8,96,768]{2,1,0:T(8,128)(2,1)}, bf16[4,96,768]{2,1,0:T(8,128)(2,1)}, bf16[4,96,768]{2,1,0:T(8,128)(2,1)}, bf16[16,768]{1,0:T(8,128)(2,1)}, bf16[16,768]{1,0:T(8,128)(2,1)}) custom-call(s32[2]{0:T(128)} %pad_add_fusion.refs_0_, bf16[512,768]{1,0:T(8,128)(2,1)} %get-tuple-element.136.refs_1_, ...), custom_call_target="tpu_custom_call" | custom-call | bytes 1024 | tf_op jit(solution)/shard_map/qkv_grad/pallas_call | solution.py:56
  176.8 3.2 %scatter_second.2 = (f32[192,768]{1,0:T(8,128)}, bf16[192,768]{1,0:T(8,128)(2,1)}, f32[192,768]{1,0:T(8,128)}, bf16[192,768]{1,0:T(8,128)(2,1)}) custom-call(s32[2]{0:T(128)} %pad_add_fusion.refs_0_, f32[384,768]{1,0:T(8,128)} %get-tuple-element.145.refs_1_, bf16[384,768]{1,0:T(8,128)(2,1)} %copy-done.3, f32[384,768]{1,0:T(8,128)} %get-tuple-element.146.refs_3_, ...), custom_call_target="tpu_custom_call" | custom-call | bytes 1024 | tf_op jit(solution)/shard_map/scatter_second/pallas_call | solution.py:56
  181.7 3.7 %output.1.refs_1_ = bf16[512,768]{1,0:T(8,128)(2,1)} custom-call(s32[2]{0:T(128)} %pad_add_fusion.refs_0_, s32[1,1024]{1,0:T(1,128)} %bitcast.49, f32[512,768]{1,0:T(8,128)} %get-tuple-element.105.refs_2_.refs_1_, bf16[512,768]{1,0:T(8,128)(2,1)} %get-tuple-element.111.refs_3_, bf16[512,768]{1,0:T(8,128)(2,1)} %copy-done.1, ...), custom_call_target="tpu_custom_call" | custom-call | bytes 1024 | tf_op jit(solution)/shard_map/output/pallas_call | solution.py:56
  188.4 3.0 %scatter_first.3 = (f32[400,384]{1,0:T(8,128)}, bf16[400,384]{1,0:T(8,128)(2,1)}, f32[400,384]{1,0:T(8,128)}, bf16[400,384]{1,0:T(8,128)(2,1)}) custom-call(s32[2]{0:T(128)} %pad_add_fusion.refs_0_, bf16[8,96,768]{2,1,0:T(8,128)(2,1)} %get-tuple-element.140.refs_5_.refs_1_, bf16[4,96,768]{2,1,0:T(8,128)(2,1)} %copy-done.17, bf16[4,96,768]{2,1,0:T(8,128)(2,1)} %copy-done.18, ...), custom_call_target="tpu_custom_call" | custom-call | bytes 1024 | tf_op jit(solution)/shard_map/scatter_first/pallas_call | solution.py:56
  193.9 13.1 %collective-permute-done.43.refs_4_ = bf16[192,768]{1,0:T(8,128)(2,1)S(1)} collective-permute-done((bf16[192,768]{1,0:T(8,128)(2,1)S(1)}, bf16[192,768]{1,0:T(8,128)(2,1)S(1)}, u32[]{:S(2)}, u32[]{:S(2)}) %collective-permute-start.43) | collective-permute-done | bytes 294944 | tf_op jit(solution)/shard_map/ppermute | solution.py:38
  207.7 2.4 scatter_third.2
  210.9 2.4 scatter_second.3
  215.2 2.5 collective-permute-start.47
  217.7 3.9 %collective-permute-done.44.refs_2_ = bf16[208,384]{1,0:T(8,128)(2,1)S(1)} collective-permute-done((bf16[208,384]{1,0:T(8,128)(2,1)}, bf16[208,384]{1,0:T(8,128)(2,1)S(1)}, u32[]{:S(2)}, u32[]{:S(2)}) %collective-permute-start.44) | collective-permute-done | bytes 159776 | tf_op jit(solution)/shard_map/ppermute | solution.py:38
  222.3 2.0 scatter_third.3
  225.8 9.5 %collective-permute-done.47.refs_2_ = bf16[96,1536]{1,0:T(8,128)(2,1)S(1)} collective-permute-done((bf16[96,1536]{1,0:T(8,128)(2,1)S(1)}, bf16[96,1536]{1,0:T(8,128)(2,1)S(1)}, u32[]{:S(2)}, u32[]{:S(2)}) %collective-permute-start.47) | collective-permute-done | bytes 294944 | tf_op jit(solution)/shard_map/ppermute | solution.py:38
  236.0 2.1 scatter_big.1
  242.9 2.6 %merge.2 = bf16[1024,768]{1,0:T(8,128)(2,1)} custom-call(s32[2]{0:T(128)} %pad_add_fusion.refs_0_, bf16[512,768]{1,0:T(8,128)(2,1)} %output.1.refs_1_, bf16[512,768]{1,0:T(8,128)(2,1)} %copy-done.9), custom_call_target="tpu_custom_call" | custom-call | bytes 1024 | tf_op jit(solution)/shard_map/merge/pallas_call | solution.py:56
  247.3 4.6 %final.1.refs_1_ = bf16[512,768]{1,0:T(8,128)(2,1)} custom-call(s32[2]{0:T(128)} %pad_add_fusion.refs_0_, bf16[1024,768]{1,0:T(8,128)(2,1)} %refs_1_.5, bf16[512,768]{1,0:T(8,128)(2,1)} %get-tuple-element.134.refs_5_.refs_2_, bf16[512,768]{1,0:T(8,128)(2,1)} %copy-done.8, f32[512,768]{1,0:T(8,128)} %get-tuple-element.135.refs_4_, ...), custom_call_target="tpu_custom_call" | custom-call | bytes 1024 | tf_op jit(solution)/shard_map/final/pallas_call | solution.py:56
  255.3 2.6 %merge.3 = bf16[1024,768]{1,0:T(8,128)(2,1)} custom-call(s32[2]{0:T(128)} %pad_add_fusion.refs_0_, bf16[512,768]{1,0:T(8,128)(2,1)} %final.1.refs_1_, bf16[512,768]{1,0:T(8,128)(2,1)} %copy-done.10), custom_call_target="tpu_custom_call" | custom-call | bytes 1024 | tf_op jit(solution)/shard_map/merge/pallas_call | solution.py:56
  (219 shorter events, 60.9 us)
Async XLA Ops:
  4.8 12.4 %collective-permute-start.3 = (bf16[112,768]{1,0:T(8,128)(2,1)S(1)}, bf16[112,768]{1,0:T(8,128)(2,1)S(1)}, u32[]{:S(2)}, u32[]{:S(2)}) collective-permute-start(bf16[112,768]{1,0:T(8,128)(2,1)S(1)} %get-tuple-element.211), channel_id=1, source_target_pairs={{0,16},{4,20},{8,24},{12,28},{16,0},{20,4},{24,8},{28,12},{1,17},{... | collective-permute-start | bytes 516104 | tf_op jit(solution)/shard_map/ppermute | solution.py:38
  9.0 11.7 %collective-permute-start.1 = (bf16[112,768]{1,0:T(8,128)(2,1)S(1)}, bf16[112,768]{1,0:T(8,128)(2,1)S(1)}, u32[]{:S(2)}, u32[]{:S(2)}) collective-permute-start(bf16[112,768]{1,0:T(8,128)(2,1)S(1)} %get-tuple-element.211), channel_id=1, source_target_pairs={{0,8},{4,12},{8,0},{12,4},{16,24},{20,28},{24,16},{28,20},{1,9},{5... | collective-permute-start | bytes 516104 | tf_op jit(solution)/shard_map/ppermute | solution.py:38
  10.7 11.6 %collective-permute-start = (bf16[112,768]{1,0:T(8,128)(2,1)S(1)}, bf16[112,768]{1,0:T(8,128)(2,1)S(1)}, u32[]{:S(2)}, u32[]{:S(2)}) collective-permute-start(bf16[112,768]{1,0:T(8,128)(2,1)S(1)} %get-tuple-element.211), channel_id=1, source_target_pairs={{0,4},{4,0},{8,12},{12,8},{16,20},{20,16},{24,28},{28,24},{1,5},{5... | collective-permute-start | bytes 516104 | tf_op jit(solution)/shard_map/ppermute | solution.py:38
  17.2 12.9 %collective-permute-start.4 = (bf16[112,768]{1,0:T(8,128)(2,1)S(1)}, bf16[112,768]{1,0:T(8,128)(2,1)S(1)}, u32[]{:S(2)}, u32[]{:S(2)}) collective-permute-start(bf16[112,768]{1,0:T(8,128)(2,1)S(1)} %collective-permute-done.3), channel_id=1, source_target_pairs={{0,4},{4,0},{8,12},{12,8},{16,20},{20,16},{24,28},{28,24},{1,5},{5... | collective-permute-start | bytes 516104 | tf_op jit(solution)/shard_map/ppermute | solution.py:38
  18.8 11.3 %collective-permute-start.5 = (bf16[112,768]{1,0:T(8,128)(2,1)S(1)}, bf16[112,768]{1,0:T(8,128)(2,1)S(1)}, u32[]{:S(2)}, u32[]{:S(2)}) collective-permute-start(bf16[112,768]{1,0:T(8,128)(2,1)S(1)} %collective-permute-done.3), channel_id=1, source_target_pairs={{0,8},{4,12},{8,0},{12,4},{16,24},{20,28},{24,16},{28,20},{1,9},{5... | collective-permute-start | bytes 516104 | tf_op jit(solution)/shard_map/ppermute | solution.py:38
  19.4 10.7 %collective-permute-start.6 = (bf16[112,768]{1,0:T(8,128)(2,1)S(1)}, bf16[112,768]{1,0:T(8,128)(2,1)S(1)}, u32[]{:S(2)}, u32[]{:S(2)}) collective-permute-start(bf16[112,768]{1,0:T(8,128)(2,1)S(1)} %collective-permute-done.3), channel_id=1, source_target_pairs={{0,12},{4,8},{8,4},{12,0},{16,28},{20,24},{24,20},{28,16},{1,13},{... | collective-permute-start | bytes 516104 | tf_op jit(solution)/shard_map/ppermute | solution.py:38
  20.7 9.3 %collective-permute-start.2 = (bf16[112,768]{1,0:T(8,128)(2,1)S(1)}, bf16[112,768]{1,0:T(8,128)(2,1)S(1)}, u32[]{:S(2)}, u32[]{:S(2)}) collective-permute-start(bf16[112,768]{1,0:T(8,128)(2,1)S(1)} %collective-permute-done.1), channel_id=1, source_target_pairs={{0,4},{4,0},{8,12},{12,8},{16,20},{20,16},{24,28},{28,24},{1,5},{5... | collective-permute-start | bytes 516104 | tf_op jit(solution)/shard_map/ppermute | solution.py:38
  30.2 21.2 %collective-permute-start.7 = (bf16[8,112,768]{2,1,0:T(8,128)(2,1)S(1)}, bf16[8,112,768]{2,1,0:T(8,128)(2,1)S(1)}, u32[]{:S(2)}, u32[]{:S(2)}) collective-permute-start(bf16[8,112,768]{2,1,0:T(8,128)(2,1)S(1)} %bitcast_dynamic-update-slice_fusion.refs_2_), channel_id=1, source_target_pairs={{0,1},{1,0},{2,3},{3,2},{4,5},{5,4},{6,7},{7,6},{8,9},{9,8},{10,11... | collective-permute-start | bytes 4128776 | tf_op jit(solution)/shard_map/ppermute | solution.py:30
  30.3 15.6 %collective-permute-start.10 = (bf16[96,1536]{1,0:T(8,128)(2,1)S(1)}, bf16[96,1536]{1,0:T(8,128)(2,1)S(1)}, u32[]{:S(2)}, u32[]{:S(2)}) collective-permute-start(bf16[96,1536]{1,0:T(8,128)(2,1)S(1)} %pad_maximum_fusion.refs_8_), channel_id=1, source_target_pairs={{0,8},{4,12},{8,0},{12,4},{16,24},{20,28},{24,16},{28,20},{1,9},{5... | collective-permute-start | bytes 884744 | tf_op jit(solution)/shard_map/ppermute | solution.py:38
  31.9 17.2 %collective-permute-start.11 = (bf16[96,1536]{1,0:T(8,128)(2,1)S(1)}, bf16[96,1536]{1,0:T(8,128)(2,1)}, u32[]{:S(2)}, u32[]{:S(2)}) collective-permute-start(bf16[96,1536]{1,0:T(8,128)(2,1)S(1)} %pad_maximum_fusion.refs_8_), channel_id=1, source_target_pairs={{0,16},{4,20},{8,24},{12,28},{16,0},{20,4},{24,8},{28,12},{1,17},{... | collective-permute-start | bytes 884744 | tf_op jit(solution)/shard_map/ppermute | solution.py:38
  35.2 41.4 %collective-permute-start.9 = (bf16[96,1536]{1,0:T(8,128)(2,1)S(1)}, bf16[96,1536]{1,0:T(8,128)(2,1)}, u32[]{:S(2)}, u32[]{:S(2)}) collective-permute-start(bf16[96,1536]{1,0:T(8,128)(2,1)S(1)} %pad_maximum_fusion.refs_8_), channel_id=1, source_target_pairs={{0,4},{4,0},{8,12},{12,8},{16,20},{20,16},{24,28},{28,24},{1,5},{5... | collective-permute-start | bytes 884744 | tf_op jit(solution)/shard_map/ppermute | solution.py:38
  49.1 29.2 %collective-permute-start.12 = (bf16[96,1536]{1,0:T(8,128)(2,1)S(1)}, bf16[96,1536]{1,0:T(8,128)(2,1)S(1)}, u32[]{:S(2)}, u32[]{:S(2)}) collective-permute-start(bf16[96,1536]{1,0:T(8,128)(2,1)S(1)} %collective-permute-done.10.refs_10_), channel_id=1, source_target_pairs={{0,4},{4,0},{8,12},{12,8},{16,20},{20,16},{24,28},{28,24},{1,5},{5... | collective-permute-start | bytes 884744 | tf_op jit(solution)/shard_map/ppermute | solution.py:38
  50.6 27.6 %collective-permute-start.13 = (bf16[96,1536]{1,0:T(8,128)(2,1)}, bf16[96,1536]{1,0:T(8,128)(2,1)S(1)}, u32[]{:S(2)}, u32[]{:S(2)}) collective-permute-start(bf16[96,1536]{1,0:T(8,128)(2,1)} %collective-permute-done.11.refs_12_), channel_id=1, source_target_pairs={{0,4},{4,0},{8,12},{12,8},{16,20},{20,16},{24,28},{28,24},{1,5},{5... | collective-permute-start | bytes 884744 | tf_op jit(solution)/shard_map/ppermute | solution.py:38
  51.1 27.2 %collective-permute-start.14 = (bf16[96,1536]{1,0:T(8,128)(2,1)}, bf16[96,1536]{1,0:T(8,128)(2,1)S(1)}, u32[]{:S(2)}, u32[]{:S(2)}) collective-permute-start(bf16[96,1536]{1,0:T(8,128)(2,1)} %collective-permute-done.11.refs_12_), channel_id=1, source_target_pairs={{0,8},{4,12},{8,0},{12,4},{16,24},{20,28},{24,16},{28,20},{1,9},{5... | collective-permute-start | bytes 884744 | tf_op jit(solution)/shard_map/ppermute | solution.py:38
  51.4 26.9 %collective-permute-start.15 = (bf16[96,1536]{1,0:T(8,128)(2,1)}, bf16[96,1536]{1,0:T(8,128)(2,1)S(1)}, u32[]{:S(2)}, u32[]{:S(2)}) collective-permute-start(bf16[96,1536]{1,0:T(8,128)(2,1)} %collective-permute-done.11.refs_12_), channel_id=1, source_target_pairs={{0,12},{4,8},{8,4},{12,0},{16,28},{20,24},{24,20},{28,16},{1,13},{... | collective-permute-start | bytes 884744 | tf_op jit(solution)/shard_map/ppermute | solution.py:38
  76.7 17.1 %collective-permute-start.8 = (bf16[512,768]{1,0:T(8,128)(2,1)}, bf16[512,768]{1,0:T(8,128)(2,1)S(1)}, u32[]{:S(2)}, u32[]{:S(2)}) collective-permute-start(bf16[512,768]{1,0:T(8,128)(2,1)} %get-tuple-element.92.refs_4_), channel_id=1, source_target_pairs={{0,2},{2,0},{1,3},{3,1},{4,6},{6,4},{5,7},{7,5},{8,10},{10,8},{9,1... | collective-permute-start | bytes 2359304 | tf_op jit(solution)/shard_map/ppermute | solution.py:34
  119.4 20.3 %collective-permute-start.26 = (bf16[512,768]{1,0:T(8,128)(2,1)S(1)}, bf16[512,768]{1,0:T(8,128)(2,1)S(1)}, u32[]{:S(2)}, u32[]{:S(2)}) collective-permute-start(bf16[512,768]{1,0:T(8,128)(2,1)S(1)} %copy-done.11), channel_id=1, source_target_pairs={{0,2},{2,0},{1,3},{3,1},{4,6},{6,4},{5,7},{7,5},{8,10},{10,8},{9,1... | collective-permute-start | bytes 2359304 | tf_op jit(solution)/shard_map/ppermute | solution.py:34
  121.2 38.7 %collective-permute-start.24 = (bf16[512,768]{1,0:T(8,128)(2,1)}, bf16[512,768]{1,0:T(8,128)(2,1)S(1)}, u32[]{:S(2)}, u32[]{:S(2)}) collective-permute-start(bf16[512,768]{1,0:T(8,128)(2,1)} %get-tuple-element.111.refs_3_), channel_id=1, source_target_pairs={{0,2},{2,0},{1,3},{3,1},{4,6},{6,4},{5,7},{7,5},{8,10},{10,8},{9,1... | collective-permute-start | bytes 2359304 | tf_op jit(solution)/shard_map/ppermute | solution.py:34
  128.7 31.2 %collective-permute-start.33 = (bf16[384,768]{1,0:T(8,128)(2,1)}, bf16[384,768]{1,0:T(8,128)(2,1)S(1)}, u32[]{:S(2)}, u32[]{:S(2)}) collective-permute-start(bf16[384,768]{1,0:T(8,128)(2,1)} %get-tuple-element.124.refs_12_), channel_id=1, source_target_pairs={{0,4},{4,0},{8,12},{12,8},{16,20},{20,16},{24,28},{28,24},{1,5},{5... | collective-permute-start | bytes 1769480 | tf_op jit(solution)/shard_map/ppermute | solution.py:38
  130.3 29.6 %collective-permute-start.34 = (bf16[384,768]{1,0:T(8,128)(2,1)}, bf16[384,768]{1,0:T(8,128)(2,1)S(1)}, u32[]{:S(2)}, u32[]{:S(2)}) collective-permute-start(bf16[384,768]{1,0:T(8,128)(2,1)} %get-tuple-element.133), channel_id=1, source_target_pairs={{0,8},{4,12},{8,0},{12,4},{16,24},{20,28},{24,16},{28,20},{1,9},{5... | collective-permute-start | bytes 1769480 | tf_op jit(solution)/shard_map/ppermute | solution.py:38
  176.3 11.1 %collective-permute-start.36 = (bf16[4,96,768]{2,1,0:T(8,128)(2,1)}, bf16[4,96,768]{2,1,0:T(8,128)(2,1)S(1)}, u32[]{:S(2)}, u32[]{:S(2)}) collective-permute-start(bf16[4,96,768]{2,1,0:T(8,128)(2,1)} %get-tuple-element.141), channel_id=1, source_target_pairs={{0,1},{1,0},{2,3},{3,2},{4,5},{5,4},{6,7},{7,6},{8,9},{9,8},{10,11... | collective-permute-start | bytes 1769480 | tf_op jit(solution)/shard_map/ppermute | solution.py:30
  176.4 11.1 %collective-permute-start.37 = (bf16[4,96,768]{2,1,0:T(8,128)(2,1)}, bf16[4,96,768]{2,1,0:T(8,128)(2,1)S(1)}, u32[]{:S(2)}, u32[]{:S(2)}) collective-permute-start(bf16[4,96,768]{2,1,0:T(8,128)(2,1)} %get-tuple-element.142), channel_id=1, source_target_pairs={{0,1},{1,0},{2,3},{3,2},{4,5},{5,4},{6,7},{7,6},{8,9},{9,8},{10,11... | collective-permute-start | bytes 1769480 | tf_op jit(solution)/shard_map/ppermute | solution.py:30
  180.0 13.3 %collective-permute-start.42 = (bf16[192,768]{1,0:T(8,128)(2,1)}, bf16[192,768]{1,0:T(8,128)(2,1)S(1)}, u32[]{:S(2)}, u32[]{:S(2)}) collective-permute-start(bf16[192,768]{1,0:T(8,128)(2,1)} %get-tuple-element.152), channel_id=1, source_target_pairs={{0,8},{4,12},{8,0},{12,4},{16,24},{20,28},{24,16},{28,20},{1,9},{5... | collective-permute-start | bytes 884744 | tf_op jit(solution)/shard_map/ppermute | solution.py:38
  185.4 56.6 %collective-permute-start.25 = (bf16[512,768]{1,0:T(8,128)(2,1)}, bf16[512,768]{1,0:T(8,128)(2,1)S(1)}, u32[]{:S(2)}, u32[]{:S(2)}) collective-permute-start(bf16[512,768]{1,0:T(8,128)(2,1)} %output.1.refs_1_), channel_id=1, source_target_pairs={{0,1},{1,0},{2,3},{3,2},{4,5},{5,4},{6,7},{7,6},{8,9},{9,8},{10,11... | collective-permute-start | bytes 2359304 | tf_op jit(solution)/shard_map/ppermute | solution.py:30
  185.9 60.6 %collective-permute-start.35 = (bf16[512,768]{1,0:T(8,128)(2,1)S(1)}, bf16[512,768]{1,0:T(8,128)(2,1)S(1)}, u32[]{:S(2)}, u32[]{:S(2)}) collective-permute-start(bf16[512,768]{1,0:T(8,128)(2,1)S(1)} %copy-done.2), channel_id=1, source_target_pairs={{0,2},{2,0},{1,3},{3,1},{4,6},{6,4},{5,7},{7,5},{8,10},{10,8},{9,1... | collective-permute-start | bytes 2359304 | tf_op jit(solution)/shard_map/ppermute | solution.py:34
  191.4 18.6 %collective-permute-start.40 = (bf16[400,384]{1,0:T(8,128)(2,1)}, bf16[400,384]{1,0:T(8,128)(2,1)S(1)}, u32[]{:S(2)}, u32[]{:S(2)}) collective-permute-start(bf16[400,384]{1,0:T(8,128)(2,1)} %get-tuple-element.148.refs_6_), channel_id=1, source_target_pairs={{0,4},{4,0},{8,12},{12,8},{16,20},{20,16},{24,28},{28,24},{1,5},{5... | collective-permute-start | bytes 921608 | tf_op jit(solution)/shard_map/ppermute | solution.py:38
  191.9 18.2 %collective-permute-start.41 = (bf16[400,384]{1,0:T(8,128)(2,1)}, bf16[400,384]{1,0:T(8,128)(2,1)S(1)}, u32[]{:S(2)}, u32[]{:S(2)}) collective-permute-start(bf16[400,384]{1,0:T(8,128)(2,1)} %get-tuple-element.151), channel_id=1, source_target_pairs={{0,8},{4,12},{8,0},{12,4},{16,24},{20,28},{24,16},{28,20},{1,9},{5... | collective-permute-start | bytes 921608 | tf_op jit(solution)/shard_map/ppermute | solution.py:38
  193.4 13.6 %collective-permute-start.43 = (bf16[192,768]{1,0:T(8,128)(2,1)S(1)}, bf16[192,768]{1,0:T(8,128)(2,1)S(1)}, u32[]{:S(2)}, u32[]{:S(2)}) collective-permute-start(bf16[192,768]{1,0:T(8,128)(2,1)S(1)} %copy-done.47), channel_id=1, source_target_pairs={{0,4},{4,0},{8,12},{12,8},{16,20},{20,16},{24,28},{28,24},{1,5},{5... | collective-permute-start | bytes 884744 | tf_op jit(solution)/shard_map/ppermute | solution.py:38
  213.3 8.3 %collective-permute-start.44 = (bf16[208,384]{1,0:T(8,128)(2,1)}, bf16[208,384]{1,0:T(8,128)(2,1)S(1)}, u32[]{:S(2)}, u32[]{:S(2)}) collective-permute-start(bf16[208,384]{1,0:T(8,128)(2,1)} %get-tuple-element.157), channel_id=1, source_target_pairs={{0,8},{4,12},{8,0},{12,4},{16,24},{20,28},{24,16},{28,20},{1,9},{5... | collective-permute-start | bytes 479240 | tf_op jit(solution)/shard_map/ppermute | solution.py:38
  215.2 20.1 %collective-permute-start.47 = (bf16[96,1536]{1,0:T(8,128)(2,1)S(1)}, bf16[96,1536]{1,0:T(8,128)(2,1)S(1)}, u32[]{:S(2)}, u32[]{:S(2)}) collective-permute-start(bf16[96,1536]{1,0:T(8,128)(2,1)S(1)} %copy-done.48), channel_id=1, source_target_pairs={{0,16},{4,20},{8,24},{12,28},{16,0},{20,4},{24,8},{28,12},{1,17},{... | collective-permute-start | bytes 884744 | tf_op jit(solution)/shard_map/ppermute | solution.py:38
  224.3 13.8 %collective-permute-start.46 = (bf16[112,768]{1,0:T(8,128)(2,1)}, bf16[112,768]{1,0:T(8,128)(2,1)S(1)}, u32[]{:S(2)}, u32[]{:S(2)}) collective-permute-start(bf16[112,768]{1,0:T(8,128)(2,1)} %get-tuple-element.161), channel_id=1, source_target_pairs={{0,16},{4,20},{8,24},{12,28},{16,0},{20,4},{24,8},{28,12},{1,17},{... | collective-permute-start | bytes 516104 | tf_op jit(solution)/shard_map/ppermute | solution.py:38
  241.5 10.4 %collective-permute-start.48 = (bf16[16,768]{1,0:T(8,128)(2,1)S(1)}, bf16[16,768]{1,0:T(8,128)(2,1)S(1)}, u32[]{:S(2)}, u32[]{:S(2)}) collective-permute-start(bf16[16,768]{1,0:T(8,128)(2,1)S(1)} %convert_element_type.16), channel_id=1, source_target_pairs={{0,2},{2,0},{1,3},{3,1},{4,6},{6,4},{5,7},{7,5},{8,10},{10,8},{9,1... | collective-permute-start | bytes 73736 | tf_op jit(solution)/shard_map/ppermute | solution.py:34
  (67 other events, 442.8 us)

commit v2 on v1

--- a/solution.py
+++ b/solution.py
@@ -42,7 +42,7 @@
     return swap_mask(value, 1 << bit)
 
 
-def call(kernel, outs, *args, scratch=(), smem=1, flops=0, name=None, after=()):
+def call(kernel, outs, *args, scratch=(), smem=1, cost=0, name=None, after=()):
     first, behind = len(args), len(args) + len(after)
 
     def run(*refs):
@@ -51,8 +51,6 @@
     specs = [pl.BlockSpec(memory_space=pltpu.SMEM)] * smem
     specs += [pl.BlockSpec(memory_space=pltpu.VMEM)] * (len(args) - smem)
     specs += [pl.BlockSpec(memory_space=pl.ANY)] * len(after)
-    size = sum(a.size * a.dtype.itemsize for a in args)
-    size += sum(o.size * jnp.dtype(o.dtype).itemsize for o in outs)
     return pl.pallas_call(
         run,
         out_shape=outs,
@@ -60,7 +58,7 @@
         out_specs=[pl.BlockSpec(memory_space=pltpu.VMEM)] * len(outs),
         scratch_shapes=list(scratch),
         compiler_params=pltpu.CompilerParams(vmem_limit_bytes=56 * 1024 * 1024),
-        cost_estimate=pl.CostEstimate(flops=0, bytes_accessed=1024, transcendentals=0),
+        cost_estimate=pl.CostEstimate(flops=cost * 10**9, bytes_accessed=1024, transcendentals=0),
         name=name,
     )(*args, *after)
 
@@ -92,14 +90,6 @@
     lax.fori_loop(0, count // step, run, 0, unroll=unroll)
 
 
-def norm_stats(value):
-    average = jnp.mean(value, -1, keepdims=True)
-    centred = value - average
-    spread = jnp.mean(centred * centred, -1, keepdims=True)
-    factor = lax.rsqrt(spread + EPSILON)
-    return centred * factor, factor
-
-
 def norm_backward(incoming, scaled, factor, gain):
     weighted = incoming * gain
     first_mean = jnp.mean(weighted, -1, keepdims=True)
@@ -123,38 +113,42 @@
     return jnp.sum(value, 0, keepdims=True)
 
 
-def norm_kernel(info, x_ref, w_ref, low_ref, vec_ref):
-    base = w_ref.shape[1] - EXTRA
-    vec_ref[...] = tile_sum(w_ref, base)
-    gain, shift = vec_ref[0:1, :], vec_ref[1:2, :]
-
+def spread_stats(value):
+    average = jnp.mean(value, -1, keepdims=True)
+    centred = value - average
+    factor = lax.rsqrt(jnp.mean(centred * centred, -1, keepdims=True) + EPSILON)
+    rows = value.shape[0]
+    return jnp.concatenate(
+        [jnp.broadcast_to(average, (rows, TILE)), jnp.broadcast_to(factor, (rows, TILE))], 1
+    )
+
+
+def stats_kernel(info, x_ref, stat_ref):
     def run(at):
-        scaled, _ = norm_stats(x_ref[pl.ds(at, 32), :].astype(F32))
-        low_ref[pl.ds(at, 32), :] = (scaled * gain + shift).astype(BF)
+        rs = pl.ds(at, 32)
+        stat_ref[rs, :] = spread_stats(x_ref[rs, :].astype(F32))
 
     loop(x_ref.shape[0], 32, run)
 
 
-def attend_kernel(
+def project_kernel(
     info,
-    low_ref,
+    x_ref,
+    stat_ref,
     own_ref,
     sib_ref,
-    seg_ref,
-    part_ref,
-    mixed_ref,
     q_ref,
     k_ref,
     v_ref,
-    probs_ref,
     wq_ref,
     wk_ref,
     wv_ref,
     wo_ref,
     firstown_ref,
+    vec_ref,
+    vecsib_ref,
+    low_ref,
     proj_ref,
-    s_ref,
-    o_ref,
 ):
     flip, core = info[0], info[1]
     width = own_ref.shape[2] // 4
@@ -162,6 +156,16 @@
     rows = low_ref.shape[0]
     heads = 2 * width // HD
     own_count = rows // 2
+    vec_ref[...] = tile_sum(own_ref, base)
+    vecsib_ref[...] = tile_sum(sib_ref, base)
+    gain, shift = vec_ref[0:1, :], vec_ref[1:2, :]
+
+    def norm(at):
+        rs = pl.ds(at, 32)
+        scaled = (x_ref[rs, :].astype(F32) - stat_ref[rs, 0:1]) * stat_ref[rs, TILE : TILE + 1]
+        low_ref[rs, :] = (scaled * gain + shift).astype(BF)
+
+    loop(rows, 32, norm)
     for r in range(CHUNKS):
         at = pl.multiple_of((r ^ flip) * base, 32)
         for side, ref in ((0, own_ref), (1, sib_ref)):
@@ -169,11 +173,9 @@
                 out[pl.ds(at, base), side * width : (side + 1) * width] = ref[
                     r, 0:base, part * width : (part + 1) * width
                 ]
-    vec_own = tile_sum(own_ref, base)
-    vec_sib = tile_sum(sib_ref, base)
-    bias_q = jnp.concatenate([vec_own[7:8, :width], vec_sib[7:8, :width]], 1)
+    bias_q = jnp.concatenate([vec_ref[7:8, :width], vecsib_ref[7:8, :width]], 1)
     bias_v = jnp.concatenate(
-        [vec_own[7:8, width : 2 * width], vec_sib[7:8, width : 2 * width]], 1
+        [vec_ref[7:8, width : 2 * width], vecsib_ref[7:8, width : 2 * width]], 1
     )
     for j in range(own_count // TILE):
         at = own_start(j * TILE, core)
@@ -190,6 +192,13 @@
     proj_ref[...] = dot(low_ref[...], wv_ref[...], 1, 0) + bias_v
     for h in range(heads):
         v_ref[h] = proj_ref[:, h * HD : (h + 1) * HD].astype(BF)
+
+
+def attend_kernel(
+    info, q_ref, k_ref, v_ref, wo_ref, seg_ref, part_ref, mixed_ref, probs_ref, s_ref, o_ref
+):
+    core = info[1]
+    heads, own_count = q_ref.shape[:2]
     lane = lax.broadcasted_iota(jnp.int32, (TILE, TILE), 1)
     line = lax.broadcasted_iota(jnp.int32, (TILE, TILE), 0)
     for j in range(own_count // TILE):
@@ -206,10 +215,10 @@
 
         def run(h, carry, j=j, end=end, off=off):
             scores = dot(q_ref[h, j * TILE : (j + 1) * TILE, :], k_ref[h, 0:end, :], 1, 1)
-            s_ref[0, :, 0:end] = scores
+            s_ref[h, :, 0:end] = scores
             for sub in range(4):
                 sl = slice(sub * 32, sub * 32 + 32)
-                sc = s_ref[0, sl, 0:end] + s_ref[heads, sl, 0:end]
+                sc = s_ref[h, sl, 0:end] + s_ref[heads, sl, 0:end]
                 weights = jnp.exp(sc - jnp.max(sc, -1, keepdims=True))
                 inverse = 1.0 / jnp.sum(weights, -1, keepdims=True)
                 probs_ref[h, sl, off : off + end] = (weights * inverse).astype(BF)
@@ -218,73 +227,87 @@
             )
             return carry
 
-        lax.fori_loop(0, heads, run, 0)
+        lax.fori_loop(0, heads, run, 0, unroll=True)
     for h in range(heads):
         mixed_ref[:, h * HD : (h + 1) * HD] = o_ref[h].astype(BF)
     part_ref[...] = dot(mixed_ref[...], wo_ref[...], 1, 1).astype(BF)
 
 
-def mlp_kernel(
-    info,
-    x_ref,
-    seg_ref,
-    cot_ref,
-    part_ref,
-    recv_ref,
-    vec_ref,
-    vecsib_ref,
-    *refs,
-):
+def mlp_pre_kernel(info, seg_ref, cot_ref, *refs):
     own_refs, sib_refs = refs[:CHUNKS], refs[CHUNKS : 2 * CHUNKS]
-    da_ref, act_ref, dhid_ref, second_ref, dy_ref, mid_ref, proj_ref = refs[2 * CHUNKS : -3]
-    fc_ref, hid_ref, dact_ref = refs[-3:]
+    fc_ref, proj_ref, dy_ref, dact_ref = refs[2 * CHUNKS :]
     flip, core = info[0], info[1]
-    own_count = part_ref.shape[0]
+    own_count = dy_ref.shape[0]
     base = own_refs[0].shape[0]
     units = own_refs[0].shape[1] // 2
+    sub = 32
+    lane = lax.broadcasted_iota(jnp.int32, (sub, TILE), 1)
+    line = lax.broadcasted_iota(jnp.int32, (sub, TILE), 0)
+
+    def mask(at):
+        src = own_start(at, core)
+        tile_at = pl.multiple_of((2 * (at // TILE) + core) * TILE, TILE)
+        seg_tile = jnp.broadcast_to(seg_ref[0:1, pl.ds(tile_at, TILE)], (sub, TILE))
+        seg_col = jnp.max(
+            jnp.where(lane == line + at % TILE, seg_tile, -2), -1, keepdims=True
+        )
+        cot = cot_ref[pl.ds(src, sub), :].astype(F32)
+        dy_ref[pl.ds(at, sub), :] = jnp.where(seg_col >= 0, cot, 0.0).astype(BF)
+
+    loop(own_count, sub, mask)
     for r in range(CHUNKS):
         at = pl.multiple_of((r ^ flip) * base, 32)
         for side, ref in ((0, own_refs[r]), (1, sib_refs[r])):
             cols = slice(side * units, (side + 1) * units)
             fc_ref[pl.ds(at, base), cols] = ref[:, 0:units]
             proj_ref[pl.ds(at, base), cols] = ref[:, units : 2 * units]
+    for side in range(2):
+        cols = slice(side * units, (side + 1) * units)
+        dact_ref[:, cols] = dot(dy_ref[...], proj_ref[:, cols], 1, 0).astype(BF)
+
+
+def mlp_kernel(
+    info,
+    x_ref,
+    part_ref,
+    recv_ref,
+    vec_ref,
+    vecsib_ref,
+    fc_ref,
+    dact_ref,
+    da_ref,
+    act_ref,
+    dhid_ref,
+    second_ref,
+    mid_ref,
+    stat_ref,
+    hid_ref,
+):
+    core = info[1]
+    own_count = part_ref.shape[0]
+    units = fc_ref.shape[1] // 2
     gain, shift, bias = vec_ref[3:4, :], vec_ref[4:5, :], vec_ref[2:3, :]
     sub = 32
-    lane = lax.broadcasted_iota(jnp.int32, (sub, TILE), 1)
-    line = lax.broadcasted_iota(jnp.int32, (sub, TILE), 0)
 
     def first(at):
         src = own_start(at, core)
-        tile_at = pl.multiple_of((2 * (at // TILE) + core) * TILE, TILE)
-        seg_tile = jnp.broadcast_to(seg_ref[0:1, pl.ds(tile_at, TILE)], (sub, TILE))
-        seg_col = jnp.max(
-            jnp.where(lane == line + at % TILE, seg_tile, -2), -1, keepdims=True
-        )
         rows = pl.ds(at, sub)
-        cot = cot_ref[pl.ds(src, sub), :].astype(F32)
-        dy_ref[rows, :] = jnp.where(seg_col >= 0, cot, 0.0).astype(BF)
         middle = (
             x_ref[pl.ds(src, sub), :].astype(F32)
             + (part_ref[rows, :].astype(F32) + recv_ref[rows, :].astype(F32))
             + bias
         )
         mid_ref[rows, :] = middle
-        scaled, _ = norm_stats(middle)
+        stats = spread_stats(middle)
+        stat_ref[rows, :] = stats
+        scaled = (middle - stats[:, 0:1]) * stats[:, TILE : TILE + 1]
         second_ref[rows, :] = (scaled * gain + shift).astype(BF)
 
     loop(own_count, sub, first)
-    step = 512
-    for c in range(2 * units // step):
-        cols = slice(c * step, (c + 1) * step)
+    for side, biases in ((0, vec_ref), (1, vecsib_ref)):
+        cols = slice(side * units, (side + 1) * units)
         hid_ref[...] = dot(second_ref[...], fc_ref[:, cols], 1, 0)
-        dact_ref[...] = dot(dy_ref[...], proj_ref[:, cols], 1, 0)
-        left, right = c * step, (c + 1) * step
-        pieces = []
-        if left < units:
-            pieces.append(vec_ref[5:6, left : min(right, units)])
-        if right > units:
-            pieces.append(vecsib_ref[5:6, max(left, units) - units : right - units])
-        bias_fc = jnp.concatenate(pieces, 1) if len(pieces) > 1 else pieces[0]
+        bias_fc = biases[5:6, :]
 
         def gelu(at, cols=cols, bias_fc=bias_fc):
             rows = pl.ds(at, 16)
@@ -294,7 +317,7 @@
             half = 0.5 * (1.0 + bend)
             act_ref[rows, cols] = (u * half).astype(BF)
             slope = half + (0.5 * CURVE) * u * (1.0 - bend * bend) * (1.0 + 0.134145 * u2)
-            dhid_ref[rows, cols] = (dact_ref[rows, :] * slope).astype(BF)
+            dhid_ref[rows, cols] = (dact_ref[rows, cols].astype(F32) * slope).astype(BF)
 
         loop(own_count, 16, gelu)
     da_ref[...] = dot(dhid_ref[...], fc_ref[...], 1, 1).astype(BF)
@@ -341,6 +364,7 @@
 def attend_back_kernel(
     info,
     mid_ref,
+    stat_ref,
     dy_ref,
     da_ref,
     recv_ref,
@@ -377,7 +401,8 @@
 
     def first(at):
         rs = pl.ds(at, sub)
-        scaled, factor = norm_stats(mid_ref[rs, :])
+        factor = stat_ref[rs, TILE : TILE + 1]
+        scaled = (mid_ref[rs, :] - stat_ref[rs, 0:1]) * factor
         incoming = da_ref[rs, :].astype(F32) + recv_ref[rs, :].astype(F32)
         dmid = dy_ref[rs, :].astype(F32) + norm_backward(incoming, scaled, factor, gain)
         dmid_ref[rs, :] = dmid
@@ -405,13 +430,13 @@
             end = (j + 1) * 2 * TILE
             off = TILE * j * (j + 1)
             rs = slice(j * TILE, (j + 1) * TILE)
-            dp_ref[:, 0:end] = dot(do_ref[h, rs, :], v_ref[h, 0:end, :], 1, 1)
+            dp_ref[h, :, 0:end] = dot(do_ref[h, rs, :], v_ref[h, 0:end, :], 1, 1)
             for s in range(4):
                 sl = slice(s * 32, s * 32 + 32)
                 delta = delta_ref[h, j * TILE + s * 32 : j * TILE + s * 32 + 32, 0:1]
                 p = probs_ref[h, sl, off : off + end].astype(F32)
-                ds_ref[sl, 0:end] = (p * (dp_ref[sl, 0:end] - delta)).astype(BF)
-            ds = ds_ref[:, 0:end]
+                ds_ref[h, sl, 0:end] = (p * (dp_ref[h, sl, 0:end] - delta)).astype(BF)
+            ds = ds_ref[h, :, 0:end]
             dqh_ref[h, rs, :] = dot(ds, k_ref[h, 0:end, :], 1, 0) * scale
             dk = dot(q_ref[h, rs, :], ds, 0, 0)
             dv = dot(do_ref[h, rs, :], probs_ref[h, :, off : off + end], 0, 0)
@@ -423,7 +448,7 @@
                 dvt_ref[h, :, 0:end] += dv
         return carry
 
-    lax.fori_loop(0, heads, head, 0)
+    lax.fori_loop(0, heads, head, 0, unroll=2)
     width2 = heads * HD
     for h in range(heads):
         dq_ref[:, h * HD : (h + 1) * HD] = dqh_ref[h].astype(BF)
@@ -464,6 +489,7 @@
     attn_ref,
     part_ref,
     x_ref,
+    stat_ref,
     mlp_sums_ref,
     att_sums_ref,
     own_ref,
@@ -498,7 +524,8 @@
 
     def run(at):
         src = own_start(at, core)
-        scaled, _ = norm_stats(x_ref[pl.ds(src, 32), :].astype(F32))
+        rs = pl.ds(src, 32)
+        scaled = (x_ref[rs, :].astype(F32) - stat_ref[rs, 0:1]) * stat_ref[rs, TILE : TILE + 1]
         incoming = part_ref[pl.ds(at, 32), :].astype(F32)
         sum_ref[0:1, :] += colsum(incoming * scaled)
         sum_ref[1:2, :] += colsum(incoming)
@@ -517,14 +544,15 @@
         out[...] = sum_ref[...].astype(BF)
 
 
-def final_kernel(info, x_ref, part_ref, recv_ref, dmid_ref, vec_ref, out_ref):
+def final_kernel(info, x_ref, stat_ref, part_ref, recv_ref, dmid_ref, vec_ref, out_ref):
     core = info[1]
     gain = vec_ref[0:1, :]
 
     def run(at):
         src = own_start(at, core)
         rs = pl.ds(at, 32)
-        scaled, factor = norm_stats(x_ref[pl.ds(src, 32), :].astype(F32))
+        factor = stat_ref[pl.ds(src, 32), TILE : TILE + 1]
+        scaled = (x_ref[pl.ds(src, 32), :].astype(F32) - stat_ref[pl.ds(src, 32), 0:1]) * factor
         incoming = part_ref[rs, :].astype(F32) + recv_ref[rs, :].astype(F32)
         out_ref[rs, :] = (
             dmid_ref[rs, :] + norm_backward(incoming, scaled, factor, gain)
@@ -755,6 +783,10 @@
     info = jnp.stack([flip, core]).astype(jnp.int32)
     seg_row = segments.reshape(1, rows)
 
+    stat_one = call(
+        stats_kernel, [shape((rows, 2 * TILE), F32)], info, inputs, name="stats"
+    )[0]
+
     bias_width = qv_bias.shape[1]
     bias_rows = lax.dynamic_update_slice(
         jnp.zeros((heads, 2 * HD), BF), qv_bias, (0, index * bias_width)
@@ -778,7 +810,7 @@
     )
     wide = jnp.concatenate([fc_weight, proj_weight.T], 1)
     if count == CHUNKS:
-        own_a = jnp.stack(gather_blocks(jnp.concatenate([mats, tile], 0)))
+        own_a = jnp.stack(gather_blocks(jnp.concatenate([mats, tile], 0), stat_one))
         wide = lax.optimization_barrier((wide, own_a))[0]
     else:
         full = lax.all_gather(mats, "dp", axis=0, tiled=True).reshape(CHUNKS, base, depth)
@@ -788,79 +820,89 @@
         own_b = lax.all_gather(wide, "dp", axis=0, tiled=True).reshape(CHUNKS, base, 2 * units)
         own_b = [own_b[r] for r in range(CHUNKS)]
     sib_a = swap_core(own_a)
-    first_low, vec = call(
-        norm_kernel,
-        [shape((rows, depth)), shape((EXTRA, depth), F32)],
-        info,
-        inputs,
-        own_a,
-        name="norm_first",
-    )
-    if count == CHUNKS:
-        blocks = gather_blocks(wide, first_low)
-    pairs = heads2 * TILE * (own_count // TILE) * (own_count // TILE + 1) * TILE
     weight = shape((depth, width2))
-    part, mixed, q, k, v, probs, wq, wk, wv, wo, first_own = call(
-        attend_kernel,
+    q, k, v, wq, wk, wv, wo, first_own, vec, vec_sib = call(
+        project_kernel,
         [
-            shape((own_count, depth)),
-            shape((own_count, width2)),
             shape((heads2, own_count, HD)),
             shape((heads2, rows, HD)),
             shape((heads2, rows, HD)),
-            shape((heads2, TILE, TILE * (own_count // TILE) * (own_count // TILE + 1))),
             weight,
             weight,
             weight,
             weight,
             shape((own_count, depth)),
+            shape((EXTRA, depth), F32),
+            shape((EXTRA, depth), F32),
         ],
         info,
-        first_low,
+        inputs,
+        stat_one,
         own_a,
         sib_a,
+        scratch=[pltpu.VMEM((rows, depth), BF), pltpu.VMEM((rows, width2), F32)],
+        cost=8,
+        name="project",
+    )
+    if count == CHUNKS:
+        blocks = gather_blocks(wide, q)
+    tiles = own_count // TILE
+    part, mixed, probs = call(
+        attend_kernel,
+        [
+            shape((own_count, depth)),
+            shape((own_count, width2)),
+            shape((heads2, TILE, TILE * tiles * (tiles + 1))),
+        ],
+        info,
+        q,
+        k,
+        v,
+        wo,
         seg_row,
         scratch=[
-            pltpu.VMEM((rows, width2), F32),
             pltpu.VMEM((heads2 + 1, TILE, rows), F32),
             pltpu.VMEM((heads2, own_count, HD), F32),
         ],
-        flops=4 * pairs * HD + 5 * rows * depth * width2,
+        cost=16,
         name="attend",
     )
     got = swap_chip(part)
     if count == CHUNKS:
         own_b = lax.optimization_barrier((blocks, part))[0]
     sib_b = [swap_core(block) for block in own_b]
-    vec_sib = jnp.sum(sib_a[:, base:].astype(F32), 0)
     hid = shape((own_count, 2 * units))
-    da, act, dhid, second, dy, middle, proj_full = call(
+    full = shape((depth, 2 * units))
+    fc_full, proj_full, dy, dact = call(
+        mlp_pre_kernel,
+        [full, full, shape((own_count, depth)), hid],
+        info,
+        seg_row,
+        cotangent,
+        *own_b,
+        *sib_b,
+        name="mlp_pre",
+    )
+    da, act, dhid, second, middle, stat_two = call(
         mlp_kernel,
         [
             shape((own_count, depth)),
             hid,
             hid,
             shape((own_count, depth)),
-            shape((own_count, depth)),
             shape((own_count, depth), F32),
-            shape((depth, 2 * units)),
+            shape((own_count, 2 * TILE), F32),
         ],
         info,
         inputs,
-        seg_row,
-        cotangent,
         part,
         got,
         vec,
         vec_sib,
-        *own_b,
-        *sib_b,
-        scratch=[
-            pltpu.VMEM((depth, 2 * units), BF),
-            pltpu.VMEM((own_count, 512), F32),
-            pltpu.VMEM((own_count, 512), F32),
-        ],
-        flops=12 * own_count * depth * units,
+        fc_full,
+        dact,
+        scratch=[pltpu.VMEM((own_count, units), F32)],
+        cost=10,
         name="mlp",
     )
     da_got = swap_chip(da)
@@ -879,7 +921,7 @@
         dy,
         proj_full,
         scratch=[pltpu.VMEM((depth, units), F32)],
-        flops=12 * own_count * depth * units,
+        cost=9,
         name="mlp_grad",
     )
     mlp_got = swap_chip(mlp_part)
@@ -904,6 +946,7 @@
         ],
         info,
         middle,
+        stat_two,
         dy,
         da,
         da_got,
@@ -920,11 +963,11 @@
             pltpu.VMEM((heads2, HD, rows), F32),
             pltpu.VMEM((heads2, HD, rows), F32),
             pltpu.VMEM((heads2, own_count, HD), F32),
-            pltpu.VMEM((TILE, rows), F32),
-            pltpu.VMEM((TILE, rows), BF),
+            pltpu.VMEM((heads2, TILE, rows), F32),
+            pltpu.VMEM((heads2, TILE, rows), BF),
             pltpu.VMEM((heads2, own_count, TILE), F32),
         ],
-        flops=8 * pairs * HD,
+        cost=18,
         name="attend_back",
         after=(big_sent,) if exact else (),
     )
@@ -935,7 +978,6 @@
         info,
         branch,
         mixed,
-        flops=2 * own_count * depth * width2,
         name="attn_grad",
         after=(mlp_got, big_state[1], big_state[3]) if exact else (),
     )[0]
@@ -949,7 +991,6 @@
         wq,
         wk,
         wv,
-        flops=6 * own_count * depth * width2,
         name="first_grad",
         after=(attn_full,),
     )
@@ -968,12 +1009,26 @@
         attn_full,
         first_part,
         inputs,
+        stat_one,
         mlp_sums,
         att_sums,
         scratch=[pltpu.VMEM((depth, width2), F32), pltpu.VMEM((EXTRA, depth), F32)],
-        flops=6 * own_count * depth * width2,
+        cost=7,
         name="qkv_grad",
     )
+    finish = lambda after: call(
+        final_kernel,
+        [shape((own_count, depth))],
+        info,
+        inputs,
+        stat_one,
+        first_part,
+        first_got,
+        dmid,
+        vec,
+        name="final",
+        after=after,
+    )[0]
     tiles = (tile_own, swap_core(tile_sib))
     if exact:
         big_state = scatter_middle(info, big_state, False, after=(qkv_own,))
@@ -982,7 +1037,8 @@
         big_state = scatter_send(big_state, (1, 0))
         small_state = scatter_send(small_state, (0, 1))
         big_last = scatter_late(info, big_state, False)
-        small_state = scatter_middle(info, small_state, True, after=(big_last[0],))
+        inputs_low = finish((small_sent,))
+        small_state = scatter_middle(info, small_state, True, after=(big_last[0], inputs_low))
         small_state = scatter_send(small_state, (1, 0))
         fc_weight_grad, proj_weight_grad = call(
             scatter_big_kernel,
@@ -1005,6 +1061,7 @@
             after=(fc_weight_grad,),
         )
     else:
+        inputs_low = finish(())
         mine = scatter_plain(qkv_own, qkv_sib)
         qkv_weight_grad = mine[:, : 3 * width].reshape(local, 3, width).transpose(1, 0, 2)
         attn_weight_grad = mine[:, 3 * width :].T
@@ -1012,18 +1069,6 @@
     tile_got = swap_chip(tile.astype(BF)).astype(F32)
     mask = (jnp.arange(EXTRA) < 2)[:, None]
     tile = jnp.where(mask, tile.astype(BF).astype(F32) + tile_got, tile)
-    inputs_low = call(
-        final_kernel,
-        [shape((own_count, depth))],
-        info,
-        inputs,
-        first_part,
-        first_got,
-        dmid,
-        vec,
-        name="final",
-        after=(small_sent,) if exact else (),
-    )[0]
     inputs_grad = all_rows(info, inputs_low)
     out_low = call(
         output_kernel,
@@ -1035,6 +1080,7 @@
         mlp_got,
         vec,
         name="output",
+        after=(inputs_low,),
     )[0]
     outputs = all_rows(info, out_low)
 

time: 259 us -> 238 us (0.919)
  waiting for transfers between devices: 68.8 us -> 50.2 us
  starting transfers between devices: 46.9 us -> 41.2 us
  local copies, waits for them, and re-layouts: 18.5 us -> 21.7 us
    ppermute x5, waiting for transfers between devices: 19.7 us -> 2.25 us  [swap_chip(): return lax.ppermute(value, 'mp', CHIP_PAIRS)]
    ppermute x24, starting transfers between devices: 36.1 us -> 31.3 us  [swap_mask(): return lax.ppermute(value, 'dp', [(i, i ^ mask) for i in range(CHUNKS)])]
    ppermute x24, waiting for transfers between devices: 45.9 us -> 41.8 us  [swap_mask(): return lax.ppermute(value, 'dp', [(i, i ^ mask) for i in range(CHUNKS)])]
    unnamed x108 -> x110, local copies, waits for them, and re-layouts: 13.8 us -> 17 us
    ppermute x20, waiting for transfers between devices: 3.25 us -> 6.17 us  [swap_core(): return lax.ppermute(value, 'mp', CORE_PAIRS)]
    pallas_call x20 -> x22, Pallas kernels: 119 us -> 121 us  [call(): pl.pallas_call(run, out_shape=outs, in_specs=specs, out_specs=[pl.BlockSp...]
  transfers between devices with their start and end apart: 49 -> 49, of which waited for: 16 -> 22; matrix products, arithmetic and copies ran while one was open for 2% -> 2% of each run, Pallas kernels for 31% -> 38%
where the time goes in v2:
time: 238 us; the launch traced here: 237 us
  Pallas kernels  121 us (51%)
  waiting for transfers between devices  50.2 us (21%)
  starting transfers between devices  41.2 us (17%)
  local copies, waits for them, and re-layouts  21.7 us (9%)
    pallas_call x22, Pallas kernels, call(): pl.pallas_call(run, out_shape=outs, in_specs=specs, out_specs=[pl.BlockSp...  121 us
    ppermute x24, waiting for transfers between devices, swap_mask(): return lax.ppermute(value, 'dp', [(i, i ^ mask) for i in range(CHUNKS)])  41.8 us
    ppermute x24, starting transfers between devices, swap_mask(): return lax.ppermute(value, 'dp', [(i, i ^ mask) for i in range(CHUNKS)])  31.3 us
    unnamed x110, local copies, waits for them, and re-layouts  17 us
    ppermute x20, waiting for transfers between devices, swap_core(): return lax.ppermute(value, 'mp', CORE_PAIRS)  6.17 us
    ppermute x5, starting transfers between devices, swap_chip(): return lax.ppermute(value, 'mp', CHIP_PAIRS)  5.64 us
  transfers between devices with their start and end apart: 49, of which 22 were waited for; matrix products, arithmetic and copies ran while one was open for 2% of the time, Pallas kernels for 38%

profile of v2, /device:TPU:0, one launch (start us, length us, event | category | flops | bytes accessed | tf_op | source)
XLA Modules:
  0.0 236.9 jit_solution(13785544813762837337)
XLA Ops:
  4.8 3.3 %collective-permute-start.1 = (bf16[112,768]{1,0:T(8,128)(2,1)S(1)}, bf16[112,768]{1,0:T(8,128)(2,1)S(1)}, u32[]{:S(2)}, u32[]{:S(2)}) collective-permute-start(bf16[112,768]{1,0:T(8,128)(2,1)S(1)} %get-tuple-element.221), channel_id=1, source_target_pairs={{0,8},{4,12},{8,0},{12,4},{16,24},{20,28},{24,16},{28,20},{1,9},{5... | collective-permute-start | bytes 516104 | tf_op jit(solution)/shard_map/ppermute | solution.py:38
  8.1 2.6 %collective-permute-start.2 = (bf16[112,768]{1,0:T(8,128)(2,1)S(1)}, bf16[112,768]{1,0:T(8,128)(2,1)S(1)}, u32[]{:S(2)}, u32[]{:S(2)}) collective-permute-start(bf16[112,768]{1,0:T(8,128)(2,1)S(1)} %get-tuple-element.221), channel_id=1, source_target_pairs={{0,16},{4,20},{8,24},{12,28},{16,0},{20,4},{24,8},{28,12},{1,17},{... | collective-permute-start | bytes 516104 | tf_op jit(solution)/shard_map/ppermute | solution.py:38
  12.8 4.1 %stats.1.refs_2_.refs_7_ = f32[1024,256]{1,0:T(8,128)} custom-call(s32[2]{0:T(128)} %pad_add_fusion.refs_0_, bf16[1024,768]{1,0:T(8,128)(2,1)} %refs_1_.7), custom_call_target="tpu_custom_call" | custom-call | bytes 1024 | tf_op jit(solution)/shard_map/stats/pallas_call | solution.py:54
  23.6 7.1 %collective-permute-done.3 = bf16[112,768]{1,0:T(8,128)(2,1)S(1)} collective-permute-done((bf16[112,768]{1,0:T(8,128)(2,1)S(1)}, bf16[112,768]{1,0:T(8,128)(2,1)S(1)}, u32[]{:S(2)}, u32[]{:S(2)}) %collective-permute-start.3) | collective-permute-done | bytes 172064 | tf_op jit(solution)/shard_map/ppermute | solution.py:38
  35.6 8.0 %project.1 = (bf16[6,512,64]{2,1,0:T(8,128)(2,1)}, bf16[6,1024,64]{2,1,0:T(8,128)(2,1)}, bf16[6,1024,64]{2,1,0:T(8,128)(2,1)}, bf16[768,384]{1,0:T(8,128)(2,1)},...) custom-call(s32[2]{0:T(128)} %pad_add_fusion.refs_0_, ...), custom_call_target="tpu_custom_call" | custom-call | flops 8000000000 | bytes 1024 | tf_op jit(solution)/shard_map/project/pallas_call | solution.py:54
  43.6 2.0 collective-permute-done.10.refs_5_
  45.6 2.8 %collective-permute-done.11.refs_7_ = bf16[96,1536]{1,0:T(8,128)(2,1)S(1)} collective-permute-done((bf16[96,1536]{1,0:T(8,128)(2,1)S(1)}, bf16[96,1536]{1,0:T(8,128)(2,1)S(1)}, u32[]{:S(2)}, u32[]{:S(2)}) %collective-permute-start.11) | collective-permute-done | bytes 294944 | tf_op jit(solution)/shard_map/ppermute | solution.py:38
  50.0 1.9 collective-permute-start.15
  53.5 13.0 %attend.1 = (bf16[512,768]{1,0:T(8,128)(2,1)}, bf16[512,384]{1,0:T(8,128)(2,1)}, bf16[6,128,2560]{2,1,0:T(8,128)(2,1)}) custom-call(s32[2]{0:T(128)} %pad_add_fusion.refs_0_, bf16[6,512,64]{2,1,0:T(8,128)(2,1)} %get-tuple-element.98.refs_1_.refs_9_, bf16[6,1024,64]{2,1,0:T(8,128)(2,1)} %get-tuple-element.99.refs_2_.refs_10_, ...), custom_call_target="tpu_custom_call" | custom-call | flops 16000000000 | bytes 1024 | tf_op jit(solution)/shard_map/attend/pallas_call | solution.py:54
  75.0 7.3 %mlp_pre.1 = (bf16[768,1536]{1,0:T(8,128)(2,1)}, bf16[768,1536]{1,0:T(8,128)(2,1)}, bf16[512,768]{1,0:T(8,128)(2,1)}, bf16[512,1536]{1,0:T(8,128)(2,1)}) custom-call(s32[2]{0:T(128)} %pad_add_fusion.refs_0_, s32[1,1024]{1,0:T(1,128)} %bitcast.49, bf16[1024,768]{1,0:T(8,128)(2,1)} %refs_2_.1, bf16[96,1536]{1,0:T(8,128)(2,1)} %copy-done.4, ...), custom_call_target="tpu_custom_call" | custom-call | bytes 1024 | tf_op jit(solution)/shard_map/mlp_pre/pallas_call | solution.py:54
  82.3 2.2 collective-permute-done.8.refs_3_
  85.4 11.5 %mlp.1 = (bf16[512,768]{1,0:T(8,128)(2,1)}, bf16[512,1536]{1,0:T(8,128)(2,1)}, bf16[512,1536]{1,0:T(8,128)(2,1)}, bf16[512,768]{1,0:T(8,128)(2,1)}, f32[512,768]{1,0:T(8,128)}, /*index=5*/f32[512,256]{1,0:T(8,128)}) custom-call(s32[2]{0:T(128)} %pad_add_fusion.refs_0_, bf16[1024,768]{1,0:T(8,128)(2,1)} %refs_1_.7, ...), custom_call_target="tpu_custom_call" | custom-call | flops 10000000000 | bytes 1024 | tf_op jit(solution)/shard_map/mlp/pallas_call | solution.py:54
  98.5 9.7 %mlp_grad.1 = (bf16[512,768]{1,0:T(8,128)(2,1)}, bf16[8,96,1536]{2,1,0:T(8,128)(2,1)}, bf16[4,96,768]{2,1,0:T(8,128)(2,1)}, bf16[4,96,768]{2,1,0:T(8,128)(2,1)},...) custom-call(s32[2]{0:T(128)} %pad_add_fusion.refs_0_, ...), custom_call_target="tpu_custom_call" | custom-call | flops 8999999488 | bytes 1024 | tf_op jit(solution)/shard_map/mlp_grad/pallas_call | solution.py:54
  113.7 4.2 %scatter_first.2 = (f32[384,768]{1,0:T(8,128)}, bf16[384,768]{1,0:T(8,128)(2,1)}, f32[384,768]{1,0:T(8,128)}, bf16[384,768]{1,0:T(8,128)(2,1)}) custom-call(s32[2]{0:T(128)} %pad_add_fusion.refs_0_, bf16[8,96,1536]{2,1,0:T(8,128)(2,1)} %get-tuple-element.129.refs_1_, bf16[4,96,768]{2,1,0:T(8,128)(2,1)} %copy-done.9, bf16[4,96,768]{2,1,0:T(8,128)(2,1)} %copy-done.10, ...), custom_call_target="tpu_custom_call" | custom-call | bytes 1024 | tf_op jit(solution)/shard_map/scatter_first/pallas_call | solution.py:54
  119.7 18.0 %attend_back.1 = (f32[512,768]{1,0:T(8,128)}, bf16[512,768]{1,0:T(8,128)(2,1)}, f32[8,768]{1,0:T(8,128)}, bf16[512,384]{1,0:T(8,128)(2,1)}, f32[768,512]{1,0:T(8...) custom-call(s32[2]{0:T(128)} %pad_add_fusion.refs_0_, f32[512,768]{1,0:T(8,128)} %get-tuple-element.118.refs_1_.refs_2_, ...), custom_call_target="tpu_custom_call" | custom-call | flops 17999998976 | bytes 1024 | tf_op jit(solution)/shard_map/attend_back/pallas_call | solution.py:54
  139.6 2.9 %attn_grad.1.refs_8_.refs_4_ = f32[768,384]{1,0:T(8,128)} custom-call(s32[2]{0:T(128)} %pad_add_fusion.refs_0_, bf16[512,768]{1,0:T(8,128)(2,1)} %get-tuple-element.142.refs_1_, bf16[512,384]{1,0:T(8,128)(2,1)} %get-tuple-element.127.refs_8_.refs_2_, bf16[512,768]{1,0:T(8,128)(2,1)} %copy-done.1, bf16[384,768]{1,0:T(8,128)(2,1)} %copy-done.2, ...), custom_call_target="tpu_custom_call" | custom-call | bytes 1024 | tf_op jit(solution)/shard_map/attn_grad/pallas_call | solution.py:54
  143.3 4.6 %first_grad.1 = (bf16[512,768]{1,0:T(8,128)(2,1)}, bf16[768,512]{1,0:T(8,128)(2,1)}) custom-call(s32[2]{0:T(128)} %pad_add_fusion.refs_0_, bf16[512,384]{1,0:T(8,128)(2,1)} %get-tuple-element.135.refs_1_.refs_2_, f32[768,512]{1,0:T(8,128)} %get-tuple-element.136.refs_2_, bf16[384,512]{1,0:T(8,128)(2,1)} %copy-done.15, bf16[384,512]{1,0:T(8,128)(2,1)} %copy-done.16, ...), custom_call_target="tpu_custom_call" | custom-call | bytes 1024 | tf_op jit(solution)/shard_map/first_grad/pallas_call | solution.py:54
  147.9 6.9 %qkv_grad.1 = (bf16[8,96,768]{2,1,0:T(8,128)(2,1)}, bf16[4,96,768]{2,1,0:T(8,128)(2,1)}, bf16[4,96,768]{2,1,0:T(8,128)(2,1)}, bf16[16,768]{1,0:T(8,128)(2,1)}, bf16[16,768]{1,0:T(8,128)(2,1)}) custom-call(s32[2]{0:T(128)} %pad_add_fusion.refs_0_, bf16[512,768]{1,0:T(8,128)(2,1)} %get-tuple-element.146.refs_1_, ...), custom_call_target="tpu_custom_call" | custom-call | flops 7000000000 | bytes 1024 | tf_op jit(solution)/shard_map/qkv_grad/pallas_call | solution.py:54
  155.8 3.2 %scatter_second.2 = (f32[192,768]{1,0:T(8,128)}, bf16[192,768]{1,0:T(8,128)(2,1)}, f32[192,768]{1,0:T(8,128)}, bf16[192,768]{1,0:T(8,128)(2,1)}) custom-call(s32[2]{0:T(128)} %pad_add_fusion.refs_0_, f32[384,768]{1,0:T(8,128)} %get-tuple-element.155.refs_1_, bf16[384,768]{1,0:T(8,128)(2,1)} %copy-done.2, f32[384,768]{1,0:T(8,128)} %get-tuple-element.156.refs_3_, ...), custom_call_target="tpu_custom_call" | custom-call | bytes 1024 | tf_op jit(solution)/shard_map/scatter_second/pallas_call | solution.py:54
  160.0 3.0 %scatter_first.3 = (f32[400,384]{1,0:T(8,128)}, bf16[400,384]{1,0:T(8,128)(2,1)}, f32[400,384]{1,0:T(8,128)}, bf16[400,384]{1,0:T(8,128)(2,1)}) custom-call(s32[2]{0:T(128)} %pad_add_fusion.refs_0_, bf16[8,96,768]{2,1,0:T(8,128)(2,1)} %get-tuple-element.150.refs_5_.refs_1_, bf16[4,96,768]{2,1,0:T(8,128)(2,1)} %copy-done.13, bf16[4,96,768]{2,1,0:T(8,128)(2,1)} %copy-done.14, ...), custom_call_target="tpu_custom_call" | custom-call | bytes 1024 | tf_op jit(solution)/shard_map/scatter_first/pallas_call | solution.py:54
  167.1 13.3 %collective-permute-done.42.refs_2_ = bf16[192,768]{1,0:T(8,128)(2,1)S(1)} collective-permute-done((bf16[192,768]{1,0:T(8,128)(2,1)S(1)}, bf16[192,768]{1,0:T(8,128)(2,1)S(1)}, u32[]{:S(2)}, u32[]{:S(2)}) %collective-permute-start.42) | collective-permute-done | bytes 294944 | tf_op jit(solution)/shard_map/ppermute | solution.py:38
  181.3 2.4 %scatter_third.2 = (f32[96,1536]{1,0:T(8,128)}, bf16[96,1536]{1,0:T(8,128)(2,1)}) custom-call(s32[2]{0:T(128)} %pad_add_fusion.refs_0_, f32[192,768]{1,0:T(8,128)} %get-tuple-element.157.refs_6_.refs_1_, bf16[192,768]{1,0:T(8,128)(2,1)} %copy-done.35, f32[192,768]{1,0:T(8,128)} %get-tuple-element.163.refs_3_, bf16[192,768]{1,0:T(8,128)(2,1)} %copy-done.36), custom_call_target="tpu_custom_call" | custom-call | bytes 1024 | tf_op jit(solution)/shard_map/scatter_third/pallas_call | solution.py:54
  184.6 4.9 %final.1.refs_6_.refs_1_ = bf16[512,768]{1,0:T(8,128)(2,1)} custom-call(s32[2]{0:T(128)} %pad_add_fusion.refs_0_, bf16[1024,768]{1,0:T(8,128)(2,1)} %refs_1_.7, f32[1024,256]{1,0:T(8,128)} %stats.1.refs_2_.refs_7_, bf16[512,768]{1,0:T(8,128)(2,1)} %get-tuple-element.144.refs_5_.refs_3_, bf16[512,768]{1,0:T(8,128)(2,1)} %copy-done.6, ...), custom_call_target="tpu_custom_call" | custom-call | bytes 1024 | tf_op jit(solution)/shard_map/final/pallas_call | solution.py:54
  190.3 2.4 %scatter_second.3 = (f32[208,384]{1,0:T(8,128)}, bf16[208,384]{1,0:T(8,128)(2,1)}, f32[208,384]{1,0:T(8,128)}, bf16[208,384]{1,0:T(8,128)(2,1)}) custom-call(s32[2]{0:T(128)} %pad_add_fusion.refs_0_, f32[400,384]{1,0:T(8,128)} %get-tuple-element.159.refs_1_, bf16[400,384]{1,0:T(8,128)(2,1)} %copy-done.17, f32[400,384]{1,0:T(8,128)} %get-tuple-element.160.refs_3_, ...), custom_call_target="tpu_custom_call" | custom-call | bytes 1024 | tf_op jit(solution)/shard_map/scatter_second/pallas_call | solution.py:54
  195.6 3.9 %collective-permute-done.44.refs_2_ = bf16[208,384]{1,0:T(8,128)(2,1)S(1)} collective-permute-done((bf16[208,384]{1,0:T(8,128)(2,1)}, bf16[208,384]{1,0:T(8,128)(2,1)S(1)}, u32[]{:S(2)}, u32[]{:S(2)}) %collective-permute-start.44) | collective-permute-done | bytes 159776 | tf_op jit(solution)/shard_map/ppermute | solution.py:38
  200.7 2.0 scatter_third.3
  202.7 2.7 %collective-permute-start.46 = (bf16[112,768]{1,0:T(8,128)(2,1)}, bf16[112,768]{1,0:T(8,128)(2,1)S(1)}, u32[]{:S(2)}, u32[]{:S(2)}) collective-permute-start(bf16[112,768]{1,0:T(8,128)(2,1)} %get-tuple-element.171), channel_id=1, source_target_pairs={{0,16},{4,20},{8,24},{12,28},{16,0},{20,4},{24,8},{28,12},{1,17},{... | collective-permute-start | bytes 516104 | tf_op jit(solution)/shard_map/ppermute | solution.py:38
  205.4 9.2 %collective-permute-done.47.refs_2_ = bf16[96,1536]{1,0:T(8,128)(2,1)S(1)} collective-permute-done((bf16[96,1536]{1,0:T(8,128)(2,1)S(1)}, bf16[96,1536]{1,0:T(8,128)(2,1)S(1)}, u32[]{:S(2)}, u32[]{:S(2)}) %collective-permute-start.47) | collective-permute-done | bytes 294944 | tf_op jit(solution)/shard_map/ppermute | solution.py:38
  215.4 2.1 scatter_big.1
  224.3 3.6 %output.1.refs_1_ = bf16[512,768]{1,0:T(8,128)(2,1)} custom-call(s32[2]{0:T(128)} %pad_add_fusion.refs_0_, s32[1,1024]{1,0:T(1,128)} %bitcast.50, f32[512,768]{1,0:T(8,128)} %get-tuple-element.118.refs_1_.refs_2_, bf16[512,768]{1,0:T(8,128)(2,1)} %get-tuple-element.124.refs_3_, bf16[512,768]{1,0:T(8,128)(2,1)} %copy-done.1, ...), custom_call_target="tpu_custom_call" | custom-call | bytes 1024 | tf_op jit(solution)/shard_map/output/pallas_call | solution.py:54
  230.7 2.6 %merge.3 = bf16[1024,768]{1,0:T(8,128)(2,1)} custom-call(s32[2]{0:T(128)} %pad_add_fusion.refs_0_, bf16[512,768]{1,0:T(8,128)(2,1)} %final.1.refs_6_.refs_1_, bf16[512,768]{1,0:T(8,128)(2,1)} %copy-done.7), custom_call_target="tpu_custom_call" | custom-call | bytes 1024 | tf_op jit(solution)/shard_map/merge/pallas_call | solution.py:54
  234.2 2.6 %merge.2 = bf16[1024,768]{1,0:T(8,128)(2,1)} custom-call(s32[2]{0:T(128)} %pad_add_fusion.refs_0_, bf16[512,768]{1,0:T(8,128)(2,1)} %output.1.refs_1_, bf16[512,768]{1,0:T(8,128)(2,1)} %copy-done.8), custom_call_target="tpu_custom_call" | custom-call | bytes 1024 | tf_op jit(solution)/shard_map/merge/pallas_call | solution.py:54
  (222 shorter events, 65.5 us)
Async XLA Ops:
  4.8 12.2 %collective-permute-start.1 = (bf16[112,768]{1,0:T(8,128)(2,1)S(1)}, bf16[112,768]{1,0:T(8,128)(2,1)S(1)}, u32[]{:S(2)}, u32[]{:S(2)}) collective-permute-start(bf16[112,768]{1,0:T(8,128)(2,1)S(1)} %get-tuple-element.221), channel_id=1, source_target_pairs={{0,8},{4,12},{8,0},{12,4},{16,24},{20,28},{24,16},{28,20},{1,9},{5... | collective-permute-start | bytes 516104 | tf_op jit(solution)/shard_map/ppermute | solution.py:38
  8.1 10.5 %collective-permute-start.2 = (bf16[112,768]{1,0:T(8,128)(2,1)S(1)}, bf16[112,768]{1,0:T(8,128)(2,1)S(1)}, u32[]{:S(2)}, u32[]{:S(2)}) collective-permute-start(bf16[112,768]{1,0:T(8,128)(2,1)S(1)} %get-tuple-element.221), channel_id=1, source_target_pairs={{0,16},{4,20},{8,24},{12,28},{16,0},{20,4},{24,8},{28,12},{1,17},{... | collective-permute-start | bytes 516104 | tf_op jit(solution)/shard_map/ppermute | solution.py:38
  10.7 12.9 %collective-permute-start = (bf16[112,768]{1,0:T(8,128)(2,1)S(1)}, bf16[112,768]{1,0:T(8,128)(2,1)S(1)}, u32[]{:S(2)}, u32[]{:S(2)}) collective-permute-start(bf16[112,768]{1,0:T(8,128)(2,1)S(1)} %get-tuple-element.221), channel_id=1, source_target_pairs={{0,4},{4,0},{8,12},{12,8},{16,20},{20,16},{24,28},{28,24},{1,5},{5... | collective-permute-start | bytes 516104 | tf_op jit(solution)/shard_map/ppermute | solution.py:38
  18.6 12.1 %collective-permute-start.4 = (bf16[112,768]{1,0:T(8,128)(2,1)S(1)}, bf16[112,768]{1,0:T(8,128)(2,1)S(1)}, u32[]{:S(2)}, u32[]{:S(2)}) collective-permute-start(bf16[112,768]{1,0:T(8,128)(2,1)S(1)} %collective-permute-done.2), channel_id=1, source_target_pairs={{0,4},{4,0},{8,12},{12,8},{16,20},{20,16},{24,28},{28,24},{1,5},{5... | collective-permute-start | bytes 516104 | tf_op jit(solution)/shard_map/ppermute | solution.py:38
  20.1 10.7 %collective-permute-start.5 = (bf16[112,768]{1,0:T(8,128)(2,1)S(1)}, bf16[112,768]{1,0:T(8,128)(2,1)S(1)}, u32[]{:S(2)}, u32[]{:S(2)}) collective-permute-start(bf16[112,768]{1,0:T(8,128)(2,1)S(1)} %collective-permute-done.2), channel_id=1, source_target_pairs={{0,8},{4,12},{8,0},{12,4},{16,24},{20,28},{24,16},{28,20},{1,9},{5... | collective-permute-start | bytes 516104 | tf_op jit(solution)/shard_map/ppermute | solution.py:38
  20.5 10.3 %collective-permute-start.6 = (bf16[112,768]{1,0:T(8,128)(2,1)S(1)}, bf16[112,768]{1,0:T(8,128)(2,1)S(1)}, u32[]{:S(2)}, u32[]{:S(2)}) collective-permute-start(bf16[112,768]{1,0:T(8,128)(2,1)S(1)} %collective-permute-done.2), channel_id=1, source_target_pairs={{0,12},{4,8},{8,4},{12,0},{16,28},{20,24},{24,20},{28,16},{1,13},{... | collective-permute-start | bytes 516104 | tf_op jit(solution)/shard_map/ppermute | solution.py:38
  22.1 8.6 %collective-permute-start.3 = (bf16[112,768]{1,0:T(8,128)(2,1)S(1)}, bf16[112,768]{1,0:T(8,128)(2,1)S(1)}, u32[]{:S(2)}, u32[]{:S(2)}) collective-permute-start(bf16[112,768]{1,0:T(8,128)(2,1)S(1)} %collective-permute-done.1), channel_id=1, source_target_pairs={{0,4},{4,0},{8,12},{12,8},{16,20},{20,16},{24,28},{28,24},{1,5},{5... | collective-permute-start | bytes 516104 | tf_op jit(solution)/shard_map/ppermute | solution.py:38
  31.0 14.6 %collective-permute-start.10 = (bf16[96,1536]{1,0:T(8,128)(2,1)S(1)}, bf16[96,1536]{1,0:T(8,128)(2,1)S(1)}, u32[]{:S(2)}, u32[]{:S(2)}) collective-permute-start(bf16[96,1536]{1,0:T(8,128)(2,1)S(1)} %pad_maximum_fusion.refs_3_), channel_id=1, source_target_pairs={{0,8},{4,12},{8,0},{12,4},{16,24},{20,28},{24,16},{28,20},{1,9},{5... | collective-permute-start | bytes 884744 | tf_op jit(solution)/shard_map/ppermute | solution.py:38
  32.1 16.4 %collective-permute-start.11 = (bf16[96,1536]{1,0:T(8,128)(2,1)S(1)}, bf16[96,1536]{1,0:T(8,128)(2,1)S(1)}, u32[]{:S(2)}, u32[]{:S(2)}) collective-permute-start(bf16[96,1536]{1,0:T(8,128)(2,1)S(1)} %pad_maximum_fusion.refs_3_), channel_id=1, source_target_pairs={{0,16},{4,20},{8,24},{12,28},{16,0},{20,4},{24,8},{28,12},{1,17},{... | collective-permute-start | bytes 884744 | tf_op jit(solution)/shard_map/ppermute | solution.py:38
  33.2 33.4 %collective-permute-start.9 = (bf16[96,1536]{1,0:T(8,128)(2,1)S(1)}, bf16[96,1536]{1,0:T(8,128)(2,1)S(1)}, u32[]{:S(2)}, u32[]{:S(2)}) collective-permute-start(bf16[96,1536]{1,0:T(8,128)(2,1)S(1)} %pad_maximum_fusion.refs_3_), channel_id=1, source_target_pairs={{0,4},{4,0},{8,12},{12,8},{16,20},{20,16},{24,28},{28,24},{1,5},{5... | collective-permute-start | bytes 884744 | tf_op jit(solution)/shard_map/ppermute | solution.py:38
  48.4 20.9 %collective-permute-start.13 = (bf16[96,1536]{1,0:T(8,128)(2,1)S(1)}, bf16[96,1536]{1,0:T(8,128)(2,1)S(1)}, u32[]{:S(2)}, u32[]{:S(2)}) collective-permute-start(bf16[96,1536]{1,0:T(8,128)(2,1)S(1)} %collective-permute-done.11.refs_7_), channel_id=1, source_target_pairs={{0,4},{4,0},{8,12},{12,8},{16,20},{20,16},{24,28},{28,24},{1,5},{5... | collective-permute-start | bytes 884744 | tf_op jit(solution)/shard_map/ppermute | solution.py:38
  50.0 19.3 %collective-permute-start.14 = (bf16[96,1536]{1,0:T(8,128)(2,1)S(1)}, bf16[96,1536]{1,0:T(8,128)(2,1)S(1)}, u32[]{:S(2)}, u32[]{:S(2)}) collective-permute-start(bf16[96,1536]{1,0:T(8,128)(2,1)S(1)} %collective-permute-done.11.refs_7_), channel_id=1, source_target_pairs={{0,8},{4,12},{8,0},{12,4},{16,24},{20,28},{24,16},{28,20},{1,9},{5... | collective-permute-start | bytes 884744 | tf_op jit(solution)/shard_map/ppermute | solution.py:38
  50.0 19.4 %collective-permute-start.15 = (bf16[96,1536]{1,0:T(8,128)(2,1)S(1)}, bf16[96,1536]{1,0:T(8,128)(2,1)S(1)}, u32[]{:S(2)}, u32[]{:S(2)}) collective-permute-start(bf16[96,1536]{1,0:T(8,128)(2,1)S(1)} %collective-permute-done.11.refs_7_), channel_id=1, source_target_pairs={{0,12},{4,8},{8,4},{12,0},{16,28},{20,24},{24,20},{28,16},{1,13},{... | collective-permute-start | bytes 884744 | tf_op jit(solution)/shard_map/ppermute | solution.py:38
  51.9 17.4 %collective-permute-start.12 = (bf16[96,1536]{1,0:T(8,128)(2,1)S(1)}, bf16[96,1536]{1,0:T(8,128)(2,1)S(1)}, u32[]{:S(2)}, u32[]{:S(2)}) collective-permute-start(bf16[96,1536]{1,0:T(8,128)(2,1)S(1)} %collective-permute-done.10.refs_5_), channel_id=1, source_target_pairs={{0,4},{4,0},{8,12},{12,8},{16,20},{20,16},{24,28},{28,24},{1,5},{5... | collective-permute-start | bytes 884744 | tf_op jit(solution)/shard_map/ppermute | solution.py:38
  66.6 18.0 %collective-permute-start.8 = (bf16[512,768]{1,0:T(8,128)(2,1)}, bf16[512,768]{1,0:T(8,128)(2,1)S(1)}, u32[]{:S(2)}, u32[]{:S(2)}) collective-permute-start(bf16[512,768]{1,0:T(8,128)(2,1)} %get-tuple-element.102.refs_2_), channel_id=1, source_target_pairs={{0,2},{2,0},{1,3},{3,1},{4,6},{6,4},{5,7},{7,5},{8,10},{10,8},{9,1... | collective-permute-start | bytes 2359304 | tf_op jit(solution)/shard_map/ppermute | solution.py:34
  97.0 21.8 %collective-permute-start.25 = (bf16[512,768]{1,0:T(8,128)(2,1)}, bf16[512,768]{1,0:T(8,128)(2,1)S(1)}, u32[]{:S(2)}, u32[]{:S(2)}) collective-permute-start(bf16[512,768]{1,0:T(8,128)(2,1)} %get-tuple-element.126.refs_4_), channel_id=1, source_target_pairs={{0,2},{2,0},{1,3},{3,1},{4,6},{6,4},{5,7},{7,5},{8,10},{10,8},{9,1... | collective-permute-start | bytes 2359304 | tf_op jit(solution)/shard_map/ppermute | solution.py:34
  110.4 27.9 %collective-permute-start.24 = (bf16[512,768]{1,0:T(8,128)(2,1)}, bf16[512,768]{1,0:T(8,128)(2,1)S(1)}, u32[]{:S(2)}, u32[]{:S(2)}) collective-permute-start(bf16[512,768]{1,0:T(8,128)(2,1)} %get-tuple-element.124.refs_3_), channel_id=1, source_target_pairs={{0,2},{2,0},{1,3},{3,1},{4,6},{6,4},{5,7},{7,5},{8,10},{10,8},{9,1... | collective-permute-start | bytes 2359304 | tf_op jit(solution)/shard_map/ppermute | solution.py:34
  118.0 20.3 %collective-permute-start.32 = (bf16[384,768]{1,0:T(8,128)(2,1)}, bf16[384,768]{1,0:T(8,128)(2,1)S(1)}, u32[]{:S(2)}, u32[]{:S(2)}) collective-permute-start(bf16[384,768]{1,0:T(8,128)(2,1)} %get-tuple-element.134.refs_13_), channel_id=1, source_target_pairs={{0,4},{4,0},{8,12},{12,8},{16,20},{20,16},{24,28},{28,24},{1,5},{5... | collective-permute-start | bytes 1769480 | tf_op jit(solution)/shard_map/ppermute | solution.py:38
  118.4 19.9 %collective-permute-start.33 = (bf16[384,768]{1,0:T(8,128)(2,1)}, bf16[384,768]{1,0:T(8,128)(2,1)S(1)}, u32[]{:S(2)}, u32[]{:S(2)}) collective-permute-start(bf16[384,768]{1,0:T(8,128)(2,1)} %get-tuple-element.143), channel_id=1, source_target_pairs={{0,8},{4,12},{8,0},{12,4},{16,24},{20,28},{24,16},{28,20},{1,9},{5... | collective-permute-start | bytes 1769480 | tf_op jit(solution)/shard_map/ppermute | solution.py:38
  137.7 4.7 %collective-permute-start.30 = (bf16[384,512]{1,0:T(8,128)(2,1)}, bf16[384,512]{1,0:T(8,128)(2,1)S(1)}, u32[]{:S(2)}, u32[]{:S(2)}) collective-permute-start(bf16[384,512]{1,0:T(8,128)(2,1)} %get-tuple-element.137), channel_id=1, source_target_pairs={{0,1},{1,0},{2,3},{3,2},{4,5},{5,4},{6,7},{7,6},{8,9},{9,8},{10,11... | collective-permute-start | bytes 1179656 | tf_op jit(solution)/shard_map/ppermute | solution.py:30
  155.3 28.4 %collective-permute-start.34 = (bf16[512,768]{1,0:T(8,128)(2,1)S(1)}, bf16[512,768]{1,0:T(8,128)(2,1)S(1)}, u32[]{:S(2)}, u32[]{:S(2)}) collective-permute-start(bf16[512,768]{1,0:T(8,128)(2,1)S(1)} %copy-done.5), channel_id=1, source_target_pairs={{0,2},{2,0},{1,3},{3,1},{4,6},{6,4},{5,7},{7,5},{8,10},{10,8},{9,1... | collective-permute-start | bytes 2359304 | tf_op jit(solution)/shard_map/ppermute | solution.py:34
  163.1 26.4 %collective-permute-start.40 = (bf16[400,384]{1,0:T(8,128)(2,1)}, bf16[400,384]{1,0:T(8,128)(2,1)S(1)}, u32[]{:S(2)}, u32[]{:S(2)}) collective-permute-start(bf16[400,384]{1,0:T(8,128)(2,1)} %get-tuple-element.158.refs_7_), channel_id=1, source_target_pairs={{0,4},{4,0},{8,12},{12,8},{16,20},{20,16},{24,28},{28,24},{1,5},{5... | collective-permute-start | bytes 921608 | tf_op jit(solution)/shard_map/ppermute | solution.py:38
  164.5 25.0 %collective-permute-start.41 = (bf16[400,384]{1,0:T(8,128)(2,1)}, bf16[400,384]{1,0:T(8,128)(2,1)S(1)}, u32[]{:S(2)}, u32[]{:S(2)}) collective-permute-start(bf16[400,384]{1,0:T(8,128)(2,1)} %get-tuple-element.161), channel_id=1, source_target_pairs={{0,8},{4,12},{8,0},{12,4},{16,24},{20,28},{24,16},{28,20},{1,9},{5... | collective-permute-start | bytes 921608 | tf_op jit(solution)/shard_map/ppermute | solution.py:38
  166.3 14.2 %collective-permute-start.42 = (bf16[192,768]{1,0:T(8,128)(2,1)S(1)}, bf16[192,768]{1,0:T(8,128)(2,1)S(1)}, u32[]{:S(2)}, u32[]{:S(2)}) collective-permute-start(bf16[192,768]{1,0:T(8,128)(2,1)S(1)} %copy-done.50), channel_id=1, source_target_pairs={{0,8},{4,12},{8,0},{12,4},{16,24},{20,28},{24,16},{28,20},{1,9},{5... | collective-permute-start | bytes 884744 | tf_op jit(solution)/shard_map/ppermute | solution.py:38
  166.6 13.9 %collective-permute-start.43 = (bf16[192,768]{1,0:T(8,128)(2,1)S(1)}, bf16[192,768]{1,0:T(8,128)(2,1)S(1)}, u32[]{:S(2)}, u32[]{:S(2)}) collective-permute-start(bf16[192,768]{1,0:T(8,128)(2,1)S(1)} %copy-done.49), channel_id=1, source_target_pairs={{0,4},{4,0},{8,12},{12,8},{16,20},{20,16},{24,28},{28,24},{1,5},{5... | collective-permute-start | bytes 884744 | tf_op jit(solution)/shard_map/ppermute | solution.py:38
  192.8 6.7 %collective-permute-start.44 = (bf16[208,384]{1,0:T(8,128)(2,1)}, bf16[208,384]{1,0:T(8,128)(2,1)S(1)}, u32[]{:S(2)}, u32[]{:S(2)}) collective-permute-start(bf16[208,384]{1,0:T(8,128)(2,1)} %get-tuple-element.167), channel_id=1, source_target_pairs={{0,8},{4,12},{8,0},{12,4},{16,24},{20,28},{24,16},{28,20},{1,9},{5... | collective-permute-start | bytes 479240 | tf_op jit(solution)/shard_map/ppermute | solution.py:38
  194.5 5.5 %collective-permute-start.45 = (bf16[208,384]{1,0:T(8,128)(2,1)}, bf16[208,384]{1,0:T(8,128)(2,1)S(1)}, u32[]{:S(2)}, u32[]{:S(2)}) collective-permute-start(bf16[208,384]{1,0:T(8,128)(2,1)} %get-tuple-element.169), channel_id=1, source_target_pairs={{0,4},{4,0},{8,12},{12,8},{16,20},{20,16},{24,28},{28,24},{1,5},{5... | collective-permute-start | bytes 479240 | tf_op jit(solution)/shard_map/ppermute | solution.py:38
  195.0 19.7 %collective-permute-start.47 = (bf16[96,1536]{1,0:T(8,128)(2,1)S(1)}, bf16[96,1536]{1,0:T(8,128)(2,1)S(1)}, u32[]{:S(2)}, u32[]{:S(2)}) collective-permute-start(bf16[96,1536]{1,0:T(8,128)(2,1)S(1)} %copy-done.48), channel_id=1, source_target_pairs={{0,16},{4,20},{8,24},{12,28},{16,0},{20,4},{24,8},{28,12},{1,17},{... | collective-permute-start | bytes 884744 | tf_op jit(solution)/shard_map/ppermute | solution.py:38
  202.7 14.8 %collective-permute-start.46 = (bf16[112,768]{1,0:T(8,128)(2,1)}, bf16[112,768]{1,0:T(8,128)(2,1)S(1)}, u32[]{:S(2)}, u32[]{:S(2)}) collective-permute-start(bf16[112,768]{1,0:T(8,128)(2,1)} %get-tuple-element.171), channel_id=1, source_target_pairs={{0,16},{4,20},{8,24},{12,28},{16,0},{20,4},{24,8},{28,12},{1,17},{... | collective-permute-start | bytes 516104 | tf_op jit(solution)/shard_map/ppermute | solution.py:38
  220.9 7.4 %collective-permute-start.48 = (bf16[16,768]{1,0:T(8,128)(2,1)S(1)}, bf16[16,768]{1,0:T(8,128)(2,1)S(1)}, u32[]{:S(2)}, u32[]{:S(2)}) collective-permute-start(bf16[16,768]{1,0:T(8,128)(2,1)S(1)} %convert_element_type.12), channel_id=1, source_target_pairs={{0,2},{2,0},{1,3},{3,1},{4,6},{6,4},{5,7},{7,5},{8,10},{10,8},{9,1... | collective-permute-start | bytes 73736 | tf_op jit(solution)/shard_map/ppermute | solution.py:34
  224.3 5.6 %collective-permute-start.39 = (bf16[512,768]{1,0:T(8,128)(2,1)S(1)}, bf16[512,768]{1,0:T(8,128)(2,1)S(1)}, u32[]{:S(2)}, u32[]{:S(2)}) collective-permute-start(bf16[512,768]{1,0:T(8,128)(2,1)S(1)} %copy-done), channel_id=1, source_target_pairs={{0,1},{1,0},{2,3},{3,2},{4,5},{5,4},{6,7},{7,6},{8,9},{9,8},{10,11... | collective-permute-start | bytes 2359304 | tf_op jit(solution)/shard_map/ppermute | solution.py:30
  227.8 5.6 %collective-permute-start.38 = (bf16[512,768]{1,0:T(8,128)(2,1)}, bf16[512,768]{1,0:T(8,128)(2,1)S(1)}, u32[]{:S(2)}, u32[]{:S(2)}) collective-permute-start(bf16[512,768]{1,0:T(8,128)(2,1)} %output.1.refs_1_), channel_id=1, source_target_pairs={{0,1},{1,0},{2,3},{3,2},{4,5},{5,4},{6,7},{7,6},{8,9},{9,8},{10,11... | collective-permute-start | bytes 2359304 | tf_op jit(solution)/shard_map/ppermute | solution.py:30
  (68 other events, 278.8 us)

commit v3 on v2

--- a/solution.py
+++ b/solution.py
@@ -67,14 +67,12 @@
     return jax.ShapeDtypeStruct(tuple(dims), dtype)
 
 
-def gather_blocks(message, behind=None):
+def gather_blocks(message, behind, far=None):
     got = {0: message}
-    got[4] = swap_mask(message, 4)
+    got[4] = swap_mask(message, 4) if far is None else far
     got[2] = swap_mask(message, 2)
     got[1] = swap_mask(message, 1)
-    four, two = got[4], got[2]
-    if behind is not None:
-        four, two = lax.optimization_barrier((four, two, behind))[:2]
+    four, two = lax.optimization_barrier((got[4], got[2], behind))[:2]
     got[7] = swap_mask(four, 3)
     got[5] = swap_mask(four, 1)
     got[6] = swap_mask(four, 2)
@@ -595,7 +593,7 @@
         out_ref[pl.ds(yours, TILE), :] = got_ref[sl, :]
 
 
-def all_rows(info, own):
+def all_rows(info, own, after=()):
     return call(
         merge_kernel,
         [shape((2 * own.shape[0], own.shape[1]))],
@@ -603,6 +601,8 @@
         own,
         swap_core(own),
         name="merge",
+        cost=3,
+        after=after,
     )[0]
 
 
@@ -722,6 +722,7 @@
         info,
         *state,
         name="scatter_second",
+        cost=2 if tiled else 0,
         after=after,
     )
 
@@ -736,6 +737,7 @@
         info,
         *state,
         name="scatter_third",
+        cost=2 if tiled else 0,
         after=after,
     )
     return left, swap_bit(send, 2)
@@ -810,7 +812,9 @@
     )
     wide = jnp.concatenate([fc_weight, proj_weight.T], 1)
     if count == CHUNKS:
-        own_a = jnp.stack(gather_blocks(jnp.concatenate([mats, tile], 0), stat_one))
+        blocks = gather_blocks(jnp.concatenate([mats, tile], 0), stat_one)
+        own_a = jnp.stack(blocks)
+        far = swap_mask(lax.optimization_barrier((wide, blocks[4]))[0], 4)
         wide = lax.optimization_barrier((wide, own_a))[0]
     else:
         full = lax.all_gather(mats, "dp", axis=0, tiled=True).reshape(CHUNKS, base, depth)
@@ -845,7 +849,7 @@
         name="project",
     )
     if count == CHUNKS:
-        blocks = gather_blocks(wide, q)
+        blocks = gather_blocks(wide, q, far)
     tiles = own_count // TILE
     part, mixed, probs = call(
         attend_kernel,
@@ -981,6 +985,10 @@
         name="attn_grad",
         after=(mlp_got, big_state[1], big_state[3]) if exact else (),
     )[0]
+    if exact:
+        big_state = scatter_middle(info, big_state, False, after=(attn_full,))
+        big_ready = big_state[0]
+        big_state = scatter_send(big_state, (1, 0))
     first_part, dkv = call(
         first_grad_kernel,
         [shape((own_count, depth)), shape((2 * width2, own_count))],
@@ -992,7 +1000,7 @@
         wk,
         wv,
         name="first_grad",
-        after=(attn_full,),
+        after=(big_ready,) if exact else (),
     )
     first_got = swap_chip(first_part)
     qkv_own, *qkv_sib, tile_own, tile_sib = call(
@@ -1015,6 +1023,7 @@
         scratch=[pltpu.VMEM((depth, width2), F32), pltpu.VMEM((EXTRA, depth), F32)],
         cost=7,
         name="qkv_grad",
+        after=(big_state[1], big_state[3]) if exact else (),
     )
     finish = lambda after: call(
         final_kernel,
@@ -1027,27 +1036,43 @@
         dmid,
         vec,
         name="final",
+        cost=5,
+        after=after,
+    )[0]
+    output = lambda after: call(
+        output_kernel,
+        [shape((own_count, depth))],
+        info,
+        seg_row,
+        middle,
+        mlp_part,
+        mlp_got,
+        vec,
+        name="output",
         after=after,
     )[0]
     tiles = (tile_own, swap_core(tile_sib))
     if exact:
-        big_state = scatter_middle(info, big_state, False, after=(qkv_own,))
-        small_state = scatter_start(info, qkv_own, qkv_sib, tiles, after=(big_state[0],))
+        big_last = scatter_late(info, big_state, False, after=(qkv_own,))
+        small_state = scatter_start(info, qkv_own, qkv_sib, tiles, after=(big_last[0],))
         small_sent = small_state[1]
-        big_state = scatter_send(big_state, (1, 0))
         small_state = scatter_send(small_state, (0, 1))
-        big_last = scatter_late(info, big_state, False)
-        inputs_low = finish((small_sent,))
-        small_state = scatter_middle(info, small_state, True, after=(big_last[0], inputs_low))
+        out_low = output((small_sent,))
+        inputs_low = finish((out_low,))
+        small_state = scatter_middle(info, small_state, True, after=(inputs_low, big_last[1]))
+        small_sent = small_state[1]
         small_state = scatter_send(small_state, (1, 0))
+        outputs = all_rows(info, out_low, (small_sent,))
         fc_weight_grad, proj_weight_grad = call(
             scatter_big_kernel,
             [shape((local, units), F32), shape((units, local), F32)],
             info,
             *big_last,
             name="scatter_big",
+            cost=2,
         )
-        small_last = scatter_late(info, small_state, True)
+        small_last = scatter_late(info, small_state, True, after=(outputs,))
+        inputs_grad = all_rows(info, inputs_low, (small_last[0],))
         qkv_weight_grad, attn_weight_grad, tile = call(
             scatter_small_kernel,
             [
@@ -1058,10 +1083,12 @@
             info,
             *small_last,
             name="scatter_small",
-            after=(fc_weight_grad,),
+            cost=2,
+            after=(fc_weight_grad, inputs_grad),
         )
     else:
-        inputs_low = finish(())
+        inputs_grad = all_rows(info, finish(()))
+        outputs = all_rows(info, output(()))
         mine = scatter_plain(qkv_own, qkv_sib)
         qkv_weight_grad = mine[:, : 3 * width].reshape(local, 3, width).transpose(1, 0, 2)
         attn_weight_grad = mine[:, 3 * width :].T
@@ -1069,21 +1096,6 @@
     tile_got = swap_chip(tile.astype(BF)).astype(F32)
     mask = (jnp.arange(EXTRA) < 2)[:, None]
     tile = jnp.where(mask, tile.astype(BF).astype(F32) + tile_got, tile)
-    inputs_grad = all_rows(info, inputs_low)
-    out_low = call(
-        output_kernel,
-        [shape((own_count, depth))],
-        info,
-        seg_row,
-        middle,
-        mlp_part,
-        mlp_got,
-        vec,
-        name="output",
-        after=(inputs_low,),
-    )[0]
-    outputs = all_rows(info, out_low)
-
     parts = lax.dynamic_slice(tile, (0, index * local), (7, local))
     bias_sum = tile[7, :width2].reshape(2, heads, HD).transpose(1, 0, 2).reshape(heads, 2 * HD)
     qv_bias_grad = lax.dynamic_slice(bias_sum, (0, index * bias_width), (heads, bias_width))

time: 238 us -> 220 us (0.924)
  waiting for transfers between devices: 50.2 us -> 29.4 us
  starting transfers between devices: 41.2 us -> 45.3 us
    ppermute x24, waiting for transfers between devices: 41.8 us -> 18.5 us  [swap_mask(): return lax.ppermute(value, 'dp', [(i, i ^ mask) for i in range(CHUNKS)])]
    ppermute x24, starting transfers between devices: 31.3 us -> 36.3 us  [swap_mask(): return lax.ppermute(value, 'dp', [(i, i ^ mask) for i in range(CHUNKS)])]
    ppermute x5, waiting for transfers between devices: 2.25 us -> 4.7 us  [swap_chip(): return lax.ppermute(value, 'mp', CHIP_PAIRS)]
    unnamed x110 -> x100, local copies, waits for them, and re-layouts: 17 us -> 15.8 us
  transfers between devices with their start and end apart: 49 -> 49, of which waited for: 22 -> 26; matrix products, arithmetic and copies ran while one was open for 2% -> 1% of each run, Pallas kernels for 38% -> 49%
where the time goes in v3:
time: 220 us
  Pallas kernels  121 us (55%)
  starting transfers between devices  45.3 us (21%)
  waiting for transfers between devices  29.4 us (13%)
  local copies, waits for them, and re-layouts  20.4 us (9%)
  other arithmetic  2.46 us (1%)
    pallas_call x22, Pallas kernels, call(): pl.pallas_call(run, out_shape=outs, in_specs=specs, out_specs=[pl.BlockSp...  121 us
    ppermute x24, starting transfers between devices, swap_mask(): return lax.ppermute(value, 'dp', [(i, i ^ mask) for i in range(CHUNKS)])  36.3 us
    ppermute x24, waiting for transfers between devices, swap_mask(): return lax.ppermute(value, 'dp', [(i, i ^ mask) for i in range(CHUNKS)])  18.5 us
    unnamed x100, local copies, waits for them, and re-layouts  15.8 us
    ppermute x20, waiting for transfers between devices, swap_core(): return lax.ppermute(value, 'mp', CORE_PAIRS)  6.17 us
    ppermute x5, waiting for transfers between devices, swap_chip(): return lax.ppermute(value, 'mp', CHIP_PAIRS)  4.7 us
    ppermute x5, starting transfers between devices, swap_chip(): return lax.ppermute(value, 'mp', CHIP_PAIRS)  4.63 us
  transfers between devices with their start and end apart: 49, of which 26 were waited for; matrix products, arithmetic and copies ran while one was open for 1% of the time, Pallas kernels for 49%

profile of v3, /device:TPU:0, one launch (start us, length us, event | category | flops | bytes accessed | tf_op | source)
XLA Modules:
  0.0 219.7 jit_solution(16445821072978967661)
XLA Ops:
  4.8 4.2 %collective-permute-start.2 = (bf16[112,768]{1,0:T(8,128)(2,1)S(1)}, bf16[112,768]{1,0:T(8,128)(2,1)S(1)}, u32[]{:S(2)}, u32[]{:S(2)}) collective-permute-start(bf16[112,768]{1,0:T(8,128)(2,1)S(1)} %get-tuple-element.223), channel_id=1, source_target_pairs={{0,16},{4,20},{8,24},{12,28},{16,0},{20,4},{24,8},{28,12},{1,17},{... | collective-permute-start | bytes 516104 | tf_op jit(solution)/shard_map/ppermute | solution.py:38
  12.8 4.2 %stats.1.refs_2_.refs_7_ = f32[1024,256]{1,0:T(8,128)} custom-call(s32[2]{0:T(128)} %pad_add_fusion.refs_0_, bf16[1024,768]{1,0:T(8,128)(2,1)} %refs_1_.7), custom_call_target="tpu_custom_call" | custom-call | bytes 1024 | tf_op jit(solution)/shard_map/stats/pallas_call | solution.py:54
  20.8 1.7 collective-permute-start.3
  22.6 7.5 %collective-permute-done.3 = bf16[112,768]{1,0:T(8,128)(2,1)S(1)} collective-permute-done((bf16[112,768]{1,0:T(8,128)(2,1)S(1)}, bf16[112,768]{1,0:T(8,128)(2,1)S(1)}, u32[]{:S(2)}, u32[]{:S(2)}) %collective-permute-start.3) | collective-permute-done | bytes 172064 | tf_op jit(solution)/shard_map/ppermute | solution.py:38
  30.3 2.2 %collective-permute-start.11 = (bf16[96,1536]{1,0:T(8,128)(2,1)S(1)}, bf16[96,1536]{1,0:T(8,128)(2,1)S(1)}, u32[]{:S(2)}, u32[]{:S(2)}) collective-permute-start(bf16[96,1536]{1,0:T(8,128)(2,1)S(1)} %pad_maximum_fusion.refs_3_), channel_id=1, source_target_pairs={{0,16},{4,20},{8,24},{12,28},{16,0},{20,4},{24,8},{28,12},{1,17},{... | collective-permute-start | bytes 884744 | tf_op jit(solution)/shard_map/ppermute | solution.py:38
  32.6 2.7 %collective-permute-start.10 = (bf16[96,1536]{1,0:T(8,128)(2,1)S(1)}, bf16[96,1536]{1,0:T(8,128)(2,1)S(1)}, u32[]{:S(2)}, u32[]{:S(2)}) collective-permute-start(bf16[96,1536]{1,0:T(8,128)(2,1)S(1)} %pad_maximum_fusion.refs_3_), channel_id=1, source_target_pairs={{0,8},{4,12},{8,0},{12,4},{16,24},{20,28},{24,16},{28,20},{1,9},{5... | collective-permute-start | bytes 884744 | tf_op jit(solution)/shard_map/ppermute | solution.py:38
  37.9 8.0 %project.1 = (bf16[6,512,64]{2,1,0:T(8,128)(2,1)}, bf16[6,1024,64]{2,1,0:T(8,128)(2,1)}, bf16[6,1024,64]{2,1,0:T(8,128)(2,1)}, bf16[768,384]{1,0:T(8,128)(2,1)},...) custom-call(s32[2]{0:T(128)} %pad_add_fusion.refs_0_, ...), custom_call_target="tpu_custom_call" | custom-call | flops 8000000000 | bytes 1024 | tf_op jit(solution)/shard_map/project/pallas_call | solution.py:54
  52.4 13.0 %attend.1 = (bf16[512,768]{1,0:T(8,128)(2,1)}, bf16[512,384]{1,0:T(8,128)(2,1)}, bf16[6,128,2560]{2,1,0:T(8,128)(2,1)}) custom-call(s32[2]{0:T(128)} %pad_add_fusion.refs_0_, bf16[6,512,64]{2,1,0:T(8,128)(2,1)} %get-tuple-element.99.refs_1_.refs_9_, bf16[6,1024,64]{2,1,0:T(8,128)(2,1)} %get-tuple-element.100.refs_2_.refs_10_, ...), custom_call_target="tpu_custom_call" | custom-call | flops 16000000000 | bytes 1024 | tf_op jit(solution)/shard_map/attend/pallas_call | solution.py:54
  74.1 7.3 %mlp_pre.1 = (bf16[768,1536]{1,0:T(8,128)(2,1)}, bf16[768,1536]{1,0:T(8,128)(2,1)}, bf16[512,768]{1,0:T(8,128)(2,1)}, bf16[512,1536]{1,0:T(8,128)(2,1)}) custom-call(s32[2]{0:T(128)} %pad_add_fusion.refs_0_, s32[1,1024]{1,0:T(1,128)} %bitcast.49, bf16[1024,768]{1,0:T(8,128)(2,1)} %refs_2_.1, bf16[96,1536]{1,0:T(8,128)(2,1)} %copy-done.3, ...), custom_call_target="tpu_custom_call" | custom-call | bytes 1024 | tf_op jit(solution)/shard_map/mlp_pre/pallas_call | solution.py:54
  81.4 2.3 %collective-permute-done.8.refs_3_ = bf16[512,768]{1,0:T(8,128)(2,1)S(1)} collective-permute-done((bf16[512,768]{1,0:T(8,128)(2,1)}, bf16[512,768]{1,0:T(8,128)(2,1)S(1)}, u32[]{:S(2)}, u32[]{:S(2)}) %collective-permute-start.8) | collective-permute-done | bytes 786464 | tf_op jit(solution)/shard_map/ppermute | solution.py:34
  84.5 11.6 %mlp.1 = (bf16[512,768]{1,0:T(8,128)(2,1)}, bf16[512,1536]{1,0:T(8,128)(2,1)}, bf16[512,1536]{1,0:T(8,128)(2,1)}, bf16[512,768]{1,0:T(8,128)(2,1)}, f32[512,768]{1,0:T(8,128)}, /*index=5*/f32[512,256]{1,0:T(8,128)}) custom-call(s32[2]{0:T(128)} %pad_add_fusion.refs_0_, bf16[1024,768]{1,0:T(8,128)(2,1)} %refs_1_.7, ...), custom_call_target="tpu_custom_call" | custom-call | flops 10000000000 | bytes 1024 | tf_op jit(solution)/shard_map/mlp/pallas_call | solution.py:54
  97.6 9.7 %mlp_grad.1 = (bf16[512,768]{1,0:T(8,128)(2,1)}, bf16[8,96,1536]{2,1,0:T(8,128)(2,1)}, bf16[4,96,768]{2,1,0:T(8,128)(2,1)}, bf16[4,96,768]{2,1,0:T(8,128)(2,1)},...) custom-call(s32[2]{0:T(128)} %pad_add_fusion.refs_0_, ...), custom_call_target="tpu_custom_call" | custom-call | flops 8999999488 | bytes 1024 | tf_op jit(solution)/shard_map/mlp_grad/pallas_call | solution.py:54
  112.9 4.3 %scatter_first.2 = (f32[384,768]{1,0:T(8,128)}, bf16[384,768]{1,0:T(8,128)(2,1)}, f32[384,768]{1,0:T(8,128)}, bf16[384,768]{1,0:T(8,128)(2,1)}) custom-call(s32[2]{0:T(128)} %pad_add_fusion.refs_0_, bf16[8,96,1536]{2,1,0:T(8,128)(2,1)} %get-tuple-element.132.refs_1_, bf16[4,96,768]{2,1,0:T(8,128)(2,1)} %copy-done.4, bf16[4,96,768]{2,1,0:T(8,128)(2,1)} %copy-done.5, ...), custom_call_target="tpu_custom_call" | custom-call | bytes 1024 | tf_op jit(solution)/shard_map/scatter_first/pallas_call | solution.py:54
  119.5 17.9 %attend_back.1 = (f32[512,768]{1,0:T(8,128)}, bf16[512,768]{1,0:T(8,128)(2,1)}, f32[8,768]{1,0:T(8,128)}, bf16[512,384]{1,0:T(8,128)(2,1)}, f32[768,512]{1,0:T(8...) custom-call(s32[2]{0:T(128)} %pad_add_fusion.refs_0_, f32[512,768]{1,0:T(8,128)} %get-tuple-element.120.refs_1_.refs_2_, ...), custom_call_target="tpu_custom_call" | custom-call | flops 17999998976 | bytes 1024 | tf_op jit(solution)/shard_map/attend_back/pallas_call | solution.py:54
  139.2 2.9 %attn_grad.1.refs_5_.refs_4_ = f32[768,384]{1,0:T(8,128)} custom-call(s32[2]{0:T(128)} %pad_add_fusion.refs_0_, bf16[512,768]{1,0:T(8,128)(2,1)} %get-tuple-element.148.refs_1_, bf16[512,384]{1,0:T(8,128)(2,1)} %get-tuple-element.130.refs_8_.refs_2_, bf16[512,768]{1,0:T(8,128)(2,1)} %copy-done, bf16[384,768]{1,0:T(8,128)(2,1)} %copy-done.1, ...), custom_call_target="tpu_custom_call" | custom-call | bytes 1024 | tf_op jit(solution)/shard_map/attn_grad/pallas_call | solution.py:54
  142.1 3.2 %scatter_second.2 = (f32[192,768]{1,0:T(8,128)}, bf16[192,768]{1,0:T(8,128)(2,1)}, f32[192,768]{1,0:T(8,128)}, bf16[192,768]{1,0:T(8,128)(2,1)}) custom-call(s32[2]{0:T(128)} %pad_add_fusion.refs_0_, f32[384,768]{1,0:T(8,128)} %get-tuple-element.145.refs_1_, bf16[384,768]{1,0:T(8,128)(2,1)} %copy-done.1, f32[384,768]{1,0:T(8,128)} %get-tuple-element.146.refs_3_, ...), custom_call_target="tpu_custom_call" | custom-call | bytes 1024 | tf_op jit(solution)/shard_map/scatter_second/pallas_call | solution.py:54
  148.8 4.7 %first_grad.1 = (bf16[512,768]{1,0:T(8,128)(2,1)}, bf16[768,512]{1,0:T(8,128)(2,1)}) custom-call(s32[2]{0:T(128)} %pad_add_fusion.refs_0_, bf16[512,384]{1,0:T(8,128)(2,1)} %get-tuple-element.138.refs_1_.refs_2_, f32[768,512]{1,0:T(8,128)} %get-tuple-element.139.refs_2_, bf16[384,512]{1,0:T(8,128)(2,1)} %copy-done.11, bf16[384,512]{1,0:T(8,128)(2,1)} %copy-done.12, ...), custom_call_target="tpu_custom_call" | custom-call | bytes 1024 | tf_op jit(solution)/shard_map/first_grad/pallas_call | solution.py:54
  155.8 6.8 %qkv_grad.1 = (bf16[8,96,768]{2,1,0:T(8,128)(2,1)}, bf16[4,96,768]{2,1,0:T(8,128)(2,1)}, bf16[4,96,768]{2,1,0:T(8,128)(2,1)}, bf16[16,768]{1,0:T(8,128)(2,1)}, bf16[16,768]{1,0:T(8,128)(2,1)}) custom-call(s32[2]{0:T(128)} %pad_add_fusion.refs_0_, bf16[512,768]{1,0:T(8,128)(2,1)} %get-tuple-element.127.refs_1_, ...), custom_call_target="tpu_custom_call" | custom-call | flops 7000000000 | bytes 1024 | tf_op jit(solution)/shard_map/qkv_grad/pallas_call | solution.py:54
  163.2 2.4 %scatter_third.2 = (f32[96,1536]{1,0:T(8,128)}, bf16[96,1536]{1,0:T(8,128)(2,1)}) custom-call(s32[2]{0:T(128)} %pad_add_fusion.refs_0_, f32[192,768]{1,0:T(8,128)} %get-tuple-element.149.refs_8_.refs_1_, bf16[192,768]{1,0:T(8,128)(2,1)} %copy-done.20, f32[192,768]{1,0:T(8,128)} %get-tuple-element.161.refs_3_, bf16[192,768]{1,0:T(8,128)(2,1)} %copy-done.22, ...), custom_call_target="tpu_custom_call" | custom-call | bytes 1024 | tf_op jit(solution)/shard_map/scatter_third/pallas_call | solution.py:54
  165.6 2.3 %collective-permute-start.43 = (bf16[96,1536]{1,0:T(8,128)(2,1)}, bf16[96,1536]{1,0:T(8,128)(2,1)S(1)}, u32[]{:S(2)}, u32[]{:S(2)}) collective-permute-start(bf16[96,1536]{1,0:T(8,128)(2,1)} %get-tuple-element.168), channel_id=1, source_target_pairs={{0,16},{4,20},{8,24},{12,28},{16,0},{20,4},{24,8},{28,12},{1,17},{... | collective-permute-start | bytes 884744 | tf_op jit(solution)/shard_map/ppermute | solution.py:38
  168.9 3.0 %scatter_first.3 = (f32[400,384]{1,0:T(8,128)}, bf16[400,384]{1,0:T(8,128)(2,1)}, f32[400,384]{1,0:T(8,128)}, bf16[400,384]{1,0:T(8,128)(2,1)}) custom-call(s32[2]{0:T(128)} %pad_add_fusion.refs_0_, bf16[8,96,768]{2,1,0:T(8,128)(2,1)} %get-tuple-element.156.refs_5_.refs_1_, bf16[4,96,768]{2,1,0:T(8,128)(2,1)} %copy-done.8, bf16[4,96,768]{2,1,0:T(8,128)(2,1)} %copy-done.9, ...), custom_call_target="tpu_custom_call" | custom-call | bytes 1024 | tf_op jit(solution)/shard_map/scatter_first/pallas_call | solution.py:54
  175.0 3.6 %output.1.refs_7_.refs_1_ = bf16[512,768]{1,0:T(8,128)(2,1)} custom-call(s32[2]{0:T(128)} %pad_add_fusion.refs_0_, s32[1,1024]{1,0:T(1,128)} %bitcast.50, f32[512,768]{1,0:T(8,128)} %get-tuple-element.120.refs_1_.refs_2_, bf16[512,768]{1,0:T(8,128)(2,1)} %get-tuple-element.126.refs_3_, bf16[512,768]{1,0:T(8,128)(2,1)} %copy-done, ...), custom_call_target="tpu_custom_call" | custom-call | bytes 1024 | tf_op jit(solution)/shard_map/output/pallas_call | solution.py:54
  179.5 4.9 %final.1.refs_5_.refs_1_ = bf16[512,768]{1,0:T(8,128)(2,1)} custom-call(s32[2]{0:T(128)} %pad_add_fusion.refs_0_, bf16[1024,768]{1,0:T(8,128)(2,1)} %refs_1_.7, f32[1024,256]{1,0:T(8,128)} %stats.1.refs_2_.refs_7_, bf16[512,768]{1,0:T(8,128)(2,1)} %get-tuple-element.151.refs_5_.refs_3_, bf16[512,768]{1,0:T(8,128)(2,1)} %copy-done.36, ...), custom_call_target="tpu_custom_call" | custom-call | flops 5000000000 | bytes 1024 | tf_op jit(solution)/shard_map/final/pallas_call | solution.py:54
  185.6 2.2 scatter_big.1
  189.0 2.4 %scatter_second.3 = (f32[208,384]{1,0:T(8,128)}, bf16[208,384]{1,0:T(8,128)(2,1)}, f32[208,384]{1,0:T(8,128)}, bf16[208,384]{1,0:T(8,128)(2,1)}) custom-call(s32[2]{0:T(128)} %pad_add_fusion.refs_0_, f32[400,384]{1,0:T(8,128)} %get-tuple-element.164.refs_1_, bf16[400,384]{1,0:T(8,128)(2,1)} %copy-done.40, f32[400,384]{1,0:T(8,128)} %get-tuple-element.165.refs_3_, ...), custom_call_target="tpu_custom_call" | custom-call | flops 2000000000 | bytes 1024 | tf_op jit(solution)/shard_map/scatter_second/pallas_call | solution.py:54
  192.9 2.6 %merge.2.refs_5_ = bf16[1024,768]{1,0:T(8,128)(2,1)} custom-call(s32[2]{0:T(128)} %pad_add_fusion.refs_0_, bf16[512,768]{1,0:T(8,128)(2,1)} %output.1.refs_7_.refs_1_, bf16[512,768]{1,0:T(8,128)(2,1)} %copy-done.39, bf16[208,384]{1,0:T(8,128)(2,1)} %get-tuple-element.169.refs_3_), custom_call_target="tpu_custom_call" | custom-call | flops 3000000000 | bytes 1024 | tf_op jit(solution)/shard_map/merge/pallas_call | solution.py:54
  198.1 2.0 scatter_third.3
  200.1 2.0 collective-permute-start.47
  203.0 2.6 %merge.3.refs_4_ = bf16[1024,768]{1,0:T(8,128)(2,1)} custom-call(s32[2]{0:T(128)} %pad_add_fusion.refs_0_, bf16[512,768]{1,0:T(8,128)(2,1)} %final.1.refs_5_.refs_1_, bf16[512,768]{1,0:T(8,128)(2,1)} %copy-done.38, f32[112,768]{1,0:T(8,128)} %get-tuple-element.173.refs_3_.refs_1_), custom_call_target="tpu_custom_call" | custom-call | flops 3000000000 | bytes 1024 | tf_op jit(solution)/shard_map/merge/pallas_call | solution.py:54
  205.6 4.4 %collective-permute-done.47.refs_2_ = bf16[112,768]{1,0:T(8,128)(2,1)S(1)} collective-permute-done((bf16[112,768]{1,0:T(8,128)(2,1)}, bf16[112,768]{1,0:T(8,128)(2,1)S(1)}, u32[]{:S(2)}, u32[]{:S(2)}) %collective-permute-start.47) | collective-permute-done | bytes 172064 | tf_op jit(solution)/shard_map/ppermute | solution.py:38
  210.7 1.9 scatter_small.1
  214.9 2.4 %collective-permute-done.48 = bf16[16,768]{1,0:T(8,128)(2,1)S(1)} collective-permute-done((bf16[16,768]{1,0:T(8,128)(2,1)S(1)}, bf16[16,768]{1,0:T(8,128)(2,1)S(1)}, u32[]{:S(2)}, u32[]{:S(2)}) %collective-permute-start.48) | collective-permute-done | bytes 24608 | tf_op jit(solution)/shard_map/ppermute | solution.py:34
  (212 shorter events, 65.9 us)
Async XLA Ops:
  4.8 12.4 %collective-permute-start.2 = (bf16[112,768]{1,0:T(8,128)(2,1)S(1)}, bf16[112,768]{1,0:T(8,128)(2,1)S(1)}, u32[]{:S(2)}, u32[]{:S(2)}) collective-permute-start(bf16[112,768]{1,0:T(8,128)(2,1)S(1)} %get-tuple-element.223), channel_id=1, source_target_pairs={{0,16},{4,20},{8,24},{12,28},{16,0},{20,4},{24,8},{28,12},{1,17},{... | collective-permute-start | bytes 516104 | tf_op jit(solution)/shard_map/ppermute | solution.py:38
  9.0 8.3 %collective-permute-start.1 = (bf16[112,768]{1,0:T(8,128)(2,1)S(1)}, bf16[112,768]{1,0:T(8,128)(2,1)S(1)}, u32[]{:S(2)}, u32[]{:S(2)}) collective-permute-start(bf16[112,768]{1,0:T(8,128)(2,1)S(1)} %get-tuple-element.223), channel_id=1, source_target_pairs={{0,8},{4,12},{8,0},{12,4},{16,24},{20,28},{24,16},{28,20},{1,9},{5... | collective-permute-start | bytes 516104 | tf_op jit(solution)/shard_map/ppermute | solution.py:38
  10.7 11.8 %collective-permute-start = (bf16[112,768]{1,0:T(8,128)(2,1)S(1)}, bf16[112,768]{1,0:T(8,128)(2,1)S(1)}, u32[]{:S(2)}, u32[]{:S(2)}) collective-permute-start(bf16[112,768]{1,0:T(8,128)(2,1)S(1)} %get-tuple-element.223), channel_id=1, source_target_pairs={{0,4},{4,0},{8,12},{12,8},{16,20},{20,16},{24,28},{28,24},{1,5},{5... | collective-permute-start | bytes 516104 | tf_op jit(solution)/shard_map/ppermute | solution.py:38
  17.3 12.8 %collective-permute-start.4 = (bf16[112,768]{1,0:T(8,128)(2,1)S(1)}, bf16[112,768]{1,0:T(8,128)(2,1)S(1)}, u32[]{:S(2)}, u32[]{:S(2)}) collective-permute-start(bf16[112,768]{1,0:T(8,128)(2,1)S(1)} %collective-permute-done.2), channel_id=1, source_target_pairs={{0,4},{4,0},{8,12},{12,8},{16,20},{20,16},{24,28},{28,24},{1,5},{5... | collective-permute-start | bytes 516104 | tf_op jit(solution)/shard_map/ppermute | solution.py:38
  19.0 11.1 %collective-permute-start.5 = (bf16[112,768]{1,0:T(8,128)(2,1)S(1)}, bf16[112,768]{1,0:T(8,128)(2,1)S(1)}, u32[]{:S(2)}, u32[]{:S(2)}) collective-permute-start(bf16[112,768]{1,0:T(8,128)(2,1)S(1)} %collective-permute-done.2), channel_id=1, source_target_pairs={{0,8},{4,12},{8,0},{12,4},{16,24},{20,28},{24,16},{28,20},{1,9},{5... | collective-permute-start | bytes 516104 | tf_op jit(solution)/shard_map/ppermute | solution.py:38
  20.5 9.7 %collective-permute-start.6 = (bf16[112,768]{1,0:T(8,128)(2,1)S(1)}, bf16[112,768]{1,0:T(8,128)(2,1)S(1)}, u32[]{:S(2)}, u32[]{:S(2)}) collective-permute-start(bf16[112,768]{1,0:T(8,128)(2,1)S(1)} %collective-permute-done.2), channel_id=1, source_target_pairs={{0,12},{4,8},{8,4},{12,0},{16,28},{20,24},{24,20},{28,16},{1,13},{... | collective-permute-start | bytes 516104 | tf_op jit(solution)/shard_map/ppermute | solution.py:38
  20.8 9.3 %collective-permute-start.3 = (bf16[112,768]{1,0:T(8,128)(2,1)S(1)}, bf16[112,768]{1,0:T(8,128)(2,1)S(1)}, u32[]{:S(2)}, u32[]{:S(2)}) collective-permute-start(bf16[112,768]{1,0:T(8,128)(2,1)S(1)} %collective-permute-done.1), channel_id=1, source_target_pairs={{0,4},{4,0},{8,12},{12,8},{16,20},{20,16},{24,28},{28,24},{1,5},{5... | collective-permute-start | bytes 516104 | tf_op jit(solution)/shard_map/ppermute | solution.py:38
  30.2 6.6 %collective-permute-start.7 = (bf16[8,112,768]{2,1,0:T(8,128)(2,1)S(1)}, bf16[8,112,768]{2,1,0:T(8,128)(2,1)S(1)}, u32[]{:S(2)}, u32[]{:S(2)}) collective-permute-start(bf16[8,112,768]{2,1,0:T(8,128)(2,1)S(1)} %bitcast_dynamic-update-slice_fusion.refs_3_), channel_id=1, source_target_pairs={{0,1},{1,0},{2,3},{3,2},{4,5},{5,4},{6,7},{7,6},{8,9},{9,8},{10,11... | collective-permute-start | bytes 4128776 | tf_op jit(solution)/shard_map/ppermute | solution.py:30
  30.3 16.8 %collective-permute-start.11 = (bf16[96,1536]{1,0:T(8,128)(2,1)S(1)}, bf16[96,1536]{1,0:T(8,128)(2,1)S(1)}, u32[]{:S(2)}, u32[]{:S(2)}) collective-permute-start(bf16[96,1536]{1,0:T(8,128)(2,1)S(1)} %pad_maximum_fusion.refs_3_), channel_id=1, source_target_pairs={{0,16},{4,20},{8,24},{12,28},{16,0},{20,4},{24,8},{28,12},{1,17},{... | collective-permute-start | bytes 884744 | tf_op jit(solution)/shard_map/ppermute | solution.py:38
  32.6 14.6 %collective-permute-start.10 = (bf16[96,1536]{1,0:T(8,128)(2,1)S(1)}, bf16[96,1536]{1,0:T(8,128)(2,1)S(1)}, u32[]{:S(2)}, u32[]{:S(2)}) collective-permute-start(bf16[96,1536]{1,0:T(8,128)(2,1)S(1)} %pad_maximum_fusion.refs_3_), channel_id=1, source_target_pairs={{0,8},{4,12},{8,0},{12,4},{16,24},{20,28},{24,16},{28,20},{1,9},{5... | collective-permute-start | bytes 884744 | tf_op jit(solution)/shard_map/ppermute | solution.py:38
  35.2 30.2 %collective-permute-start.9 = (bf16[96,1536]{1,0:T(8,128)(2,1)S(1)}, bf16[96,1536]{1,0:T(8,128)(2,1)S(1)}, u32[]{:S(2)}, u32[]{:S(2)}) collective-permute-start(bf16[96,1536]{1,0:T(8,128)(2,1)S(1)} %pad_maximum_fusion.refs_3_), channel_id=1, source_target_pairs={{0,4},{4,0},{8,12},{12,8},{16,20},{20,16},{24,28},{28,24},{1,5},{5... | collective-permute-start | bytes 884744 | tf_op jit(solution)/shard_map/ppermute | solution.py:38
  47.2 21.2 %collective-permute-start.13 = (bf16[96,1536]{1,0:T(8,128)(2,1)S(1)}, bf16[96,1536]{1,0:T(8,128)(2,1)S(1)}, u32[]{:S(2)}, u32[]{:S(2)}) collective-permute-start(bf16[96,1536]{1,0:T(8,128)(2,1)S(1)} %collective-permute-done.11.refs_7_), channel_id=1, source_target_pairs={{0,4},{4,0},{8,12},{12,8},{16,20},{20,16},{24,28},{28,24},{1,5},{5... | collective-permute-start | bytes 884744 | tf_op jit(solution)/shard_map/ppermute | solution.py:38
  48.9 19.5 %collective-permute-start.14 = (bf16[96,1536]{1,0:T(8,128)(2,1)S(1)}, bf16[96,1536]{1,0:T(8,128)(2,1)S(1)}, u32[]{:S(2)}, u32[]{:S(2)}) collective-permute-start(bf16[96,1536]{1,0:T(8,128)(2,1)S(1)} %collective-permute-done.11.refs_7_), channel_id=1, source_target_pairs={{0,8},{4,12},{8,0},{12,4},{16,24},{20,28},{24,16},{28,20},{1,9},{5... | collective-permute-start | bytes 884744 | tf_op jit(solution)/shard_map/ppermute | solution.py:38
  49.8 18.6 %collective-permute-start.15 = (bf16[96,1536]{1,0:T(8,128)(2,1)S(1)}, bf16[96,1536]{1,0:T(8,128)(2,1)S(1)}, u32[]{:S(2)}, u32[]{:S(2)}) collective-permute-start(bf16[96,1536]{1,0:T(8,128)(2,1)S(1)} %collective-permute-done.11.refs_7_), channel_id=1, source_target_pairs={{0,12},{4,8},{8,4},{12,0},{16,28},{20,24},{24,20},{28,16},{1,13},{... | collective-permute-start | bytes 884744 | tf_op jit(solution)/shard_map/ppermute | solution.py:38
  50.7 17.7 %collective-permute-start.12 = (bf16[96,1536]{1,0:T(8,128)(2,1)S(1)}, bf16[96,1536]{1,0:T(8,128)(2,1)S(1)}, u32[]{:S(2)}, u32[]{:S(2)}) collective-permute-start(bf16[96,1536]{1,0:T(8,128)(2,1)S(1)} %collective-permute-done.10.refs_5_), channel_id=1, source_target_pairs={{0,4},{4,0},{8,12},{12,8},{16,20},{20,16},{24,28},{28,24},{1,5},{5... | collective-permute-start | bytes 884744 | tf_op jit(solution)/shard_map/ppermute | solution.py:38
  65.4 18.2 %collective-permute-start.8 = (bf16[512,768]{1,0:T(8,128)(2,1)}, bf16[512,768]{1,0:T(8,128)(2,1)S(1)}, u32[]{:S(2)}, u32[]{:S(2)}) collective-permute-start(bf16[512,768]{1,0:T(8,128)(2,1)} %get-tuple-element.103.refs_2_), channel_id=1, source_target_pairs={{0,2},{2,0},{1,3},{3,1},{4,6},{6,4},{5,7},{7,5},{8,10},{10,8},{9,1... | collective-permute-start | bytes 2359304 | tf_op jit(solution)/shard_map/ppermute | solution.py:34
  96.1 22.5 %collective-permute-start.25 = (bf16[512,768]{1,0:T(8,128)(2,1)}, bf16[512,768]{1,0:T(8,128)(2,1)S(1)}, u32[]{:S(2)}, u32[]{:S(2)}) collective-permute-start(bf16[512,768]{1,0:T(8,128)(2,1)} %get-tuple-element.129.refs_4_), channel_id=1, source_target_pairs={{0,2},{2,0},{1,3},{3,1},{4,6},{6,4},{5,7},{7,5},{8,10},{10,8},{9,1... | collective-permute-start | bytes 2359304 | tf_op jit(solution)/shard_map/ppermute | solution.py:34
  109.5 28.4 %collective-permute-start.24 = (bf16[512,768]{1,0:T(8,128)(2,1)}, bf16[512,768]{1,0:T(8,128)(2,1)S(1)}, u32[]{:S(2)}, u32[]{:S(2)}) collective-permute-start(bf16[512,768]{1,0:T(8,128)(2,1)} %get-tuple-element.126.refs_3_), channel_id=1, source_target_pairs={{0,2},{2,0},{1,3},{3,1},{4,6},{6,4},{5,7},{7,5},{8,10},{10,8},{9,1... | collective-permute-start | bytes 2359304 | tf_op jit(solution)/shard_map/ppermute | solution.py:34
  117.2 20.8 %collective-permute-start.32 = (bf16[384,768]{1,0:T(8,128)(2,1)}, bf16[384,768]{1,0:T(8,128)(2,1)S(1)}, u32[]{:S(2)}, u32[]{:S(2)}) collective-permute-start(bf16[384,768]{1,0:T(8,128)(2,1)} %get-tuple-element.137.refs_13_), channel_id=1, source_target_pairs={{0,4},{4,0},{8,12},{12,8},{16,20},{20,16},{24,28},{28,24},{1,5},{5... | collective-permute-start | bytes 1769480 | tf_op jit(solution)/shard_map/ppermute | solution.py:38
  117.5 20.5 %collective-permute-start.33 = (bf16[384,768]{1,0:T(8,128)(2,1)}, bf16[384,768]{1,0:T(8,128)(2,1)S(1)}, u32[]{:S(2)}, u32[]{:S(2)}) collective-permute-start(bf16[384,768]{1,0:T(8,128)(2,1)} %get-tuple-element.147), channel_id=1, source_target_pairs={{0,8},{4,12},{8,0},{12,4},{16,24},{20,28},{24,16},{28,20},{1,9},{5... | collective-permute-start | bytes 1769480 | tf_op jit(solution)/shard_map/ppermute | solution.py:38
  137.4 10.4 %collective-permute-start.30 = (bf16[384,512]{1,0:T(8,128)(2,1)}, bf16[384,512]{1,0:T(8,128)(2,1)S(1)}, u32[]{:S(2)}, u32[]{:S(2)}) collective-permute-start(bf16[384,512]{1,0:T(8,128)(2,1)} %get-tuple-element.140), channel_id=1, source_target_pairs={{0,1},{1,0},{2,3},{3,2},{4,5},{5,4},{6,7},{7,6},{8,9},{9,8},{10,11... | collective-permute-start | bytes 1179656 | tf_op jit(solution)/shard_map/ppermute | solution.py:30
  137.4 10.4 %collective-permute-start.31 = (bf16[384,512]{1,0:T(8,128)(2,1)}, bf16[384,512]{1,0:T(8,128)(2,1)S(1)}, u32[]{:S(2)}, u32[]{:S(2)}) collective-permute-start(bf16[384,512]{1,0:T(8,128)(2,1)} %get-tuple-element.141), channel_id=1, source_target_pairs={{0,1},{1,0},{2,3},{3,2},{4,5},{5,4},{6,7},{7,6},{8,9},{9,8},{10,11... | collective-permute-start | bytes 1179656 | tf_op jit(solution)/shard_map/ppermute | solution.py:30
  145.3 9.2 %collective-permute-start.34 = (bf16[192,768]{1,0:T(8,128)(2,1)}, bf16[192,768]{1,0:T(8,128)(2,1)S(1)}, u32[]{:S(2)}, u32[]{:S(2)}) collective-permute-start(bf16[192,768]{1,0:T(8,128)(2,1)} %get-tuple-element.154), channel_id=1, source_target_pairs={{0,8},{4,12},{8,0},{12,4},{16,24},{20,28},{24,16},{28,20},{1,9},{5... | collective-permute-start | bytes 884744 | tf_op jit(solution)/shard_map/ppermute | solution.py:38
  146.2 8.9 %collective-permute-start.35 = (bf16[192,768]{1,0:T(8,128)(2,1)}, bf16[192,768]{1,0:T(8,128)(2,1)S(1)}, u32[]{:S(2)}, u32[]{:S(2)}) collective-permute-start(bf16[192,768]{1,0:T(8,128)(2,1)} %get-tuple-element.155), channel_id=1, source_target_pairs={{0,4},{4,0},{8,12},{12,8},{16,20},{20,16},{24,28},{28,24},{1,5},{5... | collective-permute-start | bytes 884744 | tf_op jit(solution)/shard_map/ppermute | solution.py:38
  153.4 25.2 %collective-permute-start.42 = (bf16[512,768]{1,0:T(8,128)(2,1)}, bf16[512,768]{1,0:T(8,128)(2,1)S(1)}, u32[]{:S(2)}, u32[]{:S(2)}) collective-permute-start(bf16[512,768]{1,0:T(8,128)(2,1)} %get-tuple-element.151.refs_5_.refs_3_), channel_id=1, source_target_pairs={{0,2},{2,0},{1,3},{3,1},{4,6},{6,4},{5,7},{7,5},{8,10},{10,8},{9,1... | collective-permute-start | bytes 2359304 | tf_op jit(solution)/shard_map/ppermute | solution.py:34
  165.6 19.3 %collective-permute-start.43 = (bf16[96,1536]{1,0:T(8,128)(2,1)}, bf16[96,1536]{1,0:T(8,128)(2,1)S(1)}, u32[]{:S(2)}, u32[]{:S(2)}) collective-permute-start(bf16[96,1536]{1,0:T(8,128)(2,1)} %get-tuple-element.168), channel_id=1, source_target_pairs={{0,16},{4,20},{8,24},{12,28},{16,0},{20,4},{24,8},{28,12},{1,17},{... | collective-permute-start | bytes 884744 | tf_op jit(solution)/shard_map/ppermute | solution.py:38
  171.9 15.9 %collective-permute-start.40 = (bf16[400,384]{1,0:T(8,128)(2,1)}, bf16[400,384]{1,0:T(8,128)(2,1)S(1)}, u32[]{:S(2)}, u32[]{:S(2)}) collective-permute-start(bf16[400,384]{1,0:T(8,128)(2,1)} %get-tuple-element.163.refs_6_), channel_id=1, source_target_pairs={{0,4},{4,0},{8,12},{12,8},{16,20},{20,16},{24,28},{28,24},{1,5},{5... | collective-permute-start | bytes 921608 | tf_op jit(solution)/shard_map/ppermute | solution.py:38
  173.5 14.8 %collective-permute-start.41 = (bf16[400,384]{1,0:T(8,128)(2,1)}, bf16[400,384]{1,0:T(8,128)(2,1)S(1)}, u32[]{:S(2)}, u32[]{:S(2)}) collective-permute-start(bf16[400,384]{1,0:T(8,128)(2,1)} %get-tuple-element.166), channel_id=1, source_target_pairs={{0,8},{4,12},{8,0},{12,4},{16,24},{20,28},{24,16},{28,20},{1,9},{5... | collective-permute-start | bytes 921608 | tf_op jit(solution)/shard_map/ppermute | solution.py:38
  178.6 13.5 %collective-permute-start.39 = (bf16[512,768]{1,0:T(8,128)(2,1)}, bf16[512,768]{1,0:T(8,128)(2,1)S(1)}, u32[]{:S(2)}, u32[]{:S(2)}) collective-permute-start(bf16[512,768]{1,0:T(8,128)(2,1)} %output.1.refs_7_.refs_1_), channel_id=1, source_target_pairs={{0,1},{1,0},{2,3},{3,2},{4,5},{5,4},{6,7},{7,6},{8,9},{9,8},{10,11... | collective-permute-start | bytes 2359304 | tf_op jit(solution)/shard_map/ppermute | solution.py:30
  184.4 17.7 %collective-permute-start.44 = (bf16[512,768]{1,0:T(8,128)(2,1)}, bf16[512,768]{1,0:T(8,128)(2,1)S(1)}, u32[]{:S(2)}, u32[]{:S(2)}) collective-permute-start(bf16[512,768]{1,0:T(8,128)(2,1)} %final.1.refs_5_.refs_1_), channel_id=1, source_target_pairs={{0,1},{1,0},{2,3},{3,2},{4,5},{5,4},{6,7},{7,6},{8,9},{9,8},{10,11... | collective-permute-start | bytes 2359304 | tf_op jit(solution)/shard_map/ppermute | solution.py:30
  191.5 6.0 %collective-permute-start.46 = (bf16[208,384]{1,0:T(8,128)(2,1)}, bf16[208,384]{1,0:T(8,128)(2,1)S(1)}, u32[]{:S(2)}, u32[]{:S(2)}) collective-permute-start(bf16[208,384]{1,0:T(8,128)(2,1)} %get-tuple-element.172), channel_id=1, source_target_pairs={{0,4},{4,0},{8,12},{12,8},{16,20},{20,16},{24,28},{28,24},{1,5},{5... | collective-permute-start | bytes 479240 | tf_op jit(solution)/shard_map/ppermute | solution.py:38
  200.1 9.9 %collective-permute-start.47 = (bf16[112,768]{1,0:T(8,128)(2,1)}, bf16[112,768]{1,0:T(8,128)(2,1)S(1)}, u32[]{:S(2)}, u32[]{:S(2)}) collective-permute-start(bf16[112,768]{1,0:T(8,128)(2,1)} %get-tuple-element.174), channel_id=1, source_target_pairs={{0,16},{4,20},{8,24},{12,28},{16,0},{20,4},{24,8},{28,12},{1,17},{... | collective-permute-start | bytes 516104 | tf_op jit(solution)/shard_map/ppermute | solution.py:38
  (63 other events, 235.5 us)

commit v4 on v3

--- a/solution.py
+++ b/solution.py
@@ -335,23 +335,21 @@
     sib_c_ref,
     sib_d_ref,
     sums_ref,
-    acc_ref,
 ):
-    flip = info[0]
     sib_refs = ((sib_a_ref, sib_b_ref), (sib_c_ref, sib_d_ref))
+    base, units = own_ref.shape[1], own_ref.shape[2] // 2
+    half = units // 2
     part_ref[...] = dot(act_ref[...], proj_ref[...], 1, 1).astype(BF)
-    base = own_ref.shape[1]
-    units = own_ref.shape[2] // 2
     for kind, left, right in ((0, second_ref, dhid_ref), (1, dy_ref, act_ref)):
         for side in range(2):
-            acc_ref[...] = dot(left[...], right[:, side * units : (side + 1) * units], 0, 0)
-            for r in range(CHUNKS):
-                at = pl.multiple_of((r ^ flip) * base, 32)
-                block = acc_ref[pl.ds(at, base), :].astype(BF)
+            value = dot(left[...], right[:, side * units : (side + 1) * units], 0, 0).astype(BF)
+            for b in range(CHUNKS):
+                block = value[b * base : (b + 1) * base, :]
                 if side:
-                    sib_refs[kind][r // 4][r % 4] = block
+                    sib_refs[kind][0][b] = block[:, :half]
+                    sib_refs[kind][1][b] = block[:, half:]
                 else:
-                    own_ref[r, :, kind * units : (kind + 1) * units] = block
+                    own_ref[b, :, kind * units : (kind + 1) * units] = block
     one = jnp.ones((8, act_ref.shape[0]), BF)
     fc_sums = dot(one, dhid_ref[...], 1, 0)
     sums_ref[0:8, :] = fc_sums[:, 0:units]
@@ -446,7 +444,7 @@
                 dvt_ref[h, :, 0:end] += dv
         return carry
 
-    lax.fori_loop(0, heads, head, 0, unroll=2)
+    lax.fori_loop(0, heads, head, 0, unroll=3)
     width2 = heads * HD
     for h in range(heads):
         dq_ref[:, h * HD : (h + 1) * HD] = dqh_ref[h].astype(BF)
@@ -461,10 +459,6 @@
                 send[twin * HD : (twin + 1) * HD, cols] = ref[h, :, pl.ds(yours, TILE)].astype(BF)
 
 
-def attn_grad_kernel(info, branch_ref, mixed_ref, out_ref):
-    out_ref[...] = dot(branch_ref[...], mixed_ref[...], 0, 0)
-
-
 def first_grad_kernel(
     info, dq_ref, keep_ref, got_k_ref, got_v_ref, wq_ref, wk_ref, wv_ref, part_ref, dkv_ref
 ):
@@ -484,7 +478,8 @@
     first_ref,
     dq_ref,
     dkv_ref,
-    attn_ref,
+    branch_ref,
+    mixed_ref,
     part_ref,
     x_ref,
     stat_ref,
@@ -495,10 +490,9 @@
     sib_b_ref,
     tile_own_ref,
     tile_sib_ref,
-    whole_ref,
     sum_ref,
 ):
-    flip, core = info[0], info[1]
+    core = info[1]
     width2 = dq_ref.shape[1]
     width = width2 // 2
     base = own_ref.shape[1]
@@ -506,18 +500,18 @@
         if part == 0:
             whole = dot(first_ref[...], dq_ref[...], 0, 0)
         elif part == 3:
-            whole = attn_ref[...]
+            whole = dot(branch_ref[...], mixed_ref[...], 0, 0)
         else:
             whole = dot(
                 first_ref[...], dkv_ref[(part - 1) * width2 : part * width2, :], 0, 1
             )
-        whole_ref[...] = whole
+        whole = whole.astype(BF)
         cols = slice(part * width, (part + 1) * width)
-        for r in range(CHUNKS):
-            at = pl.multiple_of((r ^ flip) * base, 32)
-            block = whole_ref[pl.ds(at, base), :].astype(BF)
-            own_ref[r, :, cols] = block[:, 0:width]
-            (sib_a_ref, sib_b_ref)[r // 4][r % 4, :, cols] = block[:, width:width2]
+        side_cols = slice(part % 2 * width, (part % 2 + 1) * width)
+        for b in range(CHUNKS):
+            block = whole[b * base : (b + 1) * base, :]
+            own_ref[b, :, cols] = block[:, 0:width]
+            (sib_a_ref, sib_b_ref)[part // 2][b, :, side_cols] = block[:, width:width2]
     sum_ref[...] = jnp.zeros_like(sum_ref)
 
     def run(at):
@@ -542,88 +536,100 @@
         out[...] = sum_ref[...].astype(BF)
 
 
-def final_kernel(info, x_ref, stat_ref, part_ref, recv_ref, dmid_ref, vec_ref, out_ref):
+def final_kernel(
+    info,
+    x_ref,
+    stat_ref,
+    part_ref,
+    recv_ref,
+    dmid_ref,
+    vec_ref,
+    seg_ref,
+    mid_ref,
+    mlp_ref,
+    mlp_got_ref,
+    out_ref,
+):
     core = info[1]
-    gain = vec_ref[0:1, :]
-
-    def run(at):
-        src = own_start(at, core)
-        rs = pl.ds(at, 32)
-        factor = stat_ref[pl.ds(src, 32), TILE : TILE + 1]
-        scaled = (x_ref[pl.ds(src, 32), :].astype(F32) - stat_ref[pl.ds(src, 32), 0:1]) * factor
-        incoming = part_ref[rs, :].astype(F32) + recv_ref[rs, :].astype(F32)
-        out_ref[rs, :] = (
-            dmid_ref[rs, :] + norm_backward(incoming, scaled, factor, gain)
-        ).astype(BF)
-
-    loop(part_ref.shape[0], 32, run)
-
-
-def output_kernel(info, seg_ref, mid_ref, part_ref, recv_ref, vec_ref, out_ref):
-    core = info[1]
-    bias = vec_ref[6:7, :]
+    own_count = part_ref.shape[0]
+    gain, bias = vec_ref[0:1, :], vec_ref[6:7, :]
     sub = 32
     lane = lax.broadcasted_iota(jnp.int32, (sub, TILE), 1)
     line = lax.broadcasted_iota(jnp.int32, (sub, TILE), 0)
 
     def run(at):
+        src = own_start(at, core)
+        rs = pl.ds(at, sub)
+        factor = stat_ref[pl.ds(src, sub), TILE : TILE + 1]
+        scaled = (x_ref[pl.ds(src, sub), :].astype(F32) - stat_ref[pl.ds(src, sub), 0:1]) * factor
+        incoming = part_ref[rs, :].astype(F32) + recv_ref[rs, :].astype(F32)
+        out_ref[pl.ds(own_count + at, sub), :] = (
+            dmid_ref[rs, :] + norm_backward(incoming, scaled, factor, gain)
+        ).astype(BF)
         tile_at = pl.multiple_of((2 * (at // TILE) + core) * TILE, TILE)
         seg_tile = jnp.broadcast_to(seg_ref[0:1, pl.ds(tile_at, TILE)], (sub, TILE))
         seg_col = jnp.max(
             jnp.where(lane == line + at % TILE, seg_tile, -2), -1, keepdims=True
         )
-        rs = pl.ds(at, sub)
         final = (
             mid_ref[rs, :]
-            + (part_ref[rs, :].astype(F32) + recv_ref[rs, :].astype(F32))
+            + (mlp_ref[rs, :].astype(F32) + mlp_got_ref[rs, :].astype(F32))
             + bias
         )
         out_ref[rs, :] = jnp.where(seg_col >= 0, final, 0.0).astype(BF)
 
-    loop(part_ref.shape[0], sub, run)
-
-
-def merge_kernel(info, own_ref, got_ref, out_ref):
+    loop(own_count, sub, run)
+
+
+def merge_kernel(info, own_ref, got_ref, first_ref, second_ref):
     core = info[1]
-    for j in range(own_ref.shape[0] // TILE):
-        sl = slice(j * TILE, (j + 1) * TILE)
+    count = first_ref.shape[0] // (2 * TILE)
+    for i in range(2 * count):
+        out, j = (first_ref, second_ref)[i // count], i % count
+        sl = slice(i * TILE, (i + 1) * TILE)
         mine = pl.multiple_of((2 * j + core) * TILE, TILE)
         yours = pl.multiple_of((2 * j + 1 - core) * TILE, TILE)
-        out_ref[pl.ds(mine, TILE), :] = own_ref[sl, :]
-        out_ref[pl.ds(yours, TILE), :] = got_ref[sl, :]
+        out[pl.ds(mine, TILE), :] = own_ref[sl, :]
+        out[pl.ds(yours, TILE), :] = got_ref[sl, :]
 
 
 def all_rows(info, own, after=()):
     return call(
         merge_kernel,
-        [shape((2 * own.shape[0], own.shape[1]))],
+        [shape(own.shape)] * 2,
         info,
         own,
         swap_core(own),
         name="merge",
-        cost=3,
+        cost=4,
         after=after,
-    )[0]
+    )
 
 
 def scatter_first_kernel(pieces, info, own_ref, *refs):
     got_refs, refs = refs[:pieces], refs[pieces:]
     tiles, (keep_a, send_a, keep_b, send_b) = refs[:-4], refs[-4:]
+    flip = info[0]
     base = own_ref.shape[1]
     half = own_ref.shape[2] // 2
+    span = own_ref.shape[2] // pieces
     for side, keep, send in ((0, keep_a, send_a), (1, keep_b, send_b)):
         cols = slice(side * half, (side + 1) * half)
-        got_cols = cols if pieces == 2 else slice(0, half)
         kept, sent = 0, 0
         for r in range(CHUNKS):
-            got = got_refs[r // 4 if pieces == 2 else 2 * side + r // 4]
-            value = own_ref[r, :, cols].astype(F32) + got[r % 4, :, got_cols].astype(F32)
-            if (r >> side) & 1:
-                send[sent * base : (sent + 1) * base, :] = value.astype(BF)
-                sent += 1
-            else:
-                keep[kept * base : (kept + 1) * base, :] = value
-                kept += 1
+            rows = slice(sent * base, (sent + 1) * base)
+            if not (r >> side) & 1:
+                rows = slice(kept * base, (kept + 1) * base)
+            for p in range(pieces // 2):
+                piece = side * (pieces // 2) + p
+                value = own_ref[r ^ flip, :, piece * span : (piece + 1) * span].astype(F32)
+                value = value + got_refs[piece][r ^ flip].astype(F32)
+                if (r >> side) & 1:
+                    send[rows, p * span : (p + 1) * span] = value.astype(BF)
+                else:
+                    keep[rows, p * span : (p + 1) * span] = value
+            sent += (r >> side) & 1
+            kept += 1 - ((r >> side) & 1)
         if tiles:
             value = tiles[0][:, cols].astype(F32) + tiles[1][:, cols].astype(F32)
             send[4 * base : 4 * base + EXTRA, :] = value.astype(BF)
@@ -722,7 +728,7 @@
         info,
         *state,
         name="scatter_second",
-        cost=2 if tiled else 0,
+        cost=15 if tiled else 0,
         after=after,
     )
 
@@ -737,16 +743,14 @@
         info,
         *state,
         name="scatter_third",
-        cost=2 if tiled else 0,
+        cost=15 if tiled else 0,
         after=after,
     )
     return left, swap_bit(send, 2)
 
 
 def scatter_plain(own, sib):
-    if len(sib) == 4:
-        sib = [jnp.concatenate([sib[i], sib[i + 2]], 2) for i in range(2)]
-    sib = jnp.concatenate(sib, 0)
+    sib = jnp.concatenate(sib, 2)
     total = own.astype(F32) + swap_core(sib).astype(F32)
     total = total.reshape(total.shape[0] * total.shape[1], total.shape[2])
     return lax.psum_scatter(total, "dp", scatter_dimension=0, tiled=True)
@@ -915,7 +919,7 @@
         [
             shape((own_count, depth)),
             shape((CHUNKS, base, 2 * units)),
-            *[shape((CHUNKS // 2, base, units))] * 4,
+            *[shape((CHUNKS, base, units // 2))] * 4,
             shape((24, depth), F32),
         ],
         info,
@@ -924,7 +928,6 @@
         second,
         dy,
         proj_full,
-        scratch=[pltpu.VMEM((depth, units), F32)],
         cost=9,
         name="mlp_grad",
     )
@@ -976,17 +979,8 @@
         after=(big_sent,) if exact else (),
     )
     keep_got = [swap_core(piece) for piece in send]
-    attn_full = call(
-        attn_grad_kernel,
-        [shape((depth, width2), F32)],
-        info,
-        branch,
-        mixed,
-        name="attn_grad",
-        after=(mlp_got, big_state[1], big_state[3]) if exact else (),
-    )[0]
     if exact:
-        big_state = scatter_middle(info, big_state, False, after=(attn_full,))
+        big_state = scatter_middle(info, big_state, False, after=(dq, mlp_got))
         big_ready = big_state[0]
         big_state = scatter_send(big_state, (1, 0))
     first_part, dkv = call(
@@ -1007,27 +1001,28 @@
         qkv_grad_kernel,
         [
             shape((CHUNKS, base, 4 * width)),
-            *[shape((CHUNKS // 2, base, 4 * width))] * 2,
+            *[shape((CHUNKS, base, 2 * width))] * 2,
             *[shape((EXTRA, depth))] * 2,
         ],
         info,
         first_own,
         dq,
         dkv,
-        attn_full,
+        branch,
+        mixed,
         first_part,
         inputs,
         stat_one,
         mlp_sums,
         att_sums,
-        scratch=[pltpu.VMEM((depth, width2), F32), pltpu.VMEM((EXTRA, depth), F32)],
+        scratch=[pltpu.VMEM((EXTRA, depth), F32)],
         cost=7,
         name="qkv_grad",
         after=(big_state[1], big_state[3]) if exact else (),
     )
     finish = lambda after: call(
         final_kernel,
-        [shape((own_count, depth))],
+        [shape((rows, depth))],
         info,
         inputs,
         stat_one,
@@ -1035,20 +1030,12 @@
         first_got,
         dmid,
         vec,
-        name="final",
-        cost=5,
-        after=after,
-    )[0]
-    output = lambda after: call(
-        output_kernel,
-        [shape((own_count, depth))],
-        info,
         seg_row,
         middle,
         mlp_part,
         mlp_got,
-        vec,
-        name="output",
+        name="final",
+        cost=7,
         after=after,
     )[0]
     tiles = (tile_own, swap_core(tile_sib))
@@ -1057,22 +1044,19 @@
         small_state = scatter_start(info, qkv_own, qkv_sib, tiles, after=(big_last[0],))
         small_sent = small_state[1]
         small_state = scatter_send(small_state, (0, 1))
-        out_low = output((small_sent,))
-        inputs_low = finish((out_low,))
-        small_state = scatter_middle(info, small_state, True, after=(inputs_low, big_last[1]))
-        small_sent = small_state[1]
+        both_low = finish((small_sent,))
+        small_state = scatter_middle(info, small_state, True, after=(both_low, big_last[1]))
         small_state = scatter_send(small_state, (1, 0))
-        outputs = all_rows(info, out_low, (small_sent,))
         fc_weight_grad, proj_weight_grad = call(
             scatter_big_kernel,
             [shape((local, units), F32), shape((units, local), F32)],
             info,
             *big_last,
             name="scatter_big",
-            cost=2,
+            cost=15,
         )
-        small_last = scatter_late(info, small_state, True, after=(outputs,))
-        inputs_grad = all_rows(info, inputs_low, (small_last[0],))
+        small_last = scatter_late(info, small_state, True)
+        outputs, inputs_grad = all_rows(info, both_low, (small_last[0],))
         qkv_weight_grad, attn_weight_grad, tile = call(
             scatter_small_kernel,
             [
@@ -1087,8 +1071,7 @@
             after=(fc_weight_grad, inputs_grad),
         )
     else:
-        inputs_grad = all_rows(info, finish(()))
-        outputs = all_rows(info, output(()))
+        outputs, inputs_grad = all_rows(info, finish(()))
         mine = scatter_plain(qkv_own, qkv_sib)
         qkv_weight_grad = mine[:, : 3 * width].reshape(local, 3, width).transpose(1, 0, 2)
         attn_weight_grad = mine[:, 3 * width :].T

time: 220 us -> 215 us (0.977)
  Pallas kernels: 121 us -> 114 us
  waiting for transfers between devices: 29.4 us -> 33.1 us
    pallas_call x22 -> x19, Pallas kernels: 121 us -> 114 us  [call(): pl.pallas_call(run, out_shape=outs, in_specs=specs, out_specs=[pl.BlockSp...]
    ppermute x24, waiting for transfers between devices: 18.5 us -> 22.5 us  [swap_mask(): return lax.ppermute(value, 'dp', [(i, i ^ mask) for i in range(CHUNKS)])]
    unnamed x100 -> x98, local copies, waits for them, and re-layouts: 15.8 us -> 14.5 us
    ppermute x20 -> x19, waiting for transfers between devices: 6.17 us -> 6.17 us  [swap_core(): return lax.ppermute(value, 'mp', CORE_PAIRS)]
  transfers between devices with their start and end apart: 49 -> 48, of which waited for: 26 -> 26; matrix products, arithmetic and copies ran while one was open for 1% -> 1% of each run, Pallas kernels for 49% -> 47%
where the time goes in v4:
time: 215 us
  Pallas kernels  114 us (53%)
  starting transfers between devices  45.5 us (21%)
  waiting for transfers between devices  33.1 us (15%)
  local copies, waits for them, and re-layouts  19.1 us (9%)
  other arithmetic  2.46 us (1%)
    pallas_call x19, Pallas kernels, call(): pl.pallas_call(run, out_shape=outs, in_specs=specs, out_specs=[pl.BlockSp...  114 us
    ppermute x24, starting transfers between devices, swap_mask(): return lax.ppermute(value, 'dp', [(i, i ^ mask) for i in range(CHUNKS)])  36.8 us
    ppermute x24, waiting for transfers between devices, swap_mask(): return lax.ppermute(value, 'dp', [(i, i ^ mask) for i in range(CHUNKS)])  22.5 us
    unnamed x98, local copies, waits for them, and re-layouts  14.5 us
    ppermute x19, waiting for transfers between devices, swap_core(): return lax.ppermute(value, 'mp', CORE_PAIRS)  6.17 us
    ppermute x5, starting transfers between devices, swap_chip(): return lax.ppermute(value, 'mp', CHIP_PAIRS)  4.93 us
    ppermute x5, waiting for transfers between devices, swap_chip(): return lax.ppermute(value, 'mp', CHIP_PAIRS)  4.45 us
  transfers between devices with their start and end apart: 48, of which 26 were waited for; matrix products, arithmetic and copies ran while one was open for 1% of the time, Pallas kernels for 47%

profile of v4, /device:TPU:0, one launch (start us, length us, event | category | flops | bytes accessed | tf_op | source)
XLA Modules:
  0.0 214.9 jit_solution(14895271395787953057)
XLA Ops:
  4.8 4.2 %collective-permute-start.2 = (bf16[112,768]{1,0:T(8,128)(2,1)S(1)}, bf16[112,768]{1,0:T(8,128)(2,1)S(1)}, u32[]{:S(2)}, u32[]{:S(2)}) collective-permute-start(bf16[112,768]{1,0:T(8,128)(2,1)S(1)} %get-tuple-element.227), channel_id=1, source_target_pairs={{0,16},{4,20},{8,24},{12,28},{16,0},{20,4},{24,8},{28,12},{1,17},{... | collective-permute-start | bytes 516104 | tf_op jit(solution)/shard_map/ppermute | solution.py:38
  12.8 4.2 %stats.1.refs_2_.refs_8_ = f32[1024,256]{1,0:T(8,128)} custom-call(s32[2]{0:T(128)} %pad_add_fusion.refs_0_, bf16[1024,768]{1,0:T(8,128)(2,1)} %refs_1_.7), custom_call_target="tpu_custom_call" | custom-call | bytes 1024 | tf_op jit(solution)/shard_map/stats/pallas_call | solution.py:54
  20.8 1.7 collective-permute-start.3
  22.6 7.5 %collective-permute-done.3 = bf16[112,768]{1,0:T(8,128)(2,1)S(1)} collective-permute-done((bf16[112,768]{1,0:T(8,128)(2,1)S(1)}, bf16[112,768]{1,0:T(8,128)(2,1)S(1)}, u32[]{:S(2)}, u32[]{:S(2)}) %collective-permute-start.3) | collective-permute-done | bytes 172064 | tf_op jit(solution)/shard_map/ppermute | solution.py:38
  30.3 2.2 %collective-permute-start.11 = (bf16[96,1536]{1,0:T(8,128)(2,1)S(1)}, bf16[96,1536]{1,0:T(8,128)(2,1)S(1)}, u32[]{:S(2)}, u32[]{:S(2)}) collective-permute-start(bf16[96,1536]{1,0:T(8,128)(2,1)S(1)} %pad_maximum_fusion.refs_3_), channel_id=1, source_target_pairs={{0,16},{4,20},{8,24},{12,28},{16,0},{20,4},{24,8},{28,12},{1,17},{... | collective-permute-start | bytes 884744 | tf_op jit(solution)/shard_map/ppermute | solution.py:38
  32.6 2.7 %collective-permute-start.10 = (bf16[96,1536]{1,0:T(8,128)(2,1)S(1)}, bf16[96,1536]{1,0:T(8,128)(2,1)S(1)}, u32[]{:S(2)}, u32[]{:S(2)}) collective-permute-start(bf16[96,1536]{1,0:T(8,128)(2,1)S(1)} %pad_maximum_fusion.refs_3_), channel_id=1, source_target_pairs={{0,8},{4,12},{8,0},{12,4},{16,24},{20,28},{24,16},{28,20},{1,9},{5... | collective-permute-start | bytes 884744 | tf_op jit(solution)/shard_map/ppermute | solution.py:38
  37.9 8.0 %project.1 = (bf16[6,512,64]{2,1,0:T(8,128)(2,1)}, bf16[6,1024,64]{2,1,0:T(8,128)(2,1)}, bf16[6,1024,64]{2,1,0:T(8,128)(2,1)}, bf16[768,384]{1,0:T(8,128)(2,1)},...) custom-call(s32[2]{0:T(128)} %pad_add_fusion.refs_0_, ...), custom_call_target="tpu_custom_call" | custom-call | flops 8000000000 | bytes 1024 | tf_op jit(solution)/shard_map/project/pallas_call | solution.py:54
  50.7 1.7 collective-permute-start.12
  52.4 13.0 %attend.1 = (bf16[512,768]{1,0:T(8,128)(2,1)}, bf16[512,384]{1,0:T(8,128)(2,1)}, bf16[6,128,2560]{2,1,0:T(8,128)(2,1)}) custom-call(s32[2]{0:T(128)} %pad_add_fusion.refs_0_, bf16[6,512,64]{2,1,0:T(8,128)(2,1)} %get-tuple-element.101.refs_1_.refs_9_, bf16[6,1024,64]{2,1,0:T(8,128)(2,1)} %get-tuple-element.102.refs_2_.refs_10_, ...), custom_call_target="tpu_custom_call" | custom-call | flops 16000000000 | bytes 1024 | tf_op jit(solution)/shard_map/attend/pallas_call | solution.py:54
  74.1 7.3 %mlp_pre.1 = (bf16[768,1536]{1,0:T(8,128)(2,1)}, bf16[768,1536]{1,0:T(8,128)(2,1)}, bf16[512,768]{1,0:T(8,128)(2,1)}, bf16[512,1536]{1,0:T(8,128)(2,1)}) custom-call(s32[2]{0:T(128)} %pad_add_fusion.refs_0_, s32[1,1024]{1,0:T(1,128)} %bitcast.50, bf16[1024,768]{1,0:T(8,128)(2,1)} %refs_2_.1, bf16[96,1536]{1,0:T(8,128)(2,1)} %copy-done, ...), custom_call_target="tpu_custom_call" | custom-call | bytes 1024 | tf_op jit(solution)/shard_map/mlp_pre/pallas_call | solution.py:54
  81.3 2.3 %collective-permute-done.8.refs_3_ = bf16[512,768]{1,0:T(8,128)(2,1)S(1)} collective-permute-done((bf16[512,768]{1,0:T(8,128)(2,1)}, bf16[512,768]{1,0:T(8,128)(2,1)S(1)}, u32[]{:S(2)}, u32[]{:S(2)}) %collective-permute-start.8) | collective-permute-done | bytes 786464 | tf_op jit(solution)/shard_map/ppermute | solution.py:34
  84.5 11.6 %mlp.1 = (bf16[512,768]{1,0:T(8,128)(2,1)}, bf16[512,1536]{1,0:T(8,128)(2,1)}, bf16[512,1536]{1,0:T(8,128)(2,1)}, bf16[512,768]{1,0:T(8,128)(2,1)}, f32[512,768]{1,0:T(8,128)}, /*index=5*/f32[512,256]{1,0:T(8,128)}) custom-call(s32[2]{0:T(128)} %pad_add_fusion.refs_0_, bf16[1024,768]{1,0:T(8,128)(2,1)} %refs_1_.7, ...), custom_call_target="tpu_custom_call" | custom-call | flops 10000000000 | bytes 1024 | tf_op jit(solution)/shard_map/mlp/pallas_call | solution.py:54
  97.6 8.6 %mlp_grad.1 = (bf16[512,768]{1,0:T(8,128)(2,1)}, bf16[8,96,1536]{2,1,0:T(8,128)(2,1)}, bf16[8,96,384]{2,1,0:T(8,128)(2,1)}, bf16[8,96,384]{2,1,0:T(8,128)(2,1)},...) custom-call(s32[2]{0:T(128)} %pad_add_fusion.refs_0_, ...), custom_call_target="tpu_custom_call" | custom-call | flops 8999999488 | bytes 1024 | tf_op jit(solution)/shard_map/mlp_grad/pallas_call | solution.py:54
  111.8 4.4 %scatter_first.2 = (f32[384,768]{1,0:T(8,128)}, bf16[384,768]{1,0:T(8,128)(2,1)}, f32[384,768]{1,0:T(8,128)}, bf16[384,768]{1,0:T(8,128)(2,1)}) custom-call(s32[2]{0:T(128)} %pad_add_fusion.refs_0_, bf16[8,96,1536]{2,1,0:T(8,128)(2,1)} %get-tuple-element.132.refs_1_, bf16[8,96,384]{2,1,0:T(8,128)(2,1)} %copy-done.4, bf16[8,96,384]{2,1,0:T(8,128)(2,1)} %copy-done.5, ...), custom_call_target="tpu_custom_call" | custom-call | bytes 1024 | tf_op jit(solution)/shard_map/scatter_first/pallas_call | solution.py:54
  118.5 17.7 %attend_back.1 = (f32[512,768]{1,0:T(8,128)}, bf16[512,768]{1,0:T(8,128)(2,1)}, f32[8,768]{1,0:T(8,128)}, bf16[512,384]{1,0:T(8,128)(2,1)}, f32[768,512]{1,0:T(8...) custom-call(s32[2]{0:T(128)} %pad_add_fusion.refs_0_, f32[512,768]{1,0:T(8,128)} %get-tuple-element.122.refs_1_.refs_8_, ...), custom_call_target="tpu_custom_call" | custom-call | flops 17999998976 | bytes 1024 | tf_op jit(solution)/shard_map/attend_back/pallas_call | solution.py:54
  138.1 3.2 %scatter_second.2 = (f32[192,768]{1,0:T(8,128)}, bf16[192,768]{1,0:T(8,128)(2,1)}, f32[192,768]{1,0:T(8,128)}, bf16[192,768]{1,0:T(8,128)(2,1)}) custom-call(s32[2]{0:T(128)} %pad_add_fusion.refs_0_, f32[384,768]{1,0:T(8,128)} %get-tuple-element.145.refs_1_, bf16[384,768]{1,0:T(8,128)(2,1)} %copy-done.2, f32[384,768]{1,0:T(8,128)} %get-tuple-element.146.refs_3_, ...), custom_call_target="tpu_custom_call" | custom-call | bytes 1024 | tf_op jit(solution)/shard_map/scatter_second/pallas_call | solution.py:54
  144.7 4.6 %first_grad.1 = (bf16[512,768]{1,0:T(8,128)(2,1)}, bf16[768,512]{1,0:T(8,128)(2,1)}) custom-call(s32[2]{0:T(128)} %pad_add_fusion.refs_0_, bf16[512,384]{1,0:T(8,128)(2,1)} %get-tuple-element.138.refs_5_.refs_1_.refs_2_, f32[768,512]{1,0:T(8,128)} %get-tuple-element.139.refs_2_, bf16[384,512]{1,0:T(8,128)(2,1)} %copy-done.11, bf16[384,512]{1,0:T(8,128)(2,1)} %copy-done.12, ...), custom_call_target="tpu_custom_call" | custom-call | bytes 1024 | tf_op jit(solution)/shard_map/first_grad/pallas_call | solution.py:54
  151.8 6.9 %qkv_grad.1 = (bf16[8,96,768]{2,1,0:T(8,128)(2,1)}, bf16[8,96,384]{2,1,0:T(8,128)(2,1)}, bf16[8,96,384]{2,1,0:T(8,128)(2,1)}, bf16[16,768]{1,0:T(8,128)(2,1)}, bf16[16,768]{1,0:T(8,128)(2,1)}) custom-call(s32[2]{0:T(128)} %pad_add_fusion.refs_0_, bf16[512,768]{1,0:T(8,128)(2,1)} %get-tuple-element.152.refs_1_, ...), custom_call_target="tpu_custom_call" | custom-call | flops 7000000000 | bytes 1024 | tf_op jit(solution)/shard_map/qkv_grad/pallas_call | solution.py:54
  159.3 2.4 %scatter_third.2 = (f32[96,1536]{1,0:T(8,128)}, bf16[96,1536]{1,0:T(8,128)(2,1)}) custom-call(s32[2]{0:T(128)} %pad_add_fusion.refs_0_, f32[192,768]{1,0:T(8,128)} %get-tuple-element.149.refs_8_.refs_1_, bf16[192,768]{1,0:T(8,128)(2,1)} %copy-done.20, f32[192,768]{1,0:T(8,128)} %get-tuple-element.164.refs_3_, bf16[192,768]{1,0:T(8,128)(2,1)} %copy-done.22, ...), custom_call_target="tpu_custom_call" | custom-call | bytes 1024 | tf_op jit(solution)/shard_map/scatter_third/pallas_call | solution.py:54
  161.7 2.3 %collective-permute-start.43 = (bf16[96,1536]{1,0:T(8,128)(2,1)}, bf16[96,1536]{1,0:T(8,128)(2,1)S(1)}, u32[]{:S(2)}, u32[]{:S(2)}) collective-permute-start(bf16[96,1536]{1,0:T(8,128)(2,1)} %get-tuple-element.170), channel_id=1, source_target_pairs={{0,16},{4,20},{8,24},{12,28},{16,0},{20,4},{24,8},{28,12},{1,17},{... | collective-permute-start | bytes 884744 | tf_op jit(solution)/shard_map/ppermute | solution.py:38
  165.0 3.1 %scatter_first.3 = (f32[400,384]{1,0:T(8,128)}, bf16[400,384]{1,0:T(8,128)(2,1)}, f32[400,384]{1,0:T(8,128)}, bf16[400,384]{1,0:T(8,128)(2,1)}) custom-call(s32[2]{0:T(128)} %pad_add_fusion.refs_0_, bf16[8,96,768]{2,1,0:T(8,128)(2,1)} %get-tuple-element.159.refs_5_.refs_1_, bf16[8,96,384]{2,1,0:T(8,128)(2,1)} %copy-done.8, bf16[8,96,384]{2,1,0:T(8,128)(2,1)} %copy-done.9, ...), custom_call_target="tpu_custom_call" | custom-call | bytes 1024 | tf_op jit(solution)/shard_map/scatter_first/pallas_call | solution.py:54
  172.0 6.5 %final.1.refs_5_.refs_1_ = bf16[1024,768]{1,0:T(8,128)(2,1)} custom-call(s32[2]{0:T(128)} %pad_add_fusion.refs_0_, bf16[1024,768]{1,0:T(8,128)(2,1)} %refs_1_.7, f32[1024,256]{1,0:T(8,128)} %stats.1.refs_2_.refs_8_, bf16[512,768]{1,0:T(8,128)(2,1)} %get-tuple-element.150.refs_6_.refs_3_, bf16[512,768]{1,0:T(8,128)(2,1)} %copy-done.37, ...), custom_call_target="tpu_custom_call" | custom-call | flops 7000000000 | bytes 1024 | tf_op jit(solution)/shard_map/final/pallas_call | solution.py:54
  178.6 5.8 %collective-permute-done.42.refs_4_ = bf16[400,384]{1,0:T(8,128)(2,1)S(1)} collective-permute-done((bf16[400,384]{1,0:T(8,128)(2,1)}, bf16[400,384]{1,0:T(8,128)(2,1)S(1)}, u32[]{:S(2)}, u32[]{:S(2)}) %collective-permute-start.42) | collective-permute-done | bytes 307232 | tf_op jit(solution)/shard_map/ppermute | solution.py:38
  185.2 2.4 %scatter_second.3 = (f32[208,384]{1,0:T(8,128)}, bf16[208,384]{1,0:T(8,128)(2,1)}, f32[208,384]{1,0:T(8,128)}, bf16[208,384]{1,0:T(8,128)(2,1)}) custom-call(s32[2]{0:T(128)} %pad_add_fusion.refs_0_, f32[400,384]{1,0:T(8,128)} %get-tuple-element.167.refs_1_, bf16[400,384]{1,0:T(8,128)(2,1)} %copy-done.39, f32[400,384]{1,0:T(8,128)} %get-tuple-element.168.refs_3_, ...), custom_call_target="tpu_custom_call" | custom-call | flops 15000000512 | bytes 1024 | tf_op jit(solution)/shard_map/scatter_second/pallas_call | solution.py:54
  188.2 2.2 %scatter_big.1 = (f32[96,768]{1,0:T(8,128)}, f32[768,96]{1,0:T(8,128)}) custom-call(s32[2]{0:T(128)} %pad_add_fusion.refs_0_, f32[96,1536]{1,0:T(8,128)} %get-tuple-element.165.refs_6_.refs_1_, bf16[96,1536]{1,0:T(8,128)(2,1)} %copy-done.41), custom_call_target="tpu_custom_call" | custom-call | flops 15000000512 | bytes 1024 | tf_op jit(solution)/shard_map/scatter_big/pallas_call | solution.py:54
  190.4 2.7 %collective-permute-done.44.refs_2_ = bf16[208,384]{1,0:T(8,128)(2,1)S(1)} collective-permute-done((bf16[208,384]{1,0:T(8,128)(2,1)}, bf16[208,384]{1,0:T(8,128)(2,1)S(1)}, u32[]{:S(2)}, u32[]{:S(2)}) %collective-permute-start.44) | collective-permute-done | bytes 159776 | tf_op jit(solution)/shard_map/ppermute | solution.py:38
  193.8 2.0 scatter_third.3
  195.8 2.4 %collective-permute-start.46 = (bf16[112,768]{1,0:T(8,128)(2,1)}, bf16[112,768]{1,0:T(8,128)(2,1)S(1)}, u32[]{:S(2)}, u32[]{:S(2)}) collective-permute-start(bf16[112,768]{1,0:T(8,128)(2,1)} %get-tuple-element.178), channel_id=1, source_target_pairs={{0,16},{4,20},{8,24},{12,28},{16,0},{20,4},{24,8},{28,12},{1,17},{... | collective-permute-start | bytes 516104 | tf_op jit(solution)/shard_map/ppermute | solution.py:38
  199.4 3.7 %merge.1 = (bf16[1024,768]{1,0:T(8,128)(2,1)}, bf16[1024,768]{1,0:T(8,128)(2,1)}) custom-call(s32[2]{0:T(128)} %pad_add_fusion.refs_0_, bf16[1024,768]{1,0:T(8,128)(2,1)} %final.1.refs_5_.refs_1_, bf16[1024,768]{1,0:T(8,128)(2,1)} %copy-done.34, f32[112,768]{1,0:T(8,128)} %get-tuple-element.175.refs_3_.refs_1_), custom_call_target="tpu_custom_call" | custom-call | flops 4000000000 | bytes 1024 | tf_op jit(solution)/shard_map/merge/pallas_call | solution.py:54
  203.2 2.1 collective-permute-done.46.refs_2_
  205.9 1.9 scatter_small.1
  210.4 2.1 collective-permute-done.47
  (205 shorter events, 60.5 us)
Async XLA Ops:
  4.8 12.4 %collective-permute-start.2 = (bf16[112,768]{1,0:T(8,128)(2,1)S(1)}, bf16[112,768]{1,0:T(8,128)(2,1)S(1)}, u32[]{:S(2)}, u32[]{:S(2)}) collective-permute-start(bf16[112,768]{1,0:T(8,128)(2,1)S(1)} %get-tuple-element.227), channel_id=1, source_target_pairs={{0,16},{4,20},{8,24},{12,28},{16,0},{20,4},{24,8},{28,12},{1,17},{... | collective-permute-start | bytes 516104 | tf_op jit(solution)/shard_map/ppermute | solution.py:38
  9.0 8.3 %collective-permute-start.1 = (bf16[112,768]{1,0:T(8,128)(2,1)S(1)}, bf16[112,768]{1,0:T(8,128)(2,1)S(1)}, u32[]{:S(2)}, u32[]{:S(2)}) collective-permute-start(bf16[112,768]{1,0:T(8,128)(2,1)S(1)} %get-tuple-element.227), channel_id=1, source_target_pairs={{0,8},{4,12},{8,0},{12,4},{16,24},{20,28},{24,16},{28,20},{1,9},{5... | collective-permute-start | bytes 516104 | tf_op jit(solution)/shard_map/ppermute | solution.py:38
  10.7 11.8 %collective-permute-start = (bf16[112,768]{1,0:T(8,128)(2,1)S(1)}, bf16[112,768]{1,0:T(8,128)(2,1)S(1)}, u32[]{:S(2)}, u32[]{:S(2)}) collective-permute-start(bf16[112,768]{1,0:T(8,128)(2,1)S(1)} %get-tuple-element.227), channel_id=1, source_target_pairs={{0,4},{4,0},{8,12},{12,8},{16,20},{20,16},{24,28},{28,24},{1,5},{5... | collective-permute-start | bytes 516104 | tf_op jit(solution)/shard_map/ppermute | solution.py:38
  17.3 12.8 %collective-permute-start.4 = (bf16[112,768]{1,0:T(8,128)(2,1)S(1)}, bf16[112,768]{1,0:T(8,128)(2,1)S(1)}, u32[]{:S(2)}, u32[]{:S(2)}) collective-permute-start(bf16[112,768]{1,0:T(8,128)(2,1)S(1)} %collective-permute-done.2), channel_id=1, source_target_pairs={{0,4},{4,0},{8,12},{12,8},{16,20},{20,16},{24,28},{28,24},{1,5},{5... | collective-permute-start | bytes 516104 | tf_op jit(solution)/shard_map/ppermute | solution.py:38
  19.0 11.1 %collective-permute-start.5 = (bf16[112,768]{1,0:T(8,128)(2,1)S(1)}, bf16[112,768]{1,0:T(8,128)(2,1)S(1)}, u32[]{:S(2)}, u32[]{:S(2)}) collective-permute-start(bf16[112,768]{1,0:T(8,128)(2,1)S(1)} %collective-permute-done.2), channel_id=1, source_target_pairs={{0,8},{4,12},{8,0},{12,4},{16,24},{20,28},{24,16},{28,20},{1,9},{5... | collective-permute-start | bytes 516104 | tf_op jit(solution)/shard_map/ppermute | solution.py:38
  20.5 9.7 %collective-permute-start.6 = (bf16[112,768]{1,0:T(8,128)(2,1)S(1)}, bf16[112,768]{1,0:T(8,128)(2,1)S(1)}, u32[]{:S(2)}, u32[]{:S(2)}) collective-permute-start(bf16[112,768]{1,0:T(8,128)(2,1)S(1)} %collective-permute-done.2), channel_id=1, source_target_pairs={{0,12},{4,8},{8,4},{12,0},{16,28},{20,24},{24,20},{28,16},{1,13},{... | collective-permute-start | bytes 516104 | tf_op jit(solution)/shard_map/ppermute | solution.py:38
  20.8 9.3 %collective-permute-start.3 = (bf16[112,768]{1,0:T(8,128)(2,1)S(1)}, bf16[112,768]{1,0:T(8,128)(2,1)S(1)}, u32[]{:S(2)}, u32[]{:S(2)}) collective-permute-start(bf16[112,768]{1,0:T(8,128)(2,1)S(1)} %collective-permute-done.1), channel_id=1, source_target_pairs={{0,4},{4,0},{8,12},{12,8},{16,20},{20,16},{24,28},{28,24},{1,5},{5... | collective-permute-start | bytes 516104 | tf_op jit(solution)/shard_map/ppermute | solution.py:38
  30.2 6.6 %collective-permute-start.7 = (bf16[8,112,768]{2,1,0:T(8,128)(2,1)S(1)}, bf16[8,112,768]{2,1,0:T(8,128)(2,1)S(1)}, u32[]{:S(2)}, u32[]{:S(2)}) collective-permute-start(bf16[8,112,768]{2,1,0:T(8,128)(2,1)S(1)} %bitcast_dynamic-update-slice_fusion.refs_3_), channel_id=1, source_target_pairs={{0,1},{1,0},{2,3},{3,2},{4,5},{5,4},{6,7},{7,6},{8,9},{9,8},{10,11... | collective-permute-start | bytes 4128776 | tf_op jit(solution)/shard_map/ppermute | solution.py:30
  30.3 16.8 %collective-permute-start.11 = (bf16[96,1536]{1,0:T(8,128)(2,1)S(1)}, bf16[96,1536]{1,0:T(8,128)(2,1)S(1)}, u32[]{:S(2)}, u32[]{:S(2)}) collective-permute-start(bf16[96,1536]{1,0:T(8,128)(2,1)S(1)} %pad_maximum_fusion.refs_3_), channel_id=1, source_target_pairs={{0,16},{4,20},{8,24},{12,28},{16,0},{20,4},{24,8},{28,12},{1,17},{... | collective-permute-start | bytes 884744 | tf_op jit(solution)/shard_map/ppermute | solution.py:38
  32.6 14.6 %collective-permute-start.10 = (bf16[96,1536]{1,0:T(8,128)(2,1)S(1)}, bf16[96,1536]{1,0:T(8,128)(2,1)S(1)}, u32[]{:S(2)}, u32[]{:S(2)}) collective-permute-start(bf16[96,1536]{1,0:T(8,128)(2,1)S(1)} %pad_maximum_fusion.refs_3_), channel_id=1, source_target_pairs={{0,8},{4,12},{8,0},{12,4},{16,24},{20,28},{24,16},{28,20},{1,9},{5... | collective-permute-start | bytes 884744 | tf_op jit(solution)/shard_map/ppermute | solution.py:38
  35.2 30.2 %collective-permute-start.9 = (bf16[96,1536]{1,0:T(8,128)(2,1)S(1)}, bf16[96,1536]{1,0:T(8,128)(2,1)S(1)}, u32[]{:S(2)}, u32[]{:S(2)}) collective-permute-start(bf16[96,1536]{1,0:T(8,128)(2,1)S(1)} %pad_maximum_fusion.refs_3_), channel_id=1, source_target_pairs={{0,4},{4,0},{8,12},{12,8},{16,20},{20,16},{24,28},{28,24},{1,5},{5... | collective-permute-start | bytes 884744 | tf_op jit(solution)/shard_map/ppermute | solution.py:38
  47.2 21.2 %collective-permute-start.13 = (bf16[96,1536]{1,0:T(8,128)(2,1)S(1)}, bf16[96,1536]{1,0:T(8,128)(2,1)S(1)}, u32[]{:S(2)}, u32[]{:S(2)}) collective-permute-start(bf16[96,1536]{1,0:T(8,128)(2,1)S(1)} %collective-permute-done.11.refs_7_), channel_id=1, source_target_pairs={{0,4},{4,0},{8,12},{12,8},{16,20},{20,16},{24,28},{28,24},{1,5},{5... | collective-permute-start | bytes 884744 | tf_op jit(solution)/shard_map/ppermute | solution.py:38
  48.9 19.5 %collective-permute-start.14 = (bf16[96,1536]{1,0:T(8,128)(2,1)S(1)}, bf16[96,1536]{1,0:T(8,128)(2,1)S(1)}, u32[]{:S(2)}, u32[]{:S(2)}) collective-permute-start(bf16[96,1536]{1,0:T(8,128)(2,1)S(1)} %collective-permute-done.11.refs_7_), channel_id=1, source_target_pairs={{0,8},{4,12},{8,0},{12,4},{16,24},{20,28},{24,16},{28,20},{1,9},{5... | collective-permute-start | bytes 884744 | tf_op jit(solution)/shard_map/ppermute | solution.py:38
  49.8 18.6 %collective-permute-start.15 = (bf16[96,1536]{1,0:T(8,128)(2,1)S(1)}, bf16[96,1536]{1,0:T(8,128)(2,1)S(1)}, u32[]{:S(2)}, u32[]{:S(2)}) collective-permute-start(bf16[96,1536]{1,0:T(8,128)(2,1)S(1)} %collective-permute-done.11.refs_7_), channel_id=1, source_target_pairs={{0,12},{4,8},{8,4},{12,0},{16,28},{20,24},{24,20},{28,16},{1,13},{... | collective-permute-start | bytes 884744 | tf_op jit(solution)/shard_map/ppermute | solution.py:38
  50.7 17.7 %collective-permute-start.12 = (bf16[96,1536]{1,0:T(8,128)(2,1)S(1)}, bf16[96,1536]{1,0:T(8,128)(2,1)S(1)}, u32[]{:S(2)}, u32[]{:S(2)}) collective-permute-start(bf16[96,1536]{1,0:T(8,128)(2,1)S(1)} %collective-permute-done.10.refs_5_), channel_id=1, source_target_pairs={{0,4},{4,0},{8,12},{12,8},{16,20},{20,16},{24,28},{28,24},{1,5},{5... | collective-permute-start | bytes 884744 | tf_op jit(solution)/shard_map/ppermute | solution.py:38
  65.4 18.2 %collective-permute-start.8 = (bf16[512,768]{1,0:T(8,128)(2,1)}, bf16[512,768]{1,0:T(8,128)(2,1)S(1)}, u32[]{:S(2)}, u32[]{:S(2)}) collective-permute-start(bf16[512,768]{1,0:T(8,128)(2,1)} %get-tuple-element.105.refs_2_), channel_id=1, source_target_pairs={{0,2},{2,0},{1,3},{3,1},{4,6},{6,4},{5,7},{7,5},{8,10},{10,8},{9,1... | collective-permute-start | bytes 2359304 | tf_op jit(solution)/shard_map/ppermute | solution.py:34
  96.1 21.5 %collective-permute-start.24 = (bf16[512,768]{1,0:T(8,128)(2,1)}, bf16[512,768]{1,0:T(8,128)(2,1)S(1)}, u32[]{:S(2)}, u32[]{:S(2)}) collective-permute-start(bf16[512,768]{1,0:T(8,128)(2,1)} %get-tuple-element.125.refs_4_), channel_id=1, source_target_pairs={{0,2},{2,0},{1,3},{3,1},{4,6},{6,4},{5,7},{7,5},{8,10},{10,8},{9,1... | collective-permute-start | bytes 2359304 | tf_op jit(solution)/shard_map/ppermute | solution.py:34
  108.5 28.3 %collective-permute-start.33 = (bf16[512,768]{1,0:T(8,128)(2,1)}, bf16[512,768]{1,0:T(8,128)(2,1)S(1)}, u32[]{:S(2)}, u32[]{:S(2)}) collective-permute-start(bf16[512,768]{1,0:T(8,128)(2,1)} %get-tuple-element.148.refs_9_), channel_id=1, source_target_pairs={{0,2},{2,0},{1,3},{3,1},{4,6},{6,4},{5,7},{7,5},{8,10},{10,8},{9,1... | collective-permute-start | bytes 2359304 | tf_op jit(solution)/shard_map/ppermute | solution.py:34
  116.2 20.6 %collective-permute-start.31 = (bf16[384,768]{1,0:T(8,128)(2,1)}, bf16[384,768]{1,0:T(8,128)(2,1)S(1)}, u32[]{:S(2)}, u32[]{:S(2)}) collective-permute-start(bf16[384,768]{1,0:T(8,128)(2,1)} %get-tuple-element.137.refs_13_), channel_id=1, source_target_pairs={{0,4},{4,0},{8,12},{12,8},{16,20},{20,16},{24,28},{28,24},{1,5},{5... | collective-permute-start | bytes 1769480 | tf_op jit(solution)/shard_map/ppermute | solution.py:38
  116.5 20.2 %collective-permute-start.32 = (bf16[384,768]{1,0:T(8,128)(2,1)}, bf16[384,768]{1,0:T(8,128)(2,1)S(1)}, u32[]{:S(2)}, u32[]{:S(2)}) collective-permute-start(bf16[384,768]{1,0:T(8,128)(2,1)} %get-tuple-element.147), channel_id=1, source_target_pairs={{0,8},{4,12},{8,0},{12,4},{16,24},{20,28},{24,16},{28,20},{1,9},{5... | collective-permute-start | bytes 1769480 | tf_op jit(solution)/shard_map/ppermute | solution.py:38
  136.3 7.6 %collective-permute-start.29 = (bf16[384,512]{1,0:T(8,128)(2,1)}, bf16[384,512]{1,0:T(8,128)(2,1)S(1)}, u32[]{:S(2)}, u32[]{:S(2)}) collective-permute-start(bf16[384,512]{1,0:T(8,128)(2,1)} %get-tuple-element.140), channel_id=1, source_target_pairs={{0,1},{1,0},{2,3},{3,2},{4,5},{5,4},{6,7},{7,6},{8,9},{9,8},{10,11... | collective-permute-start | bytes 1179656 | tf_op jit(solution)/shard_map/ppermute | solution.py:30
  136.3 7.6 %collective-permute-start.30 = (bf16[384,512]{1,0:T(8,128)(2,1)}, bf16[384,512]{1,0:T(8,128)(2,1)S(1)}, u32[]{:S(2)}, u32[]{:S(2)}) collective-permute-start(bf16[384,512]{1,0:T(8,128)(2,1)} %get-tuple-element.141), channel_id=1, source_target_pairs={{0,1},{1,0},{2,3},{3,2},{4,5},{5,4},{6,7},{7,6},{8,9},{9,8},{10,11... | collective-permute-start | bytes 1179656 | tf_op jit(solution)/shard_map/ppermute | solution.py:30
  141.3 9.2 %collective-permute-start.35 = (bf16[192,768]{1,0:T(8,128)(2,1)}, bf16[192,768]{1,0:T(8,128)(2,1)S(1)}, u32[]{:S(2)}, u32[]{:S(2)}) collective-permute-start(bf16[192,768]{1,0:T(8,128)(2,1)} %get-tuple-element.157), channel_id=1, source_target_pairs={{0,8},{4,12},{8,0},{12,4},{16,24},{20,28},{24,16},{28,20},{1,9},{5... | collective-permute-start | bytes 884744 | tf_op jit(solution)/shard_map/ppermute | solution.py:38
  142.2 8.9 %collective-permute-start.36 = (bf16[192,768]{1,0:T(8,128)(2,1)}, bf16[192,768]{1,0:T(8,128)(2,1)S(1)}, u32[]{:S(2)}, u32[]{:S(2)}) collective-permute-start(bf16[192,768]{1,0:T(8,128)(2,1)} %get-tuple-element.158), channel_id=1, source_target_pairs={{0,4},{4,0},{8,12},{12,8},{16,20},{20,16},{24,28},{28,24},{1,5},{5... | collective-permute-start | bytes 884744 | tf_op jit(solution)/shard_map/ppermute | solution.py:38
  149.3 21.9 %collective-permute-start.34 = (bf16[512,768]{1,0:T(8,128)(2,1)}, bf16[512,768]{1,0:T(8,128)(2,1)S(1)}, u32[]{:S(2)}, u32[]{:S(2)}) collective-permute-start(bf16[512,768]{1,0:T(8,128)(2,1)} %get-tuple-element.150.refs_6_.refs_3_), channel_id=1, source_target_pairs={{0,2},{2,0},{1,3},{3,1},{4,6},{6,4},{5,7},{7,5},{8,10},{10,8},{9,1... | collective-permute-start | bytes 2359304 | tf_op jit(solution)/shard_map/ppermute | solution.py:34
  161.7 16.9 %collective-permute-start.43 = (bf16[96,1536]{1,0:T(8,128)(2,1)}, bf16[96,1536]{1,0:T(8,128)(2,1)S(1)}, u32[]{:S(2)}, u32[]{:S(2)}) collective-permute-start(bf16[96,1536]{1,0:T(8,128)(2,1)} %get-tuple-element.170), channel_id=1, source_target_pairs={{0,16},{4,20},{8,24},{12,28},{16,0},{20,4},{24,8},{28,12},{1,17},{... | collective-permute-start | bytes 884744 | tf_op jit(solution)/shard_map/ppermute | solution.py:38
  168.1 10.5 %collective-permute-start.41 = (bf16[400,384]{1,0:T(8,128)(2,1)}, bf16[400,384]{1,0:T(8,128)(2,1)S(1)}, u32[]{:S(2)}, u32[]{:S(2)}) collective-permute-start(bf16[400,384]{1,0:T(8,128)(2,1)} %get-tuple-element.166.refs_11_), channel_id=1, source_target_pairs={{0,4},{4,0},{8,12},{12,8},{16,20},{20,16},{24,28},{28,24},{1,5},{5... | collective-permute-start | bytes 921608 | tf_op jit(solution)/shard_map/ppermute | solution.py:38
  169.6 14.8 %collective-permute-start.42 = (bf16[400,384]{1,0:T(8,128)(2,1)}, bf16[400,384]{1,0:T(8,128)(2,1)S(1)}, u32[]{:S(2)}, u32[]{:S(2)}) collective-permute-start(bf16[400,384]{1,0:T(8,128)(2,1)} %get-tuple-element.169), channel_id=1, source_target_pairs={{0,8},{4,12},{8,0},{12,4},{16,24},{20,28},{24,16},{28,20},{1,9},{5... | collective-permute-start | bytes 921608 | tf_op jit(solution)/shard_map/ppermute | solution.py:38
  178.5 19.7 %collective-permute-start.40 = (bf16[1024,768]{1,0:T(8,128)(2,1)}, bf16[1024,768]{1,0:T(8,128)(2,1)S(1)}, u32[]{:S(2)}, u32[]{:S(2)}) collective-permute-start(bf16[1024,768]{1,0:T(8,128)(2,1)} %final.1.refs_5_.refs_1_), channel_id=1, source_target_pairs={{0,1},{1,0},{2,3},{3,2},{4,5},{5,4},{6,7},{7,6},{8,9},{9,8},{10,11... | collective-permute-start | bytes 4718600 | tf_op jit(solution)/shard_map/ppermute | solution.py:30
  187.5 5.6 %collective-permute-start.44 = (bf16[208,384]{1,0:T(8,128)(2,1)}, bf16[208,384]{1,0:T(8,128)(2,1)S(1)}, u32[]{:S(2)}, u32[]{:S(2)}) collective-permute-start(bf16[208,384]{1,0:T(8,128)(2,1)} %get-tuple-element.172), channel_id=1, source_target_pairs={{0,8},{4,12},{8,0},{12,4},{16,24},{20,28},{24,16},{28,20},{1,9},{5... | collective-permute-start | bytes 479240 | tf_op jit(solution)/shard_map/ppermute | solution.py:38
  187.5 5.6 %collective-permute-start.45 = (bf16[208,384]{1,0:T(8,128)(2,1)}, bf16[208,384]{1,0:T(8,128)(2,1)S(1)}, u32[]{:S(2)}, u32[]{:S(2)}) collective-permute-start(bf16[208,384]{1,0:T(8,128)(2,1)} %get-tuple-element.174), channel_id=1, source_target_pairs={{0,4},{4,0},{8,12},{12,8},{16,20},{20,16},{24,28},{28,24},{1,5},{5... | collective-permute-start | bytes 479240 | tf_op jit(solution)/shard_map/ppermute | solution.py:38
  195.8 9.4 %collective-permute-start.46 = (bf16[112,768]{1,0:T(8,128)(2,1)}, bf16[112,768]{1,0:T(8,128)(2,1)S(1)}, u32[]{:S(2)}, u32[]{:S(2)}) collective-permute-start(bf16[112,768]{1,0:T(8,128)(2,1)} %get-tuple-element.178), channel_id=1, source_target_pairs={{0,16},{4,20},{8,24},{12,28},{16,0},{20,4},{24,8},{28,12},{1,17},{... | collective-permute-start | bytes 516104 | tf_op jit(solution)/shard_map/ppermute | solution.py:38
  (61 other events, 239.5 us)

commit v5 on v4

--- a/solution.py
+++ b/solution.py
@@ -105,6 +105,10 @@
 def own_start(start, core):
     tile = start // TILE
     return pl.multiple_of((2 * tile + core) * TILE + start % TILE, 32)
+
+
+def fold(value):
+    return jnp.sum(value.reshape(value.shape[0] // 8, 8, value.shape[1]), 0)
 
 
 def colsum(value):
@@ -386,6 +390,7 @@
     dp_ref,
     ds_ref,
     delta_ref,
+    acc_ref,
 ):
     core = info[1]
     own_count = mid_ref.shape[0]
@@ -404,11 +409,14 @@
         dmid_ref[rs, :] = dmid
         low = dmid.astype(BF)
         branch_ref[rs, :] = low
-        sums_ref[2:3, :] += colsum(low.astype(F32))
-        sums_ref[3:4, :] += colsum(incoming * scaled)
-        sums_ref[4:5, :] += colsum(incoming)
-
+        acc_ref[0] += fold(low.astype(F32))
+        acc_ref[1] += fold(incoming * scaled)
+        acc_ref[2] += fold(incoming)
+
+    acc_ref[...] = jnp.zeros_like(acc_ref)
     loop(own_count, sub, first)
+    for i in range(3):
+        sums_ref[2 + i : 3 + i, :] = colsum(acc_ref[i])
     dm_ref[...] = dot(branch_ref[...], wo_ref[...], 1, 0).astype(BF)
     for h in range(heads):
         cols = slice(h * HD, (h + 1) * HD)
@@ -444,7 +452,7 @@
                 dvt_ref[h, :, 0:end] += dv
         return carry
 
-    lax.fori_loop(0, heads, head, 0, unroll=3)
+    lax.fori_loop(0, heads, head, 0, unroll=True)
     width2 = heads * HD
     for h in range(heads):
         dq_ref[:, h * HD : (h + 1) * HD] = dqh_ref[h].astype(BF)
@@ -491,6 +499,7 @@
     tile_own_ref,
     tile_sib_ref,
     sum_ref,
+    acc_ref,
 ):
     core = info[1]
     width2 = dq_ref.shape[1]
@@ -519,10 +528,13 @@
         rs = pl.ds(src, 32)
         scaled = (x_ref[rs, :].astype(F32) - stat_ref[rs, 0:1]) * stat_ref[rs, TILE : TILE + 1]
         incoming = part_ref[pl.ds(at, 32), :].astype(F32)
-        sum_ref[0:1, :] += colsum(incoming * scaled)
-        sum_ref[1:2, :] += colsum(incoming)
-
+        acc_ref[0] += fold(incoming * scaled)
+        acc_ref[1] += fold(incoming)
+
+    acc_ref[...] = jnp.zeros_like(acc_ref)
     loop(part_ref.shape[0], 32, run)
+    for i in range(2):
+        sum_ref[i : i + 1, :] = colsum(acc_ref[i])
     ones = jnp.ones((8, dq_ref.shape[0]), BF)
     qs = dot(ones, dq_ref[...], 1, 0)[0:1, :]
     vs = dot(ones, dkv_ref[width2 : 2 * width2, :], 1, 1)[0:1, :]
@@ -686,7 +698,7 @@
     proj_ref[...] = jnp.transpose(total[:, units:])
 
 
-def scatter_small_kernel(info, left, got, qkv_ref, attn_ref, tile_ref):
+def scatter_small_kernel(info, left, got, qkv_ref, attn_ref, tile_ref, tile_low_ref):
     base = left.shape[0] - EXTRA
     width = qkv_ref.shape[2]
     total = left[0:base, :] + got[0:base, :].astype(F32)
@@ -694,7 +706,9 @@
         qkv_ref[p] = total[:, p * width : (p + 1) * width]
     attn_ref[...] = jnp.transpose(total[:, 3 * width :])
     rows = slice(base, base + EXTRA)
-    tile_ref[...] = left[rows, :].astype(BF).astype(F32) + got[rows, :].astype(F32)
+    tile = left[rows, :].astype(BF).astype(F32) + got[rows, :].astype(F32)
+    tile_ref[...] = tile
+    tile_low_ref[...] = tile.astype(BF)
 
 
 def scatter_start(info, own, sib, tiles=(), after=()):
@@ -973,6 +987,7 @@
             pltpu.VMEM((heads2, TILE, rows), F32),
             pltpu.VMEM((heads2, TILE, rows), BF),
             pltpu.VMEM((heads2, own_count, TILE), F32),
+            pltpu.VMEM((3, 8, depth), F32),
         ],
         cost=18,
         name="attend_back",
@@ -1015,7 +1030,7 @@
         stat_one,
         mlp_sums,
         att_sums,
-        scratch=[pltpu.VMEM((EXTRA, depth), F32)],
+        scratch=[pltpu.VMEM((EXTRA, depth), F32), pltpu.VMEM((2, 8, depth), F32)],
         cost=7,
         name="qkv_grad",
         after=(big_state[1], big_state[3]) if exact else (),
@@ -1057,12 +1072,13 @@
         )
         small_last = scatter_late(info, small_state, True)
         outputs, inputs_grad = all_rows(info, both_low, (small_last[0],))
-        qkv_weight_grad, attn_weight_grad, tile = call(
+        qkv_weight_grad, attn_weight_grad, tile, tile_low = call(
             scatter_small_kernel,
             [
                 shape((3, local, width), F32),
                 shape((width, local), F32),
                 shape((EXTRA, depth), F32),
+                shape((EXTRA, depth)),
             ],
             info,
             *small_last,
@@ -1076,9 +1092,10 @@
         qkv_weight_grad = mine[:, : 3 * width].reshape(local, 3, width).transpose(1, 0, 2)
         attn_weight_grad = mine[:, 3 * width :].T
         tile = lax.psum(tiles[0].astype(F32) + tiles[1].astype(F32), "dp")
-    tile_got = swap_chip(tile.astype(BF)).astype(F32)
+        tile_low = tile.astype(BF)
+    tile_got = swap_chip(tile_low).astype(F32)
     mask = (jnp.arange(EXTRA) < 2)[:, None]
-    tile = jnp.where(mask, tile.astype(BF).astype(F32) + tile_got, tile)
+    tile = jnp.where(mask, tile_low.astype(F32) + tile_got, tile)
     parts = lax.dynamic_slice(tile, (0, index * local), (7, local))
     bias_sum = tile[7, :width2].reshape(2, heads, HD).transpose(1, 0, 2).reshape(heads, 2 * HD)
     qv_bias_grad = lax.dynamic_slice(bias_sum, (0, index * bias_width), (heads, bias_width))

time: 215 us -> 212 us (0.986)
  Pallas kernels: 114 us -> 110 us
    pallas_call x19, Pallas kernels: 114 us -> 110 us  [call(): pl.pallas_call(run, out_shape=outs, in_specs=specs, out_specs=[pl.BlockSp...]
  transfers between devices with their start and end apart: 48 -> 48, of which waited for: 26 -> 26; matrix products, arithmetic and copies ran while one was open for 1% -> 1% of each run, Pallas kernels for 47% -> 46%
where the time goes in v5:
time: 212 us; the launch traced here: 211 us
  Pallas kernels  110 us (52%)
  starting transfers between devices  45.6 us (22%)
  waiting for transfers between devices  33.3 us (16%)
  local copies, waits for them, and re-layouts  19.1 us (9%)
    pallas_call x19, Pallas kernels, call(): pl.pallas_call(run, out_shape=outs, in_specs=specs, out_specs=[pl.BlockSp...  110 us
    ppermute x24, starting transfers between devices, swap_mask(): return lax.ppermute(value, 'dp', [(i, i ^ mask) for i in range(CHUNKS)])  36.8 us
    ppermute x24, waiting for transfers between devices, swap_mask(): return lax.ppermute(value, 'dp', [(i, i ^ mask) for i in range(CHUNKS)])  22.5 us
    unnamed x98, local copies, waits for them, and re-layouts  14.5 us
    ppermute x19, waiting for transfers between devices, swap_core(): return lax.ppermute(value, 'mp', CORE_PAIRS)  6.17 us
    ppermute x5, starting transfers between devices, swap_chip(): return lax.ppermute(value, 'mp', CHIP_PAIRS)  4.92 us
    ppermute x5, waiting for transfers between devices, swap_chip(): return lax.ppermute(value, 'mp', CHIP_PAIRS)  4.65 us
  transfers between devices with their start and end apart: 48, of which 26 were waited for; matrix products, arithmetic and copies ran while one was open for 1% of the time, Pallas kernels for 46%

profile of v5, /device:TPU:0, one launch (start us, length us, event | category | flops | bytes accessed | tf_op | source)
XLA Modules:
  0.0 211.1 jit_solution(2643890662300332721)
XLA Ops:
  4.8 4.2 %collective-permute-start.2 = (bf16[112,768]{1,0:T(8,128)(2,1)S(1)}, bf16[112,768]{1,0:T(8,128)(2,1)S(1)}, u32[]{:S(2)}, u32[]{:S(2)}) collective-permute-start(bf16[112,768]{1,0:T(8,128)(2,1)S(1)} %get-tuple-element.229), channel_id=1, source_target_pairs={{0,16},{4,20},{8,24},{12,28},{16,0},{20,4},{24,8},{28,12},{1,17},{... | collective-permute-start | bytes 516104 | tf_op jit(solution)/shard_map/ppermute | solution.py:38
  12.8 4.2 %stats.1.refs_2_.refs_8_ = f32[1024,256]{1,0:T(8,128)} custom-call(s32[2]{0:T(128)} %pad_add_fusion.refs_0_, bf16[1024,768]{1,0:T(8,128)(2,1)} %refs_1_.7), custom_call_target="tpu_custom_call" | custom-call | bytes 1024 | tf_op jit(solution)/shard_map/stats/pallas_call | solution.py:54
  20.8 1.7 collective-permute-start.3
  22.6 7.5 %collective-permute-done.3 = bf16[112,768]{1,0:T(8,128)(2,1)S(1)} collective-permute-done((bf16[112,768]{1,0:T(8,128)(2,1)S(1)}, bf16[112,768]{1,0:T(8,128)(2,1)S(1)}, u32[]{:S(2)}, u32[]{:S(2)}) %collective-permute-start.3) | collective-permute-done | bytes 172064 | tf_op jit(solution)/shard_map/ppermute | solution.py:38
  30.3 2.2 %collective-permute-start.11 = (bf16[96,1536]{1,0:T(8,128)(2,1)S(1)}, bf16[96,1536]{1,0:T(8,128)(2,1)S(1)}, u32[]{:S(2)}, u32[]{:S(2)}) collective-permute-start(bf16[96,1536]{1,0:T(8,128)(2,1)S(1)} %pad_maximum_fusion.refs_3_), channel_id=1, source_target_pairs={{0,16},{4,20},{8,24},{12,28},{16,0},{20,4},{24,8},{28,12},{1,17},{... | collective-permute-start | bytes 884744 | tf_op jit(solution)/shard_map/ppermute | solution.py:38
  32.6 2.7 %collective-permute-start.10 = (bf16[96,1536]{1,0:T(8,128)(2,1)S(1)}, bf16[96,1536]{1,0:T(8,128)(2,1)S(1)}, u32[]{:S(2)}, u32[]{:S(2)}) collective-permute-start(bf16[96,1536]{1,0:T(8,128)(2,1)S(1)} %pad_maximum_fusion.refs_3_), channel_id=1, source_target_pairs={{0,8},{4,12},{8,0},{12,4},{16,24},{20,28},{24,16},{28,20},{1,9},{5... | collective-permute-start | bytes 884744 | tf_op jit(solution)/shard_map/ppermute | solution.py:38
  37.9 8.0 %project.1 = (bf16[6,512,64]{2,1,0:T(8,128)(2,1)}, bf16[6,1024,64]{2,1,0:T(8,128)(2,1)}, bf16[6,1024,64]{2,1,0:T(8,128)(2,1)}, bf16[768,384]{1,0:T(8,128)(2,1)},...) custom-call(s32[2]{0:T(128)} %pad_add_fusion.refs_0_, ...), custom_call_target="tpu_custom_call" | custom-call | flops 8000000000 | bytes 1024 | tf_op jit(solution)/shard_map/project/pallas_call | solution.py:54
  50.7 1.7 collective-permute-start.12
  52.4 13.0 %attend.1 = (bf16[512,768]{1,0:T(8,128)(2,1)}, bf16[512,384]{1,0:T(8,128)(2,1)}, bf16[6,128,2560]{2,1,0:T(8,128)(2,1)}) custom-call(s32[2]{0:T(128)} %pad_add_fusion.refs_0_, bf16[6,512,64]{2,1,0:T(8,128)(2,1)} %get-tuple-element.102.refs_1_.refs_9_, bf16[6,1024,64]{2,1,0:T(8,128)(2,1)} %get-tuple-element.103.refs_2_.refs_10_, ...), custom_call_target="tpu_custom_call" | custom-call | flops 16000000000 | bytes 1024 | tf_op jit(solution)/shard_map/attend/pallas_call | solution.py:54
  74.1 7.3 %mlp_pre.1 = (bf16[768,1536]{1,0:T(8,128)(2,1)}, bf16[768,1536]{1,0:T(8,128)(2,1)}, bf16[512,768]{1,0:T(8,128)(2,1)}, bf16[512,1536]{1,0:T(8,128)(2,1)}) custom-call(s32[2]{0:T(128)} %pad_add_fusion.refs_0_, s32[1,1024]{1,0:T(1,128)} %bitcast.50, bf16[1024,768]{1,0:T(8,128)(2,1)} %refs_2_.1, bf16[96,1536]{1,0:T(8,128)(2,1)} %copy-done, ...), custom_call_target="tpu_custom_call" | custom-call | bytes 1024 | tf_op jit(solution)/shard_map/mlp_pre/pallas_call | solution.py:54
  81.3 2.3 %collective-permute-done.8.refs_3_ = bf16[512,768]{1,0:T(8,128)(2,1)S(1)} collective-permute-done((bf16[512,768]{1,0:T(8,128)(2,1)}, bf16[512,768]{1,0:T(8,128)(2,1)S(1)}, u32[]{:S(2)}, u32[]{:S(2)}) %collective-permute-start.8) | collective-permute-done | bytes 786464 | tf_op jit(solution)/shard_map/ppermute | solution.py:34
  84.5 11.6 %mlp.1 = (bf16[512,768]{1,0:T(8,128)(2,1)}, bf16[512,1536]{1,0:T(8,128)(2,1)}, bf16[512,1536]{1,0:T(8,128)(2,1)}, bf16[512,768]{1,0:T(8,128)(2,1)}, f32[512,768]{1,0:T(8,128)}, /*index=5*/f32[512,256]{1,0:T(8,128)}) custom-call(s32[2]{0:T(128)} %pad_add_fusion.refs_0_, bf16[1024,768]{1,0:T(8,128)(2,1)} %refs_1_.7, ...), custom_call_target="tpu_custom_call" | custom-call | flops 10000000000 | bytes 1024 | tf_op jit(solution)/shard_map/mlp/pallas_call | solution.py:54
  97.6 8.6 %mlp_grad.1 = (bf16[512,768]{1,0:T(8,128)(2,1)}, bf16[8,96,1536]{2,1,0:T(8,128)(2,1)}, bf16[8,96,384]{2,1,0:T(8,128)(2,1)}, bf16[8,96,384]{2,1,0:T(8,128)(2,1)},...) custom-call(s32[2]{0:T(128)} %pad_add_fusion.refs_0_, ...), custom_call_target="tpu_custom_call" | custom-call | flops 8999999488 | bytes 1024 | tf_op jit(solution)/shard_map/mlp_grad/pallas_call | solution.py:54
  111.8 4.4 %scatter_first.2 = (f32[384,768]{1,0:T(8,128)}, bf16[384,768]{1,0:T(8,128)(2,1)}, f32[384,768]{1,0:T(8,128)}, bf16[384,768]{1,0:T(8,128)(2,1)}) custom-call(s32[2]{0:T(128)} %pad_add_fusion.refs_0_, bf16[8,96,1536]{2,1,0:T(8,128)(2,1)} %get-tuple-element.133.refs_1_, bf16[8,96,384]{2,1,0:T(8,128)(2,1)} %copy-done.4, bf16[8,96,384]{2,1,0:T(8,128)(2,1)} %copy-done.5, ...), custom_call_target="tpu_custom_call" | custom-call | bytes 1024 | tf_op jit(solution)/shard_map/scatter_first/pallas_call | solution.py:54
  118.5 14.8 %attend_back.1 = (f32[512,768]{1,0:T(8,128)}, bf16[512,768]{1,0:T(8,128)(2,1)}, f32[8,768]{1,0:T(8,128)}, bf16[512,384]{1,0:T(8,128)(2,1)}, f32[768,512]{1,0:T(8...) custom-call(s32[2]{0:T(128)} %pad_add_fusion.refs_0_, f32[512,768]{1,0:T(8,128)} %get-tuple-element.123.refs_1_.refs_8_, ...), custom_call_target="tpu_custom_call" | custom-call | flops 17999998976 | bytes 1024 | tf_op jit(solution)/shard_map/attend_back/pallas_call | solution.py:54
  135.1 3.2 %scatter_second.2 = (f32[192,768]{1,0:T(8,128)}, bf16[192,768]{1,0:T(8,128)(2,1)}, f32[192,768]{1,0:T(8,128)}, bf16[192,768]{1,0:T(8,128)(2,1)}) custom-call(s32[2]{0:T(128)} %pad_add_fusion.refs_0_, f32[384,768]{1,0:T(8,128)} %get-tuple-element.146.refs_1_, bf16[384,768]{1,0:T(8,128)(2,1)} %copy-done.2, f32[384,768]{1,0:T(8,128)} %get-tuple-element.147.refs_3_, ...), custom_call_target="tpu_custom_call" | custom-call | bytes 1024 | tf_op jit(solution)/shard_map/scatter_second/pallas_call | solution.py:54
  141.8 4.6 %first_grad.1 = (bf16[512,768]{1,0:T(8,128)(2,1)}, bf16[768,512]{1,0:T(8,128)(2,1)}) custom-call(s32[2]{0:T(128)} %pad_add_fusion.refs_0_, bf16[512,384]{1,0:T(8,128)(2,1)} %get-tuple-element.139.refs_5_.refs_1_.refs_2_, f32[768,512]{1,0:T(8,128)} %get-tuple-element.140.refs_2_, bf16[384,512]{1,0:T(8,128)(2,1)} %copy-done.11, bf16[384,512]{1,0:T(8,128)(2,1)} %copy-done.12, ...), custom_call_target="tpu_custom_call" | custom-call | bytes 1024 | tf_op jit(solution)/shard_map/first_grad/pallas_call | solution.py:54
  148.8 6.7 %qkv_grad.1 = (bf16[8,96,768]{2,1,0:T(8,128)(2,1)}, bf16[8,96,384]{2,1,0:T(8,128)(2,1)}, bf16[8,96,384]{2,1,0:T(8,128)(2,1)}, bf16[16,768]{1,0:T(8,128)(2,1)}, bf16[16,768]{1,0:T(8,128)(2,1)}) custom-call(s32[2]{0:T(128)} %pad_add_fusion.refs_0_, bf16[512,768]{1,0:T(8,128)(2,1)} %get-tuple-element.153.refs_1_, ...), custom_call_target="tpu_custom_call" | custom-call | flops 7000000000 | bytes 1024 | tf_op jit(solution)/shard_map/qkv_grad/pallas_call | solution.py:54
  156.2 2.4 %scatter_third.2 = (f32[96,1536]{1,0:T(8,128)}, bf16[96,1536]{1,0:T(8,128)(2,1)}) custom-call(s32[2]{0:T(128)} %pad_add_fusion.refs_0_, f32[192,768]{1,0:T(8,128)} %get-tuple-element.150.refs_8_.refs_1_, bf16[192,768]{1,0:T(8,128)(2,1)} %copy-done.20, f32[192,768]{1,0:T(8,128)} %get-tuple-element.165.refs_3_, bf16[192,768]{1,0:T(8,128)(2,1)} %copy-done.22, ...), custom_call_target="tpu_custom_call" | custom-call | bytes 1024 | tf_op jit(solution)/shard_map/scatter_third/pallas_call | solution.py:54
  158.6 2.3 %collective-permute-start.43 = (bf16[96,1536]{1,0:T(8,128)(2,1)}, bf16[96,1536]{1,0:T(8,128)(2,1)S(1)}, u32[]{:S(2)}, u32[]{:S(2)}) collective-permute-start(bf16[96,1536]{1,0:T(8,128)(2,1)} %get-tuple-element.171), channel_id=1, source_target_pairs={{0,16},{4,20},{8,24},{12,28},{16,0},{20,4},{24,8},{28,12},{1,17},{... | collective-permute-start | bytes 884744 | tf_op jit(solution)/shard_map/ppermute | solution.py:38
  161.9 3.1 %scatter_first.3 = (f32[400,384]{1,0:T(8,128)}, bf16[400,384]{1,0:T(8,128)(2,1)}, f32[400,384]{1,0:T(8,128)}, bf16[400,384]{1,0:T(8,128)(2,1)}) custom-call(s32[2]{0:T(128)} %pad_add_fusion.refs_0_, bf16[8,96,768]{2,1,0:T(8,128)(2,1)} %get-tuple-element.160.refs_5_.refs_1_, bf16[8,96,384]{2,1,0:T(8,128)(2,1)} %copy-done.8, bf16[8,96,384]{2,1,0:T(8,128)(2,1)} %copy-done.9, ...), custom_call_target="tpu_custom_call" | custom-call | bytes 1024 | tf_op jit(solution)/shard_map/scatter_first/pallas_call | solution.py:54
  168.9 6.5 %final.1.refs_5_.refs_1_ = bf16[1024,768]{1,0:T(8,128)(2,1)} custom-call(s32[2]{0:T(128)} %pad_add_fusion.refs_0_, bf16[1024,768]{1,0:T(8,128)(2,1)} %refs_1_.7, f32[1024,256]{1,0:T(8,128)} %stats.1.refs_2_.refs_8_, bf16[512,768]{1,0:T(8,128)(2,1)} %get-tuple-element.151.refs_6_.refs_3_, bf16[512,768]{1,0:T(8,128)(2,1)} %copy-done.37, ...), custom_call_target="tpu_custom_call" | custom-call | flops 7000000000 | bytes 1024 | tf_op jit(solution)/shard_map/final/pallas_call | solution.py:54
  175.5 5.8 %collective-permute-done.42.refs_4_ = bf16[400,384]{1,0:T(8,128)(2,1)S(1)} collective-permute-done((bf16[400,384]{1,0:T(8,128)(2,1)}, bf16[400,384]{1,0:T(8,128)(2,1)S(1)}, u32[]{:S(2)}, u32[]{:S(2)}) %collective-permute-start.42) | collective-permute-done | bytes 307232 | tf_op jit(solution)/shard_map/ppermute | solution.py:38
  182.0 2.4 %scatter_second.3 = (f32[208,384]{1,0:T(8,128)}, bf16[208,384]{1,0:T(8,128)(2,1)}, f32[208,384]{1,0:T(8,128)}, bf16[208,384]{1,0:T(8,128)(2,1)}) custom-call(s32[2]{0:T(128)} %pad_add_fusion.refs_0_, f32[400,384]{1,0:T(8,128)} %get-tuple-element.168.refs_1_, bf16[400,384]{1,0:T(8,128)(2,1)} %copy-done.39, f32[400,384]{1,0:T(8,128)} %get-tuple-element.169.refs_3_, ...), custom_call_target="tpu_custom_call" | custom-call | flops 15000000512 | bytes 1024 | tf_op jit(solution)/shard_map/scatter_second/pallas_call | solution.py:54
  185.1 2.2 %scatter_big.1 = (f32[96,768]{1,0:T(8,128)}, f32[768,96]{1,0:T(8,128)}) custom-call(s32[2]{0:T(128)} %pad_add_fusion.refs_0_, f32[96,1536]{1,0:T(8,128)} %get-tuple-element.166.refs_6_.refs_1_, bf16[96,1536]{1,0:T(8,128)(2,1)} %copy-done.41), custom_call_target="tpu_custom_call" | custom-call | flops 15000000512 | bytes 1024 | tf_op jit(solution)/shard_map/scatter_big/pallas_call | solution.py:54
  187.3 2.7 %collective-permute-done.44.refs_2_ = bf16[208,384]{1,0:T(8,128)(2,1)S(1)} collective-permute-done((bf16[208,384]{1,0:T(8,128)(2,1)}, bf16[208,384]{1,0:T(8,128)(2,1)S(1)}, u32[]{:S(2)}, u32[]{:S(2)}) %collective-permute-start.44) | collective-permute-done | bytes 159776 | tf_op jit(solution)/shard_map/ppermute | solution.py:38
  190.7 2.0 scatter_third.3
  192.7 2.5 %collective-permute-start.46 = (bf16[112,768]{1,0:T(8,128)(2,1)}, bf16[112,768]{1,0:T(8,128)(2,1)S(1)}, u32[]{:S(2)}, u32[]{:S(2)}) collective-permute-start(bf16[112,768]{1,0:T(8,128)(2,1)} %get-tuple-element.179), channel_id=1, source_target_pairs={{0,16},{4,20},{8,24},{12,28},{16,0},{20,4},{24,8},{28,12},{1,17},{... | collective-permute-start | bytes 516104 | tf_op jit(solution)/shard_map/ppermute | solution.py:38
  196.3 3.7 %merge.1 = (bf16[1024,768]{1,0:T(8,128)(2,1)}, bf16[1024,768]{1,0:T(8,128)(2,1)}) custom-call(s32[2]{0:T(128)} %pad_add_fusion.refs_0_, bf16[1024,768]{1,0:T(8,128)(2,1)} %final.1.refs_5_.refs_1_, bf16[1024,768]{1,0:T(8,128)(2,1)} %copy-done.34, f32[112,768]{1,0:T(8,128)} %get-tuple-element.176.refs_3_.refs_1_), custom_call_target="tpu_custom_call" | custom-call | flops 4000000000 | bytes 1024 | tf_op jit(solution)/shard_map/merge/pallas_call | solution.py:54
  200.0 2.1 collective-permute-done.46.refs_2_
  202.8 1.9 scatter_small.1
  206.5 2.3 %collective-permute-done.47 = bf16[16,768]{1,0:T(8,128)(2,1)S(1)} collective-permute-done((bf16[16,768]{1,0:T(8,128)(2,1)}, bf16[16,768]{1,0:T(8,128)(2,1)S(1)}, u32[]{:S(2)}, u32[]{:S(2)}) %collective-permute-start.47) | collective-permute-done | bytes 24608 | tf_op jit(solution)/shard_map/ppermute | solution.py:34
  (204 shorter events, 59.6 us)
Async XLA Ops:
  4.8 12.4 %collective-permute-start.2 = (bf16[112,768]{1,0:T(8,128)(2,1)S(1)}, bf16[112,768]{1,0:T(8,128)(2,1)S(1)}, u32[]{:S(2)}, u32[]{:S(2)}) collective-permute-start(bf16[112,768]{1,0:T(8,128)(2,1)S(1)} %get-tuple-element.229), channel_id=1, source_target_pairs={{0,16},{4,20},{8,24},{12,28},{16,0},{20,4},{24,8},{28,12},{1,17},{... | collective-permute-start | bytes 516104 | tf_op jit(solution)/shard_map/ppermute | solution.py:38
  9.0 8.3 %collective-permute-start.1 = (bf16[112,768]{1,0:T(8,128)(2,1)S(1)}, bf16[112,768]{1,0:T(8,128)(2,1)S(1)}, u32[]{:S(2)}, u32[]{:S(2)}) collective-permute-start(bf16[112,768]{1,0:T(8,128)(2,1)S(1)} %get-tuple-element.229), channel_id=1, source_target_pairs={{0,8},{4,12},{8,0},{12,4},{16,24},{20,28},{24,16},{28,20},{1,9},{5... | collective-permute-start | bytes 516104 | tf_op jit(solution)/shard_map/ppermute | solution.py:38
  10.7 11.8 %collective-permute-start = (bf16[112,768]{1,0:T(8,128)(2,1)S(1)}, bf16[112,768]{1,0:T(8,128)(2,1)S(1)}, u32[]{:S(2)}, u32[]{:S(2)}) collective-permute-start(bf16[112,768]{1,0:T(8,128)(2,1)S(1)} %get-tuple-element.229), channel_id=1, source_target_pairs={{0,4},{4,0},{8,12},{12,8},{16,20},{20,16},{24,28},{28,24},{1,5},{5... | collective-permute-start | bytes 516104 | tf_op jit(solution)/shard_map/ppermute | solution.py:38
  17.3 12.8 %collective-permute-start.4 = (bf16[112,768]{1,0:T(8,128)(2,1)S(1)}, bf16[112,768]{1,0:T(8,128)(2,1)S(1)}, u32[]{:S(2)}, u32[]{:S(2)}) collective-permute-start(bf16[112,768]{1,0:T(8,128)(2,1)S(1)} %collective-permute-done.2), channel_id=1, source_target_pairs={{0,4},{4,0},{8,12},{12,8},{16,20},{20,16},{24,28},{28,24},{1,5},{5... | collective-permute-start | bytes 516104 | tf_op jit(solution)/shard_map/ppermute | solution.py:38
  19.0 11.1 %collective-permute-start.5 = (bf16[112,768]{1,0:T(8,128)(2,1)S(1)}, bf16[112,768]{1,0:T(8,128)(2,1)S(1)}, u32[]{:S(2)}, u32[]{:S(2)}) collective-permute-start(bf16[112,768]{1,0:T(8,128)(2,1)S(1)} %collective-permute-done.2), channel_id=1, source_target_pairs={{0,8},{4,12},{8,0},{12,4},{16,24},{20,28},{24,16},{28,20},{1,9},{5... | collective-permute-start | bytes 516104 | tf_op jit(solution)/shard_map/ppermute | solution.py:38
  20.5 9.7 %collective-permute-start.6 = (bf16[112,768]{1,0:T(8,128)(2,1)S(1)}, bf16[112,768]{1,0:T(8,128)(2,1)S(1)}, u32[]{:S(2)}, u32[]{:S(2)}) collective-permute-start(bf16[112,768]{1,0:T(8,128)(2,1)S(1)} %collective-permute-done.2), channel_id=1, source_target_pairs={{0,12},{4,8},{8,4},{12,0},{16,28},{20,24},{24,20},{28,16},{1,13},{... | collective-permute-start | bytes 516104 | tf_op jit(solution)/shard_map/ppermute | solution.py:38
  20.8 9.3 %collective-permute-start.3 = (bf16[112,768]{1,0:T(8,128)(2,1)S(1)}, bf16[112,768]{1,0:T(8,128)(2,1)S(1)}, u32[]{:S(2)}, u32[]{:S(2)}) collective-permute-start(bf16[112,768]{1,0:T(8,128)(2,1)S(1)} %collective-permute-done.1), channel_id=1, source_target_pairs={{0,4},{4,0},{8,12},{12,8},{16,20},{20,16},{24,28},{28,24},{1,5},{5... | collective-permute-start | bytes 516104 | tf_op jit(solution)/shard_map/ppermute | solution.py:38
  30.2 6.6 %collective-permute-start.7 = (bf16[8,112,768]{2,1,0:T(8,128)(2,1)S(1)}, bf16[8,112,768]{2,1,0:T(8,128)(2,1)S(1)}, u32[]{:S(2)}, u32[]{:S(2)}) collective-permute-start(bf16[8,112,768]{2,1,0:T(8,128)(2,1)S(1)} %bitcast_dynamic-update-slice_fusion.refs_3_), channel_id=1, source_target_pairs={{0,1},{1,0},{2,3},{3,2},{4,5},{5,4},{6,7},{7,6},{8,9},{9,8},{10,11... | collective-permute-start | bytes 4128776 | tf_op jit(solution)/shard_map/ppermute | solution.py:30
  30.3 16.8 %collective-permute-start.11 = (bf16[96,1536]{1,0:T(8,128)(2,1)S(1)}, bf16[96,1536]{1,0:T(8,128)(2,1)S(1)}, u32[]{:S(2)}, u32[]{:S(2)}) collective-permute-start(bf16[96,1536]{1,0:T(8,128)(2,1)S(1)} %pad_maximum_fusion.refs_3_), channel_id=1, source_target_pairs={{0,16},{4,20},{8,24},{12,28},{16,0},{20,4},{24,8},{28,12},{1,17},{... | collective-permute-start | bytes 884744 | tf_op jit(solution)/shard_map/ppermute | solution.py:38
  32.6 14.6 %collective-permute-start.10 = (bf16[96,1536]{1,0:T(8,128)(2,1)S(1)}, bf16[96,1536]{1,0:T(8,128)(2,1)S(1)}, u32[]{:S(2)}, u32[]{:S(2)}) collective-permute-start(bf16[96,1536]{1,0:T(8,128)(2,1)S(1)} %pad_maximum_fusion.refs_3_), channel_id=1, source_target_pairs={{0,8},{4,12},{8,0},{12,4},{16,24},{20,28},{24,16},{28,20},{1,9},{5... | collective-permute-start | bytes 884744 | tf_op jit(solution)/shard_map/ppermute | solution.py:38
  35.2 30.2 %collective-permute-start.9 = (bf16[96,1536]{1,0:T(8,128)(2,1)S(1)}, bf16[96,1536]{1,0:T(8,128)(2,1)S(1)}, u32[]{:S(2)}, u32[]{:S(2)}) collective-permute-start(bf16[96,1536]{1,0:T(8,128)(2,1)S(1)} %pad_maximum_fusion.refs_3_), channel_id=1, source_target_pairs={{0,4},{4,0},{8,12},{12,8},{16,20},{20,16},{24,28},{28,24},{1,5},{5... | collective-permute-start | bytes 884744 | tf_op jit(solution)/shard_map/ppermute | solution.py:38
  47.2 21.2 %collective-permute-start.13 = (bf16[96,1536]{1,0:T(8,128)(2,1)S(1)}, bf16[96,1536]{1,0:T(8,128)(2,1)S(1)}, u32[]{:S(2)}, u32[]{:S(2)}) collective-permute-start(bf16[96,1536]{1,0:T(8,128)(2,1)S(1)} %collective-permute-done.11.refs_7_), channel_id=1, source_target_pairs={{0,4},{4,0},{8,12},{12,8},{16,20},{20,16},{24,28},{28,24},{1,5},{5... | collective-permute-start | bytes 884744 | tf_op jit(solution)/shard_map/ppermute | solution.py:38
  48.9 19.5 %collective-permute-start.14 = (bf16[96,1536]{1,0:T(8,128)(2,1)S(1)}, bf16[96,1536]{1,0:T(8,128)(2,1)S(1)}, u32[]{:S(2)}, u32[]{:S(2)}) collective-permute-start(bf16[96,1536]{1,0:T(8,128)(2,1)S(1)} %collective-permute-done.11.refs_7_), channel_id=1, source_target_pairs={{0,8},{4,12},{8,0},{12,4},{16,24},{20,28},{24,16},{28,20},{1,9},{5... | collective-permute-start | bytes 884744 | tf_op jit(solution)/shard_map/ppermute | solution.py:38
  49.8 18.6 %collective-permute-start.15 = (bf16[96,1536]{1,0:T(8,128)(2,1)S(1)}, bf16[96,1536]{1,0:T(8,128)(2,1)S(1)}, u32[]{:S(2)}, u32[]{:S(2)}) collective-permute-start(bf16[96,1536]{1,0:T(8,128)(2,1)S(1)} %collective-permute-done.11.refs_7_), channel_id=1, source_target_pairs={{0,12},{4,8},{8,4},{12,0},{16,28},{20,24},{24,20},{28,16},{1,13},{... | collective-permute-start | bytes 884744 | tf_op jit(solution)/shard_map/ppermute | solution.py:38
  50.7 17.7 %collective-permute-start.12 = (bf16[96,1536]{1,0:T(8,128)(2,1)S(1)}, bf16[96,1536]{1,0:T(8,128)(2,1)S(1)}, u32[]{:S(2)}, u32[]{:S(2)}) collective-permute-start(bf16[96,1536]{1,0:T(8,128)(2,1)S(1)} %collective-permute-done.10.refs_5_), channel_id=1, source_target_pairs={{0,4},{4,0},{8,12},{12,8},{16,20},{20,16},{24,28},{28,24},{1,5},{5... | collective-permute-start | bytes 884744 | tf_op jit(solution)/shard_map/ppermute | solution.py:38
  65.4 18.2 %collective-permute-start.8 = (bf16[512,768]{1,0:T(8,128)(2,1)}, bf16[512,768]{1,0:T(8,128)(2,1)S(1)}, u32[]{:S(2)}, u32[]{:S(2)}) collective-permute-start(bf16[512,768]{1,0:T(8,128)(2,1)} %get-tuple-element.106.refs_2_), channel_id=1, source_target_pairs={{0,2},{2,0},{1,3},{3,1},{4,6},{6,4},{5,7},{7,5},{8,10},{10,8},{9,1... | collective-permute-start | bytes 2359304 | tf_op jit(solution)/shard_map/ppermute | solution.py:34
  96.1 21.5 %collective-permute-start.24 = (bf16[512,768]{1,0:T(8,128)(2,1)}, bf16[512,768]{1,0:T(8,128)(2,1)S(1)}, u32[]{:S(2)}, u32[]{:S(2)}) collective-permute-start(bf16[512,768]{1,0:T(8,128)(2,1)} %get-tuple-element.126.refs_4_), channel_id=1, source_target_pairs={{0,2},{2,0},{1,3},{3,1},{4,6},{6,4},{5,7},{7,5},{8,10},{10,8},{9,1... | collective-permute-start | bytes 2359304 | tf_op jit(solution)/shard_map/ppermute | solution.py:34
  108.5 25.3 %collective-permute-start.33 = (bf16[512,768]{1,0:T(8,128)(2,1)}, bf16[512,768]{1,0:T(8,128)(2,1)S(1)}, u32[]{:S(2)}, u32[]{:S(2)}) collective-permute-start(bf16[512,768]{1,0:T(8,128)(2,1)} %get-tuple-element.149.refs_9_), channel_id=1, source_target_pairs={{0,2},{2,0},{1,3},{3,1},{4,6},{6,4},{5,7},{7,5},{8,10},{10,8},{9,1... | collective-permute-start | bytes 2359304 | tf_op jit(solution)/shard_map/ppermute | solution.py:34
  116.2 17.7 %collective-permute-start.31 = (bf16[384,768]{1,0:T(8,128)(2,1)}, bf16[384,768]{1,0:T(8,128)(2,1)S(1)}, u32[]{:S(2)}, u32[]{:S(2)}) collective-permute-start(bf16[384,768]{1,0:T(8,128)(2,1)} %get-tuple-element.138.refs_13_), channel_id=1, source_target_pairs={{0,4},{4,0},{8,12},{12,8},{16,20},{20,16},{24,28},{28,24},{1,5},{5... | collective-permute-start | bytes 1769480 | tf_op jit(solution)/shard_map/ppermute | solution.py:38
  116.5 17.3 %collective-permute-start.32 = (bf16[384,768]{1,0:T(8,128)(2,1)}, bf16[384,768]{1,0:T(8,128)(2,1)S(1)}, u32[]{:S(2)}, u32[]{:S(2)}) collective-permute-start(bf16[384,768]{1,0:T(8,128)(2,1)} %get-tuple-element.148), channel_id=1, source_target_pairs={{0,8},{4,12},{8,0},{12,4},{16,24},{20,28},{24,16},{28,20},{1,9},{5... | collective-permute-start | bytes 1769480 | tf_op jit(solution)/shard_map/ppermute | solution.py:38
  133.3 7.6 %collective-permute-start.29 = (bf16[384,512]{1,0:T(8,128)(2,1)}, bf16[384,512]{1,0:T(8,128)(2,1)S(1)}, u32[]{:S(2)}, u32[]{:S(2)}) collective-permute-start(bf16[384,512]{1,0:T(8,128)(2,1)} %get-tuple-element.141), channel_id=1, source_target_pairs={{0,1},{1,0},{2,3},{3,2},{4,5},{5,4},{6,7},{7,6},{8,9},{9,8},{10,11... | collective-permute-start | bytes 1179656 | tf_op jit(solution)/shard_map/ppermute | solution.py:30
  133.3 7.6 %collective-permute-start.30 = (bf16[384,512]{1,0:T(8,128)(2,1)}, bf16[384,512]{1,0:T(8,128)(2,1)S(1)}, u32[]{:S(2)}, u32[]{:S(2)}) collective-permute-start(bf16[384,512]{1,0:T(8,128)(2,1)} %get-tuple-element.142), channel_id=1, source_target_pairs={{0,1},{1,0},{2,3},{3,2},{4,5},{5,4},{6,7},{7,6},{8,9},{9,8},{10,11... | collective-permute-start | bytes 1179656 | tf_op jit(solution)/shard_map/ppermute | solution.py:30
  138.3 9.2 %collective-permute-start.35 = (bf16[192,768]{1,0:T(8,128)(2,1)}, bf16[192,768]{1,0:T(8,128)(2,1)S(1)}, u32[]{:S(2)}, u32[]{:S(2)}) collective-permute-start(bf16[192,768]{1,0:T(8,128)(2,1)} %get-tuple-element.158), channel_id=1, source_target_pairs={{0,8},{4,12},{8,0},{12,4},{16,24},{20,28},{24,16},{28,20},{1,9},{5... | collective-permute-start | bytes 884744 | tf_op jit(solution)/shard_map/ppermute | solution.py:38
  139.2 8.9 %collective-permute-start.36 = (bf16[192,768]{1,0:T(8,128)(2,1)}, bf16[192,768]{1,0:T(8,128)(2,1)S(1)}, u32[]{:S(2)}, u32[]{:S(2)}) collective-permute-start(bf16[192,768]{1,0:T(8,128)(2,1)} %get-tuple-element.159), channel_id=1, source_target_pairs={{0,4},{4,0},{8,12},{12,8},{16,20},{20,16},{24,28},{28,24},{1,5},{5... | collective-permute-start | bytes 884744 | tf_op jit(solution)/shard_map/ppermute | solution.py:38
  146.3 21.7 %collective-permute-start.34 = (bf16[512,768]{1,0:T(8,128)(2,1)}, bf16[512,768]{1,0:T(8,128)(2,1)S(1)}, u32[]{:S(2)}, u32[]{:S(2)}) collective-permute-start(bf16[512,768]{1,0:T(8,128)(2,1)} %get-tuple-element.151.refs_6_.refs_3_), channel_id=1, source_target_pairs={{0,2},{2,0},{1,3},{3,1},{4,6},{6,4},{5,7},{7,5},{8,10},{10,8},{9,1... | collective-permute-start | bytes 2359304 | tf_op jit(solution)/shard_map/ppermute | solution.py:34
  158.6 16.9 %collective-permute-start.43 = (bf16[96,1536]{1,0:T(8,128)(2,1)}, bf16[96,1536]{1,0:T(8,128)(2,1)S(1)}, u32[]{:S(2)}, u32[]{:S(2)}) collective-permute-start(bf16[96,1536]{1,0:T(8,128)(2,1)} %get-tuple-element.171), channel_id=1, source_target_pairs={{0,16},{4,20},{8,24},{12,28},{16,0},{20,4},{24,8},{28,12},{1,17},{... | collective-permute-start | bytes 884744 | tf_op jit(solution)/shard_map/ppermute | solution.py:38
  164.9 10.5 %collective-permute-start.41 = (bf16[400,384]{1,0:T(8,128)(2,1)}, bf16[400,384]{1,0:T(8,128)(2,1)S(1)}, u32[]{:S(2)}, u32[]{:S(2)}) collective-permute-start(bf16[400,384]{1,0:T(8,128)(2,1)} %get-tuple-element.167.refs_11_), channel_id=1, source_target_pairs={{0,4},{4,0},{8,12},{12,8},{16,20},{20,16},{24,28},{28,24},{1,5},{5... | collective-permute-start | bytes 921608 | tf_op jit(solution)/shard_map/ppermute | solution.py:38
  166.5 14.8 %collective-permute-start.42 = (bf16[400,384]{1,0:T(8,128)(2,1)}, bf16[400,384]{1,0:T(8,128)(2,1)S(1)}, u32[]{:S(2)}, u32[]{:S(2)}) collective-permute-start(bf16[400,384]{1,0:T(8,128)(2,1)} %get-tuple-element.170), channel_id=1, source_target_pairs={{0,8},{4,12},{8,0},{12,4},{16,24},{20,28},{24,16},{28,20},{1,9},{5... | collective-permute-start | bytes 921608 | tf_op jit(solution)/shard_map/ppermute | solution.py:38
  175.4 19.7 %collective-permute-start.40 = (bf16[1024,768]{1,0:T(8,128)(2,1)}, bf16[1024,768]{1,0:T(8,128)(2,1)S(1)}, u32[]{:S(2)}, u32[]{:S(2)}) collective-permute-start(bf16[1024,768]{1,0:T(8,128)(2,1)} %final.1.refs_5_.refs_1_), channel_id=1, source_target_pairs={{0,1},{1,0},{2,3},{3,2},{4,5},{5,4},{6,7},{7,6},{8,9},{9,8},{10,11... | collective-permute-start | bytes 4718600 | tf_op jit(solution)/shard_map/ppermute | solution.py:30
  184.4 5.5 %collective-permute-start.44 = (bf16[208,384]{1,0:T(8,128)(2,1)}, bf16[208,384]{1,0:T(8,128)(2,1)S(1)}, u32[]{:S(2)}, u32[]{:S(2)}) collective-permute-start(bf16[208,384]{1,0:T(8,128)(2,1)} %get-tuple-element.173), channel_id=1, source_target_pairs={{0,8},{4,12},{8,0},{12,4},{16,24},{20,28},{24,16},{28,20},{1,9},{5... | collective-permute-start | bytes 479240 | tf_op jit(solution)/shard_map/ppermute | solution.py:38
  184.4 5.6 %collective-permute-start.45 = (bf16[208,384]{1,0:T(8,128)(2,1)}, bf16[208,384]{1,0:T(8,128)(2,1)S(1)}, u32[]{:S(2)}, u32[]{:S(2)}) collective-permute-start(bf16[208,384]{1,0:T(8,128)(2,1)} %get-tuple-element.175), channel_id=1, source_target_pairs={{0,4},{4,0},{8,12},{12,8},{16,20},{20,16},{24,28},{28,24},{1,5},{5... | collective-permute-start | bytes 479240 | tf_op jit(solution)/shard_map/ppermute | solution.py:38
  192.7 9.4 %collective-permute-start.46 = (bf16[112,768]{1,0:T(8,128)(2,1)}, bf16[112,768]{1,0:T(8,128)(2,1)S(1)}, u32[]{:S(2)}, u32[]{:S(2)}) collective-permute-start(bf16[112,768]{1,0:T(8,128)(2,1)} %get-tuple-element.179), channel_id=1, source_target_pairs={{0,16},{4,20},{8,24},{12,28},{16,0},{20,4},{24,8},{28,12},{1,17},{... | collective-permute-start | bytes 516104 | tf_op jit(solution)/shard_map/ppermute | solution.py:38
  (61 other events, 239.0 us)
